TPU v7x, 32 devices: a whole 2x2x4 slice. The times are simulated.
32 devices in a mesh: dp: 8 (over z, core), tensor: 4 (over y, x).
Axes of the slice: x: 2, y: 2, z: 4, core: 2. Of those that a mesh axis runs over, the one named last changes fastest.
Arguments:
- tokens: bfloat16 [4096, 2048], P('dp'), may hold values from -6 to 6
- cotangent: bfloat16 [4096, 2048], P('dp'), may hold values from -6 to 6
- block_ids: int32 [4096], replicated, may hold values from 0 to 31, as said below
- routes: int32 [4096, 6], P('dp'), may hold values from 0 to 11, all different within a row; in each aligned block of 512 rows (0 to 511, 512 to 1023, ...) at most 384 rows name the same one
- first_gain: float32 [2048], replicated, may hold values from 0.5 to 1.5
- query_weight: bfloat16 [2048, 3072], P(None, 'tensor'), may hold values from -0.125 to 0.125
- latent_down: bfloat16 [2048, 576], replicated, may hold values from -0.125 to 0.125
- latent_gain: float32 [512], replicated, may hold values from 0.5 to 1.5
- latent_up: bfloat16 [512, 4096], P(None, 'tensor'), may hold values from -0.25 to 0.25
- output_weight: bfloat16 [2048, 2048], P('tensor'), may hold values from -2 to 2
- second_gain: float32 [2048], replicated, may hold values from 0.5 to 1.5
- router_weight: bfloat16 [2048, 12], replicated, may hold values from -0.0625 to 0.0625
- gate_weight: bfloat16 [12, 2048, 1408], P(None, None, 'tensor'), may hold values from -0.125 to 0.125
- up_weight: bfloat16 [12, 2048, 1408], P(None, None, 'tensor'), may hold values from -0.125 to 0.125
- down_weight: bfloat16 [12, 1408, 2048], P(None, 'tensor'), may hold values from -0.3125 to 0.3125
- shared_gate: bfloat16 [2048, 2816], P(None, 'tensor'), may hold values from -0.125 to 0.125
- shared_up: bfloat16 [2048, 2816], P(None, 'tensor'), may hold values from -0.125 to 0.125
- shared_down: bfloat16 [2816, 2048], P('tensor'), may hold values from -0.15625 to 0.15625
Outputs:
- result: bfloat16 [4096, 2048], P('dp')
- token_grad: bfloat16 [4096, 2048], P('dp')
- grad_first_gain: float32 [2048], P('dp')
- grad_query: float32 [2048, 3072], P('dp', 'tensor')
- grad_latent_down: float32 [2048, 576], P(('dp', 'tensor'))
- grad_latent_gain: float32 [512], P(('dp', 'tensor'))
- grad_latent_up: float32 [512, 4096], P('dp', 'tensor')
- grad_output: float32 [2048, 2048], P('tensor', 'dp')
- grad_second_gain: float32 [2048], P('dp')
- grad_router: float32 [2048, 12], P(('dp', 'tensor'))
- grad_gate: float32 [12, 2048, 1408], P(None, 'dp', 'tensor')
- grad_up: float32 [12, 2048, 1408], P(None, 'dp', 'tensor')
- grad_down: float32 [12, 1408, 2048], P(None, 'tensor', 'dp')
- grad_shared_gate: float32 [2048, 2816], P('dp', 'tensor')
- grad_shared_up: float32 [2048, 2816], P('dp', 'tensor')
- grad_shared_down: float32 [2816, 2048], P('tensor', 'dp')
Inputs may be any that keep to these rules, and one draw needn't show every extreme that they name: `routes`: each row names 6 different experts. In the rows of one index of dp no expert is named by more than 384 rows, and in some draws' devices one expert by exactly 384. `block_ids`: Non-decreasing along the positions; the j-th aligned run of 256 positions holds the blocks 2 j and 2 j + 1, each of 64 to 192 positions.
All inputs are finite; a program needn't handle non-finite values.
Results may differ from a plain program's by a relative error of at most 0.025.
Values may be sent and summed in bfloat16 or wider, within the bound.
A program may use at most 448 MiB of HBM per device.

v0:
```python
import jax
import jax.numpy as jnp
from jax import lax
from jax.sharding import PartitionSpec as P

ND = 128
RD = 64
VD = 128
KVL = 512
EXPERTS = 12
TOP = 6
CAP = 384


EPSILON = 1e-06
HIGHEST = lax.Precision.HIGHEST


def rotary_tables(places, rotary_width):
    halfway = rotary_width // 2
    frequency = 10000.0 ** (-jnp.arange(halfway, dtype=jnp.float32) * 2.0 / rotary_width)
    angles = places.astype(jnp.float32)[:, None] * frequency[None, :]
    return (jnp.cos(angles), jnp.sin(angles))


def rotate(values, cosine, sine_table):
    halfway = values.shape[-1] // 2
    leading = values[..., :halfway]
    trailing = values[..., halfway:]
    return jnp.concatenate(
        [leading * cosine - trailing * sine_table, trailing * cosine + leading * sine_table],
        axis=-1,
    )


def norm_rows(values, gain_row):
    factor = lax.rsqrt(jnp.mean(values * values, axis=-1, keepdims=True) + EPSILON)
    return (values * factor * gain_row, factor)


def norm_back(values, factor, gain_row, upstream):
    weighted = upstream * gain_row
    common = jnp.mean(weighted * values, axis=-1, keepdims=True)
    return (
        factor * weighted - values * factor * factor * factor * common,
        jnp.sum(upstream * values * factor, axis=0),
    )


def silu_slope(before):
    sigmoid = jax.nn.sigmoid(before)
    return sigmoid * (1.0 + before * (1.0 - sigmoid))


def slot_table(route_rows):
    flat_routes = route_rows.reshape(-1)
    pair_count = flat_routes.shape[0]
    matches = (flat_routes[:, None] == jnp.arange(EXPERTS, dtype=jnp.int32)[None, :]).astype(
        jnp.int32
    )
    slot_rank = jnp.sum(matches * (jnp.cumsum(matches, axis=0) - 1), axis=1)
    slot_index = jnp.full((EXPERTS, CAP), pair_count, dtype=jnp.int32)
    return slot_index.at[flat_routes, slot_rank].set(jnp.arange(pair_count, dtype=jnp.int32))


def over_rows(former, latter):
    return lax.dot_general(
        former, latter, (((0,), (0,)), ((), ())), preferred_element_type=jnp.float32
    )


def over_cols(former, latter):
    return lax.dot_general(
        former, latter, (((1,), (1,)), ((), ())), preferred_element_type=jnp.float32
    )


def exact_rows(former, latter):
    return lax.dot_general(
        former.astype(jnp.float32), latter, (((0,), (0,)), ((), ())), precision=HIGHEST
    )


def exact_cols(former, latter):
    return lax.dot_general(
        former, latter.astype(jnp.float32), (((1,), (1,)), ((), ())), precision=HIGHEST
    )


def head_scores(query_head, key_nope, key_rope, visible, factor):
    scores = over_cols(query_head[:, :ND], key_nope) + over_cols(query_head[:, ND:], key_rope)
    return jnp.where(visible, scores * factor, -1e30)


def shards(
    tokens,
    cotangent,
    block_ids,
    routes,
    first_gain,
    query_weight,
    latent_down,
    latent_gain,
    latent_up,
    output_weight,
    second_gain,
    router_weight,
    gate_weight,
    up_weight,
    down_weight,
    shared_gate,
    shared_up,
    shared_down,
):
    row_count = tokens.shape[0]
    model_width = tokens.shape[1]
    key_count = block_ids.shape[0]
    head_count = query_weight.shape[1] // (ND + RD)
    row_start = lax.axis_index("dp") * row_count
    cosine, sine_table = rotary_tables(
        (row_start + jnp.arange(row_count, dtype=jnp.int32)) % key_count, RD
    )
    own_blocks = lax.dynamic_slice_in_dim(block_ids, row_start, row_count, 0)
    visible = block_ids[None, :] <= own_blocks[:, None]
    factor = (ND + RD) ** (-0.5)
    rows_float = tokens.astype(jnp.float32)
    normed_first, first_factor = norm_rows(rows_float, first_gain)
    attention_input = normed_first.astype(jnp.bfloat16)
    query_raw = jnp.dot(attention_input, query_weight, preferred_element_type=jnp.float32).reshape(
        row_count, head_count, ND + RD
    )
    queries = jnp.concatenate(
        [query_raw[..., :ND], rotate(query_raw[..., ND:], cosine[:, None], sine_table[:, None])],
        axis=-1,
    ).astype(jnp.bfloat16)
    compressed = jnp.dot(attention_input, latent_down, preferred_element_type=jnp.float32)
    latent_raw = compressed[:, :KVL]
    latent_float, latent_factor = norm_rows(latent_raw, latent_gain)
    latent = latent_float.astype(jnp.bfloat16)
    key_rope = rotate(compressed[:, KVL:], cosine, sine_table).astype(jnp.bfloat16)
    all_latent, all_rope = (
        lax.all_gather(latent, "dp", axis=0, tiled=True),
        lax.all_gather(key_rope, "dp", axis=0, tiled=True),
    )
    expanded = (
        jnp.dot(all_latent, latent_up, preferred_element_type=jnp.float32)
        .astype(jnp.bfloat16)
        .reshape(key_count, head_count, ND + VD)
    )
    head_mixes = []
    log_sums = []
    for head_number in range(head_count):
        scores = head_scores(
            queries[:, head_number], expanded[:, head_number, :ND], all_rope, visible, factor
        )
        highest = jnp.max(scores, axis=1, keepdims=True)
        weights = jnp.exp(scores - highest)
        summed = jnp.sum(weights, axis=1, keepdims=True)
        chances = (weights / summed).astype(jnp.bfloat16)
        head_mixes.append(
            jnp.dot(chances, expanded[:, head_number, ND:], preferred_element_type=jnp.float32)
        )
        log_sums.append(highest + jnp.log(summed))
    attended = jnp.concatenate(head_mixes, axis=1).astype(jnp.bfloat16)
    attention_part = jnp.dot(attended, output_weight, preferred_element_type=jnp.float32)
    residual = rows_float + lax.psum(attention_part.astype(jnp.bfloat16), "tensor").astype(
        jnp.float32
    )
    normed_second, second_factor = norm_rows(residual, second_gain)
    expert_input = normed_second.astype(jnp.bfloat16)
    router = jax.nn.softmax(
        jnp.dot(expert_input, router_weight, preferred_element_type=jnp.float32), axis=-1
    )
    picked = (routes[:, :, None] == jnp.arange(EXPERTS, dtype=jnp.int32)[None, None, :]).astype(
        jnp.float32
    )
    route_gates = jnp.sum(picked * router[:, None, :], axis=2)
    slot_index = slot_table(routes)
    slot_token = slot_index // TOP
    buffer = jnp.concatenate([expert_input, jnp.zeros((1, model_width), jnp.bfloat16)], axis=0)[
        slot_token
    ]
    slot_gate = jnp.concatenate([route_gates.reshape(-1), jnp.zeros((1,), jnp.float32)], axis=0)[
        slot_index
    ]
    gate_pre = jnp.einsum("ecd,edf->ecf", buffer, gate_weight, preferred_element_type=jnp.float32)
    up_pre = jnp.einsum("ecd,edf->ecf", buffer, up_weight, preferred_element_type=jnp.float32)
    hidden = (jax.nn.silu(gate_pre) * up_pre).astype(jnp.bfloat16)
    expert_out = jnp.einsum("ecf,efd->ecd", hidden, down_weight, preferred_element_type=jnp.float32)
    routed = (
        jnp.zeros((row_count + 1, model_width), jnp.float32)
        .at[slot_token.reshape(-1)]
        .add((slot_gate[..., None] * expert_out).reshape(-1, model_width))[:row_count]
    )
    shared_pre = jnp.dot(expert_input, shared_gate, preferred_element_type=jnp.float32)
    shared_lift = jnp.dot(expert_input, shared_up, preferred_element_type=jnp.float32)
    shared_hidden = (jax.nn.silu(shared_pre) * shared_lift).astype(jnp.bfloat16)
    shared_out = jnp.dot(shared_hidden, shared_down, preferred_element_type=jnp.float32)
    expert_total = lax.psum((routed + shared_out).astype(jnp.bfloat16), "tensor").astype(
        jnp.float32
    )
    result = (residual + expert_total).astype(jnp.bfloat16)
    upstream = cotangent.astype(jnp.float32)
    grad_shared_down = over_rows(shared_hidden, cotangent)
    shared_back = over_cols(cotangent, shared_down)
    shared_pre_grad = (shared_back * shared_lift * silu_slope(shared_pre)).astype(jnp.bfloat16)
    shared_lift_grad = (shared_back * jax.nn.silu(shared_pre)).astype(jnp.bfloat16)
    grad_shared_gate = over_rows(expert_input, shared_pre_grad)
    grad_shared_up = over_rows(expert_input, shared_lift_grad)
    input_grad = over_cols(shared_pre_grad, shared_gate) + over_cols(shared_lift_grad, shared_up)
    slot_upstream = jnp.concatenate([cotangent, jnp.zeros((1, model_width), jnp.bfloat16)], axis=0)[
        slot_token
    ].astype(jnp.float32)
    out_grad = (slot_gate[..., None] * slot_upstream).astype(jnp.bfloat16)
    slot_gate_grad = jnp.sum(slot_upstream * expert_out, axis=2)
    grad_down = jnp.einsum("ecf,ecd->efd", hidden, out_grad, preferred_element_type=jnp.float32)
    hidden_grad = jnp.einsum(
        "ecd,efd->ecf", out_grad, down_weight, preferred_element_type=jnp.float32
    )
    gate_grad = (hidden_grad * up_pre * silu_slope(gate_pre)).astype(jnp.bfloat16)
    lift_grad = (hidden_grad * jax.nn.silu(gate_pre)).astype(jnp.bfloat16)
    grad_gate = jnp.einsum("ecd,ecf->edf", buffer, gate_grad, preferred_element_type=jnp.float32)
    grad_up = jnp.einsum("ecd,ecf->edf", buffer, lift_grad, preferred_element_type=jnp.float32)
    buffer_grad = jnp.einsum(
        "ecf,edf->ecd", gate_grad, gate_weight, preferred_element_type=jnp.float32
    ) + jnp.einsum("ecf,edf->ecd", lift_grad, up_weight, preferred_element_type=jnp.float32)
    input_grad = (
        input_grad
        + jnp.zeros((row_count + 1, model_width), jnp.float32)
        .at[slot_token.reshape(-1)]
        .add(buffer_grad.reshape(-1, model_width))[:row_count]
    )
    pair_grad = (
        jnp.zeros((row_count * TOP + 1,), jnp.float32)
        .at[slot_index.reshape(-1)]
        .add(slot_gate_grad.reshape(-1))[: row_count * TOP]
        .reshape(row_count, TOP)
    )
    router_grad = jnp.sum(picked * pair_grad[:, :, None], axis=1)
    logit_grad = router * (router_grad - jnp.sum(router * router_grad, axis=1, keepdims=True))
    grad_router = exact_rows(expert_input, logit_grad)
    input_grad = input_grad + exact_cols(logit_grad, router_weight)
    input_grad = lax.psum(input_grad.astype(jnp.bfloat16), "tensor").astype(jnp.float32)
    residual_grad, grad_second_gain = norm_back(residual, second_factor, second_gain, input_grad)
    residual_grad = residual_grad + upstream
    output_grad = residual_grad.astype(jnp.bfloat16)
    grad_output = over_rows(attended, output_grad)
    attended_grad = over_cols(output_grad, output_weight).astype(jnp.bfloat16)
    query_grads = []
    expanded_grads = []
    rope_grad = jnp.zeros((key_count, RD), jnp.float32)
    for head_number in range(head_count):
        query_head = queries[:, head_number]
        key_nope = expanded[:, head_number, :ND]
        head_values = expanded[:, head_number, ND:]
        scores = head_scores(query_head, key_nope, all_rope, visible, factor)
        chances = jnp.exp(scores - log_sums[head_number])
        head_grad = attended_grad[:, head_number * VD : (head_number + 1) * VD]
        chance_grad = over_cols(head_grad, head_values)
        score_grad = (
            chances * (chance_grad - jnp.sum(chances * chance_grad, axis=1, keepdims=True))
        ).astype(jnp.bfloat16)
        nope_grad = jnp.dot(score_grad, key_nope, preferred_element_type=jnp.float32) * factor
        rotary_grad = jnp.dot(score_grad, all_rope, preferred_element_type=jnp.float32) * factor
        query_grads.append(
            jnp.concatenate([nope_grad, rotate(rotary_grad, cosine, -sine_table)], axis=1)
        )
        key_grad = over_rows(score_grad, query_head[:, :ND]) * factor
        value_grad = over_rows(chances.astype(jnp.bfloat16), head_grad)
        expanded_grads.append(jnp.concatenate([key_grad, value_grad], axis=1))
        rope_grad = rope_grad + over_rows(score_grad, query_head[:, ND:]) * factor
    query_grad = jnp.concatenate(query_grads, axis=1).astype(jnp.bfloat16)
    expanded_grad = jnp.concatenate(expanded_grads, axis=1)
    grad_query = over_rows(attention_input, query_grad)
    grad_latent_up = exact_rows(all_latent, expanded_grad)
    compressed_grad = lax.psum_scatter(
        jnp.concatenate([exact_cols(expanded_grad, latent_up), rope_grad], axis=1).astype(
            jnp.bfloat16
        ),
        "dp",
        scatter_dimension=0,
        tiled=True,
    ).astype(jnp.float32)
    latent_grad, grad_latent_gain = norm_back(
        latent_raw, latent_factor, latent_gain, compressed_grad[:, :KVL]
    )
    down_grad = jnp.concatenate(
        [latent_grad, rotate(compressed_grad[:, KVL:], cosine, -sine_table)], axis=1
    )
    grad_latent_down = exact_rows(attention_input, down_grad)
    attention_grad = over_cols(query_grad, query_weight) + exact_cols(down_grad, latent_down)
    attention_grad = lax.psum(attention_grad.astype(jnp.bfloat16), "tensor").astype(jnp.float32)
    token_grad, grad_first_gain = norm_back(rows_float, first_factor, first_gain, attention_grad)
    token_grad = (token_grad + residual_grad).astype(jnp.bfloat16)
    common_grads = (
        lax.psum_scatter(grad_latent_down, ("dp", "tensor"), scatter_dimension=0, tiled=True),
        lax.psum_scatter(grad_latent_gain, ("dp", "tensor"), scatter_dimension=0, tiled=True),
        lax.psum_scatter(grad_router, ("dp", "tensor"), scatter_dimension=0, tiled=True),
    )
    split_grads = (
        lax.psum_scatter(
            grad_first_gain.astype(jnp.bfloat16), "dp", scatter_dimension=0, tiled=True
        ).astype(jnp.float32),
        lax.psum_scatter(
            grad_query.astype(jnp.bfloat16), "dp", scatter_dimension=0, tiled=True
        ).astype(jnp.float32),
        lax.psum_scatter(
            grad_latent_up.astype(jnp.bfloat16), "dp", scatter_dimension=0, tiled=True
        ).astype(jnp.float32),
        lax.psum_scatter(
            grad_output.astype(jnp.bfloat16), "dp", scatter_dimension=1, tiled=True
        ).astype(jnp.float32),
        lax.psum_scatter(
            grad_second_gain.astype(jnp.bfloat16), "dp", scatter_dimension=0, tiled=True
        ).astype(jnp.float32),
        lax.psum_scatter(
            grad_gate.astype(jnp.bfloat16), "dp", scatter_dimension=1, tiled=True
        ).astype(jnp.float32),
        lax.psum_scatter(
            grad_up.astype(jnp.bfloat16), "dp", scatter_dimension=1, tiled=True
        ).astype(jnp.float32),
        lax.psum_scatter(
            grad_down.astype(jnp.bfloat16), "dp", scatter_dimension=2, tiled=True
        ).astype(jnp.float32),
        lax.psum_scatter(
            grad_shared_gate.astype(jnp.bfloat16), "dp", scatter_dimension=0, tiled=True
        ).astype(jnp.float32),
        lax.psum_scatter(
            grad_shared_up.astype(jnp.bfloat16), "dp", scatter_dimension=0, tiled=True
        ).astype(jnp.float32),
        lax.psum_scatter(
            grad_shared_down.astype(jnp.bfloat16), "dp", scatter_dimension=1, tiled=True
        ).astype(jnp.float32),
    )
    return (
        result,
        token_grad,
        split_grads[0],
        split_grads[1],
        common_grads[0],
        common_grads[1],
        split_grads[2],
        split_grads[3],
        split_grads[4],
        common_grads[2],
        split_grads[5],
        split_grads[6],
        split_grads[7],
        split_grads[8],
        split_grads[9],
        split_grads[10],
    )


def solution(mesh):
    in_specs = (
        P("dp", None),
        P("dp", None),
        P(),
        P("dp", None),
        P(),
        P(None, "tensor"),
        P(),
        P(),
        P(None, "tensor"),
        P("tensor", None),
        P(),
        P(),
        P(None, None, "tensor"),
        P(None, None, "tensor"),
        P(None, "tensor", None),
        P(None, "tensor"),
        P(None, "tensor"),
        P("tensor", None),
    )
    out_specs = (
        P("dp", None),
        P("dp", None),
        P("dp"),
        P("dp", "tensor"),
        P(("dp", "tensor"), None),
        P(("dp", "tensor")),
        P("dp", "tensor"),
        P("tensor", "dp"),
        P("dp"),
        P(("dp", "tensor"), None),
        P(None, "dp", "tensor"),
        P(None, "dp", "tensor"),
        P(None, "tensor", "dp"),
        P("dp", "tensor"),
        P("dp", "tensor"),
        P("tensor", "dp"),
    )
    return jax.shard_map(shards, mesh=mesh, in_specs=in_specs, out_specs=out_specs, check_vma=False)
```

profile of v0, /device:TPU:0, one launch (start us, length us, event | category | flops | bytes accessed | tf_op | source)
XLA Modules:
  0.0 1907.7 jit_solution(2176622956842079716)
XLA Ops:
  33.5 20.0 %all_gather.7 = bf16[4096,64]{0,1:T(8,128)(2,1)} all-gather(bf16[512,64]{0,1:T(8,128)(2,1)S(1)} %pad_maximum_fusion.8), channel_id=1, replica_groups=mesh['dp'=8,'tensor'=4] {'dp'}, dimensions={0}, use_global_device_ids=true | all-gather | bytes 589824 | tf_op jit(solution)/shard_map/all_gather | solution.py:143
  54.4 15.6 all-gather.2.cloned.1.call-done
  138.5 37.1 %gather_fusion.2 = bf16[4608,2048]{1,0:T(8,128)(2,1)} fusion(bf16[513,2048]{1,0:T(8,128)(2,1)} %concatenate.44, s32[5120]{0:T(1024)S(1)} %pad_clamp_fusion), kind=kCustom, calls=%fused_computation.2 | custom fusion | bytes 37767168 | tf_op jit(solution)/shard_map/gather | solution.py:211
  208.4 37.4 %gather_fusion.1 = bf16[4608,2048]{1,0:T(8,128)(2,1)} fusion(bf16[513,2048]{1,0:T(8,128)(2,1)} %concatenate.43, s32[5120]{0:T(1024)S(1)} %pad_clamp_fusion), kind=kCustom, calls=%fused_computation.1 | custom fusion | bytes 37767168 | tf_op jit(solution)/shard_map/gather | solution.py:180
  245.7 23.0 %fusion.189 = f32[12,384,352]{1,2,0:T(8,128)} fusion(bf16[12,384,2048]{2,1,0:T(8,128)(2,1)} %bitcast.156, bf16[12,2048,352]{1,2,0:T(8,128)(2,1)} %param.30), kind=kOutput, calls=%fused_computation.344 | convolution fusion | flops 6643777536 | bytes 42663936 | tf_op jit(solution)/shard_map/ecd,edf->ecf/dot_general | solution.py:186
  268.8 24.2 %multiply_convert_fusion.6 = (bf16[12,384,352]{1,2,0:T(8,128)(2,1)}, f32[12,384,352]{1,2,0:T(8,128)}) fusion(f32[12,384,352]{1,2,0:T(8,128)} %fusion.189, bf16[12,384,2048]{2,1,0:T(8,128)(2,1)} %bitcast.157, bf16[12,2048,352]{1,2,0:T(8,128)(2,1)} %param.31), kind=kOutput, calls=%fused_computation.54 | convolution fusion | flops 6653509632 | bytes 52396032 | tf_op jit(solution)/shard_map/ecd,edf->ecf/dot_general | solution.py:187
  293.0 27.2 %fusion.1 = (f32[12,384]{1,0:T(8,128)S(1)}, f32[12,384,2048]{2,1,0:T(8,128)}) fusion(bf16[12,384,2048]{2,1,0:T(8,128)(2,1)} %bitcast.160, bf16[12,384,352]{1,2,0:T(8,128)(2,1)} %get-tuple-element.58, bf16[12,352,2048]{2,1,0:T(8,128)(2,1)} %param.32), kind=kOutput, calls=%fused_computation.10 | convolution fusion | flops 6672084480 | bytes 77187072 | tf_op jit(solution)/shard_map/ecf,efd->ecd/dot_general | solution.py:189
  320.2 32.1 %scatter_custom_fusion.2 = f32[3073]{0:T(1024)S(1)} fusion(s32[4608]{0:T(1024)S(1)} %fusion.165, f32[4608]{0:T(1024)S(1)} %reshape.396, f32[]{:T(128)} %constant.37.clone.1), kind=kCustom, calls=%fused_computation.311 | custom fusion | flops 4608 | bytes 12296 | tf_op jit(solution)/shard_map/scatter-add | solution.py:236
  355.7 24.1 %gather_fusion = f32[4608]{0:T(1024)S(1)} fusion(f32[3073]{0:T(1024)S(1)} %pad_maximum_fusion.9, s32[5120]{0:T(1024)S(1)} %pad_clamp_fusion.1), kind=kCustom, calls=%fused_computation | custom fusion | bytes 55296 | tf_op jit(solution)/shard_map/gather | solution.py:183
  379.9 22.0 %multiply_convert_fusion.4 = (bf16[12,384,352]{1,2,0:T(8,128)(2,1)}, bf16[12,384,352]{1,2,0:T(8,128)(2,1)}) fusion(f32[12,384,352]{1,2,0:T(8,128)} %fusion.189, f32[12,384,352]{1,2,0:T(8,128)} %get-tuple-element.59, bf16[12,352,2048]{2,1,0:T(8,128)(2,1)} %param.32, bf16[12,384,2048]{2,1,0:T(8,128)(2,1)} %bitcast.161, f32[12,384]{1,0:T(8,128)S(1)} %reshape.353), kind=kOutput, calls=%fused_computation.52 | convolution fusion | flops 6693175296 | bytes 55658496 | tf_op jit(solution)/shard_map/ecd,efd->ecf/dot_general | solution.py:217
  401.8 22.8 %fusion.194 = f32[12,384,2048]{2,1,0:T(8,128)} fusion(bf16[12,384,352]{1,2,0:T(8,128)(2,1)} %get-tuple-element.29, bf16[12,2048,352]{1,2,0:T(8,128)(2,1)} %param.30), kind=kOutput, calls=%fused_computation.349 | convolution fusion | flops 6643777536 | bytes 58294272 | tf_op jit(solution)/shard_map/ecf,edf->ecd/dot_general | solution.py:224
  424.7 31.3 %convolution_add_fusion = f32[12,384,2048]{2,1,0:T(8,128)} fusion(f32[12,384,2048]{2,1,0:T(8,128)} %fusion.194, bf16[12,384,352]{1,2,0:T(8,128)(2,1)} %get-tuple-element.28, bf16[12,2048,352]{1,2,0:T(8,128)(2,1)} %param.31), kind=kOutput, calls=%fused_computation.12 | convolution fusion | flops 6653214720 | bytes 96043008 | tf_op jit(solution)/shard_map/ecf,edf->ecd/dot_general | solution.py:226
  455.9 60.9 %scatter_custom_fusion.1 = f32[513,2048]{1,0:T(8,128)} fusion(s32[4608]{0:T(1024)} %fusion.164, f32[4608,2048]{1,0:T(8,128)} %bitcast.163, f32[]{:T(128)} %constant.37.clone.1), kind=kCustom, calls=%fused_computation.126 | custom fusion | flops 9437184 | bytes 4203008 | tf_op jit(solution)/shard_map/scatter-add | solution.py:231
  525.3 69.6 %all-reduce.13.cloned.1.call-done = bf16[512,2048]{1,0:T(8,128)(2,1)} async-done(((bf16[512,2048]{1,0:T(8,128)(2,1)}), bf16[512,2048]{1,0:T(8,128)(2,1)}) %all-reduce.13.cloned.1.call-update) | async-done | bytes 2097168 | tf_op jit(solution)/shard_map/psum | solution.py:243
  682.5 18.1 convolution_convert_fusion.3
  708.1 19.2 %convolution_convert_fusion.10 = bf16[512,1024]{1,0:T(8,128)(2,1)} fusion(bf16[4096,512]{0,1:T(8,128)(2,1)} %all-gather.2.cloned.1.call-done, f32[4096,1024]{0,1:T(8,128)} %convolution_dynamic-update-slice_fusion), kind=kOutput, calls=%fused_computation.130 | convolution fusion | flops 25770328064 | bytes 22020096 | tf_op jit(solution)/shard_map/dot_general | solution.py:79
  780.0 27.2 %broadcast_multiply_fusion = f32[12,384,2048]{2,1,0:T(8,128)} fusion(f32[12,384,2048]{2,1,0:T(8,128)} %get-tuple-element.61, f32[12,384]{1,0:T(8,128)S(1)} %copy-done.54), kind=kLoop, calls=%fused_computation.11 | loop fusion | flops 9437184 | bytes 75515904 | tf_op jit(solution)/shard_map/mul | solution.py:193
  807.2 60.7 %scatter_custom_fusion = f32[513,2048]{1,0:T(8,128)} fusion(s32[4608]{0:T(1024)} %fusion.164, f32[4608,2048]{1,0:T(8,128)} %bitcast.164, f32[]{:T(128)} %constant.37.clone.1), kind=kCustom, calls=%fused_computation.128 | custom fusion | flops 9437184 | bytes 4203008 | tf_op jit(solution)/shard_map/scatter-add | solution.py:193
  890.9 19.5 %fusion.6 = bf16[12,352,2048]{2,1,0:T(8,128)(2,1)} fusion(bf16[12,384,352]{1,2,0:T(8,128)(2,1)} %get-tuple-element.58, bf16[12,384,2048]{2,1,0:T(8,128)(2,1)} %bitcast.162, f32[12,384]{1,0:T(8,128)S(1)} %copy-done.54), kind=kOutput, calls=%fused_computation.19 | convolution fusion | flops 6680739840 | bytes 39438336 | tf_op jit(solution)/shard_map/ecf,ecd->efd/dot_general | solution.py:216
  910.7 19.7 %convolution_convert_fusion = bf16[12,2048,352]{1,2,0:T(8,128)(2,1)} fusion(bf16[12,384,352]{1,2,0:T(8,128)(2,1)} %get-tuple-element.28, bf16[12,384,2048]{2,1,0:T(8,128)(2,1)} %bitcast.158), kind=kOutput, calls=%fused_computation.20 | convolution fusion | flops 6652428288 | bytes 39419904 | tf_op jit(solution)/shard_map/ecd,ecf->edf/dot_general | solution.py:223
  930.4 19.7 %convolution_convert_fusion.1 = bf16[12,2048,352]{1,2,0:T(8,128)(2,1)} fusion(bf16[12,384,352]{1,2,0:T(8,128)(2,1)} %get-tuple-element.29, bf16[12,384,2048]{2,1,0:T(8,128)(2,1)} %bitcast.159), kind=kOutput, calls=%fused_computation.21 | convolution fusion | flops 6652428288 | bytes 39419904 | tf_op jit(solution)/shard_map/ecd,ecf->edf/dot_general | solution.py:222
  966.9 37.6 %reduce-scatter.31.cloned.1.call-done = bf16[256,704]{0,1:T(8,128)(2,1)} async-done(((bf16[2048,704]{0,1:T(8,128)(2,1)}), bf16[256,704]{0,1:T(8,128)(2,1)}) %reduce-scatter.31.cloned.1.call-update) | async-done | bytes 360464 | tf_op jit(solution)/shard_map/reduce_scatter | solution.py:325
  1006.3 38.8 %reduce-scatter.35.cloned.1.call-done = bf16[704,256]{1,0:T(8,128)(2,1)} async-done(((bf16[704,2048]{1,0:T(8,128)(2,1)}), bf16[704,256]{1,0:T(8,128)(2,1)}) %reduce-scatter.35.cloned.1.call-update) | async-done | bytes 360464 | tf_op jit(solution)/shard_map/reduce_scatter | solution.py:331
  1047.0 35.8 %reduce-scatter.23.cloned.1.call-done = bf16[512,256]{1,0:T(8,128)(2,1)} async-done(((bf16[512,2048]{1,0:T(8,128)(2,1)}), bf16[512,256]{1,0:T(8,128)(2,1)}) %reduce-scatter.23.cloned.1.call-update) | async-done | bytes 262160 | tf_op jit(solution)/shard_map/reduce_scatter | solution.py:310
  1084.5 40.1 %reduce-scatter.17.cloned.1.call-done = bf16[256,768]{1,0:T(8,128)(2,1)} async-done(((bf16[2048,768]{1,0:T(8,128)(2,1)}), bf16[256,768]{1,0:T(8,128)(2,1)}) %reduce-scatter.17.cloned.1.call-update) | async-done | bytes 393232 | tf_op jit(solution)/shard_map/reduce_scatter | solution.py:304
  1126.6 37.9 %all-reduce.3 = f32[512]{0:T(512)S(1)} all-reduce(f32[512]{0:T(512)S(1)} %get-tuple-element.20), channel_id=6, replica_groups=mesh['dp'=8,'tensor'=4] {'dp','tensor'}, use_global_device_ids=true, to_apply=%region_41.42.clone | all-reduce | flops 512 | bytes 4096
  1165.1 67.6 %all-reduce.15.cloned.1.call-done = (bf16[512,2048]{1,0:T(8,128)(2,1)}, bf16[512,2048]{1,0:T(8,128)(2,1)}) async-done(((bf16[512,2048]{1,0:T(8,128)(2,1)}, bf16[512,2048]{1,0:T(8,128)(2,1)}), (bf16[512,2048]{1,0:T(8,128)(2,1)}, bf16[512,2048]{1,0:T(8,128)(2,1)})) %all-reduce.15.cloned.1.call-update) | async-done | bytes 4194320 | tf_op jit(solution)/shard_map/psum | solution.py:199
  1236.5 17.1 all-reduce.5
  1262.4 146.4 %reduce-scatter.29.cloned.1.call-done = bf16[12,352,256]{2,1,0:T(8,128)(2,1)} async-done(((bf16[12,352,2048]{2,1,0:T(8,128)(2,1)}), bf16[12,352,256]{2,1,0:T(8,128)(2,1)}) %reduce-scatter.29.cloned.1.call-update) | async-done | bytes 2162704 | tf_op jit(solution)/shard_map/reduce_scatter | solution.py:322
  1412.8 169.5 %reduce-scatter.27.cloned.1.call-done = bf16[12,256,352]{1,2,0:T(8,128)(2,1)} async-done(((bf16[12,2048,352]{1,2,0:T(8,128)(2,1)}), bf16[12,256,352]{1,2,0:T(8,128)(2,1)}) %reduce-scatter.27.cloned.1.call-update) | async-done | bytes 2162704 | tf_op jit(solution)/shard_map/reduce_scatter | solution.py:319
  1586.3 169.7 %reduce-scatter.25.cloned.1.call-done = bf16[12,256,352]{1,2,0:T(8,128)(2,1)} async-done(((bf16[12,2048,352]{1,2,0:T(8,128)(2,1)}), bf16[12,256,352]{1,2,0:T(8,128)(2,1)}) %reduce-scatter.25.cloned.1.call-update) | async-done | bytes 2162704 | tf_op jit(solution)/shard_map/reduce_scatter | solution.py:316
  1760.1 140.8 %reduce-scatter.19.cloned.1.call-done = f32[64,576]{1,0:T(8,128)} async-done(((f32[2048,576]{1,0:T(8,128)}), f32[64,576]{1,0:T(8,128)}) %reduce-scatter.19.cloned.1.call-update) | async-done | bytes 147472 | tf_op jit(solution)/shard_map/reduce_scatter | solution.py:296
  (411 shorter events, 358.8 us)
Async XLA Ops:
  7.2 16.0 copy-start
  7.2 62.8 %all-gather.2.cloned.1.call-start = ((), (), s32[]{:S(2)}) async-start(), calls=%async_computation.12 | async-start | bytes 4718592 | tf_op jit(solution)/shard_map/all_gather | solution.py:142
  15.9 169.4 %all-reduce.11.cloned.1.call-start = ((), (), s32[]{:S(2)}) async-start(), calls=%async_computation.13 | async-start | bytes 4194304 | tf_op jit(solution)/shard_map/psum | solution.py:166
  77.1 32.4 %copy-start.23 = (bf16[4096,1024]{0,1:T(8,128)(2,1)}, bf16[4096,1024]{0,1:T(8,128)(2,1)S(1)}, u32[]{:S(2)}) copy-start(bf16[4096,1024]{0,1:T(8,128)(2,1)S(1)} %convolution_convert_fusion.2) | copy-start | bytes 25165828
  86.1 27.2 %copy-start.47 = (bf16[512,128]{0,1:T(8,128)(2,1)}, bf16[512,128]{0,1:T(8,128)(2,1)S(1)}, u32[]{:S(2)}) copy-start(bf16[512,128]{0,1:T(8,128)(2,1)S(1)} %fusion.72) | copy-start | bytes 393220
  95.2 18.2 copy-start.49
  104.1 9.3 copy-start.51
  116.7 478.3 %all-reduce.13.cloned.1.call-start = ((), (), s32[]{:S(2)}) async-start(), calls=%async_computation.14 | async-start | bytes 4194304 | tf_op jit(solution)/shard_map/psum | solution.py:243
  175.7 12.8 copy-start.55
  293.0 60.3 %copy-start.58 = (s32[512,6]{0,1:T(8,128)S(1)}, s32[512,6]{0,1:T(8,128)}, u32[]{:S(2)}) copy-start(s32[512,6]{0,1:T(8,128)} %param.21) | copy-start | bytes 36868
  379.8 22.0 %copy-start.53 = (f32[12,384]{1,0:T(8,128)}, f32[12,384]{1,0:T(8,128)S(1)}, u32[]{:S(2)}) copy-start(f32[12,384]{1,0:T(8,128)S(1)} %reshape.353) | copy-start | bytes 55300
  455.9 60.9 %copy-start.43 = (bf16[2048,12]{0,1:T(8,128)(2,1)S(1)}, bf16[2048,12]{0,1:T(8,128)(2,1)}, u32[]{:S(2)}) copy-start(bf16[2048,12]{0,1:T(8,128)(2,1)} %param.29) | copy-start | bytes 147460
  516.9 78.0 %copy-start.56 = (f32[2048]{0:T(1024)S(1)}, f32[2048]{0:T(1024)}, u32[]{:S(2)}) copy-start(f32[2048]{0:T(1024)} %param.28) | copy-start | bytes 24580
  516.9 78.0 %copy-start.65 = (f32[512]{0:T(512)S(1)}, f32[512]{0:T(512)}, u32[]{:S(2)}) copy-start(f32[512]{0:T(512)} %copy-done.64) | copy-start | bytes 6148
  525.1 353.2 %reduce-scatter.15.cloned.1.call-start = ((), (), s32[]{:S(2)}) async-start(), calls=%async_computation.15 | async-start | bytes 5308416 | tf_op jit(solution)/shard_map/reduce_scatter | solution.py:276
  595.0 13.0 slice-start.6
  608.0 31.6 %copy-start.34 = (bf16[512,512]{1,0:T(8,128)(2,1)}, bf16[512,512]{1,0:T(8,128)(2,1)S(1)}, u32[]{:S(2)}) copy-start(bf16[512,512]{1,0:T(8,128)(2,1)S(1)} %convolution_convert_fusion.11) | copy-start | bytes 1572868
  608.0 14.8 slice-start
  622.8 11.3 slice-start.4
  703.1 258.8 %reduce-scatter.37.cloned.1.call-start = ((), (), s32[]{:S(2)}) async-start(), calls=%async_computation.26 | async-start | bytes 1081344
  708.0 255.3 %reduce-scatter.21.cloned.1.call-start = ((), (), s32[]{:S(2)}) async-start(), calls=%async_computation.18 | async-start | bytes 1179648 | tf_op jit(solution)/shard_map/reduce_scatter | solution.py:307
  727.3 237.6 %reduce-scatter.33.cloned.1.call-start = ((), (), s32[]{:S(2)}) async-start(), calls=%async_computation.24 | async-start | bytes 3244032 | tf_op jit(solution)/shard_map/reduce_scatter | solution.py:328
  732.6 271.9 %reduce-scatter.31.cloned.1.call-start = ((), (), s32[]{:S(2)}) async-start(), calls=%async_computation.23 | async-start | bytes 3244032 | tf_op jit(solution)/shard_map/reduce_scatter | solution.py:325
  737.7 307.4 %reduce-scatter.35.cloned.1.call-start = ((), (), s32[]{:S(2)}) async-start(), calls=%async_computation.25 | async-start | bytes 3244032 | tf_op jit(solution)/shard_map/reduce_scatter | solution.py:331
  742.9 339.9 %reduce-scatter.23.cloned.1.call-start = ((), (), s32[]{:S(2)}) async-start(), calls=%async_computation.19 | async-start | bytes 2359296 | tf_op jit(solution)/shard_map/reduce_scatter | solution.py:310
  755.2 369.4 %reduce-scatter.17.cloned.1.call-start = ((), (), s32[]{:S(2)}) async-start(), calls=%async_computation.16 | async-start | bytes 3538944 | tf_op jit(solution)/shard_map/reduce_scatter | solution.py:304
  779.5 453.2 %all-reduce.15.cloned.1.call-start = ((), (), s32[]{:S(2)}) async-start(), calls=%async_computation.27 | async-start | bytes 8388608 | tf_op jit(solution)/shard_map/psum | solution.py:199
  890.9 517.8 %reduce-scatter.29.cloned.1.call-start = ((), (), s32[]{:S(2)}) async-start(), calls=%async_computation.22 | async-start | bytes 19464192 | tf_op jit(solution)/shard_map/reduce_scatter | solution.py:322
  910.4 671.8 %reduce-scatter.27.cloned.1.call-start = ((), (), s32[]{:S(2)}) async-start(), calls=%async_computation.21 | async-start | bytes 19464192 | tf_op jit(solution)/shard_map/reduce_scatter | solution.py:319
  930.4 825.6 %reduce-scatter.25.cloned.1.call-start = ((), (), s32[]{:S(2)}) async-start(), calls=%async_computation.20 | async-start | bytes 19464192 | tf_op jit(solution)/shard_map/reduce_scatter | solution.py:316
  950.2 950.7 %reduce-scatter.19.cloned.1.call-start = ((), (), s32[]{:S(2)}) async-start(), calls=%async_computation.17 | async-start | bytes 5406720 | tf_op jit(solution)/shard_map/reduce_scatter | solution.py:296
  966.9 269.6 %copy-start.78 = (bf16[2048]{0:T(1024)(128)(2,1)S(1)}, bf16[2048]{0:T(1024)(128)(2,1)}, u32[]{:S(2)}) copy-start(bf16[2048]{0:T(1024)(128)(2,1)} %get-tuple-element.16) | copy-start | bytes 12292
  (88 other events, 348.3 us)
Sparse Core Ops, SparseCore 0:
  16.0 53.9 all-gather.1
  116.8 68.4 all-reduce.10
  525.3 69.6 all-reduce.12
  703.2 54.9 reduce-scatter.14
  760.3 133.3 reduce-scatter.36
  895.9 28.3 reduce-scatter.20
  926.7 37.0 reduce-scatter.32
  966.3 38.1 reduce-scatter.30
  1006.9 38.1 reduce-scatter.34
  1047.4 35.3 reduce-scatter.22
  1085.8 38.8 reduce-scatter.16
  1129.0 103.6 all-reduce.14
  1235.1 173.6 reduce-scatter.28
  1410.9 171.2 reduce-scatter.26
  1584.5 171.5 reduce-scatter.24
  1758.7 142.1 reduce-scatter.18
where the time goes:
time: 1910 us
  waiting for transfers between devices  941 us (49%)
  matrix products  442 us (23%)
  other arithmetic  287 us (15%)
  local copies, waits for them, and re-layouts  145 us (8%)
  blocking collectives  75 us (4%)
    reduce_scatter x1, waiting for transfers between devices, shards(): lax.psum_scatter(grad_gate.astype(jnp.bfloat16), 'dp', scatter_dimension=...  170 us
    reduce_scatter x1, waiting for transfers between devices, shards(): lax.psum_scatter(grad_up.astype(jnp.bfloat16), 'dp', scatter_dimension=1,...  169 us
    reduce_scatter x1, waiting for transfers between devices, shards(): lax.psum_scatter(grad_down.astype(jnp.bfloat16), 'dp', scatter_dimension=...  146 us
    reduce_scatter x1, waiting for transfers between devices, shards(): lax.psum_scatter(grad_latent_down, ('dp', 'tensor'), scatter_dimension=0,...  141 us
    psum x1, waiting for transfers between devices, shards(): lax.psum(input_grad.astype(jnp.bfloat16), 'tensor').astype(jnp.float32)  69.6 us
    psum x1, waiting for transfers between devices, shards(): lax.psum((routed + shared_out).astype(jnp.bfloat16), 'tensor')  67.6 us
    scatter-add x1, other arithmetic, shards(): input_grad = input_grad + jnp.zeros((row_count + 1, model_width), jnp.flo...  60.9 us
    scatter-add x1, other arithmetic, shards(): routed = jnp.zeros((row_count + 1, model_width), jnp.float32).at[slot_tok...  60.7 us
  transfers between devices with their start and end apart: 16, of which 12 were waited for; matrix products, arithmetic and copies ran while one was open for 19% of the time, Pallas kernels for 0%

commit v1 on v0

v1 whole, which is shorter than its diff:
```python
import jax
import jax.numpy as jnp
from jax import lax
from jax.experimental import pallas as pl
from jax.experimental.pallas import tpu as pltpu
from jax.sharding import Mesh
from jax.sharding import PartitionSpec as P

ND = 128
RD = 64
VD = 128
KVL = 512
EXPERTS = 12
LAT = 640
EPSILON = 1e-06
LOG2E = 1.4426950408889634
BF = jnp.bfloat16
F32 = jnp.float32
VMEM_LIMIT = 60 * 1024 * 1024
DP = ("dpo", "core")
SPREAD = ("dpo", "tensor")
ALL = ("dpo", "core", "tensor")


def nn(former, latter):
    return jnp.dot(former, latter, preferred_element_type=F32)


def nt(former, latter):
    return lax.dot_general(former, latter, (((1,), (1,)), ((), ())), preferred_element_type=F32)


def tn(former, latter):
    return lax.dot_general(former, latter, (((0,), (0,)), ((), ())), preferred_element_type=F32)


def rotary_tables(places):
    halfway = RD // 2
    frequency = 10000.0 ** (-jnp.arange(halfway, dtype=F32) * 2.0 / RD)
    angles = places.astype(F32)[:, None] * frequency[None, :]
    return jnp.cos(angles), jnp.sin(angles)


def rotate(values, cosine, sine_table):
    halfway = values.shape[-1] // 2
    leading = values[..., :halfway]
    trailing = values[..., halfway:]
    return jnp.concatenate(
        [leading * cosine - trailing * sine_table, trailing * cosine + leading * sine_table],
        axis=-1,
    )


def norm_rows(values, gain_row):
    factor = lax.rsqrt(jnp.mean(values * values, axis=-1, keepdims=True) + EPSILON)
    return values * factor * gain_row, factor


def norm_back(values, factor, gain_row, upstream):
    weighted = upstream * gain_row
    common = jnp.mean(weighted * values, axis=-1, keepdims=True)
    return (
        factor * weighted - values * factor * factor * factor * common,
        jnp.sum(upstream * values * factor, axis=0),
    )


def expert_unit(gate_pre, up_pre, hidden_grad, gate):
    sigmoid = 0.5 * jnp.tanh(0.5 * gate_pre) + 0.5
    silu = gate_pre * sigmoid
    hidden = silu * up_pre
    scaled = gate * hidden_grad
    d_up = scaled * silu
    d_gate = scaled * up_pre * (sigmoid + silu - silu * sigmoid)
    return (
        (gate * hidden).astype(BF),
        d_gate.astype(BF),
        d_up.astype(BF),
        hidden * hidden_grad,
    )


def weight_copies(routed, shared, held, sems, step, slot, steps, width, begin):
    def each(refs):
        for i, ref in enumerate(refs):
            copy = pltpu.make_async_copy(
                ref, held.at[slot, pl.ds(i * width, width)], sems.at[slot, i]
            )
            if begin:
                copy.start()
            else:
                copy.wait()

    @pl.when(step < steps - 1)
    def _():
        rows = pl.ds(pl.multiple_of(step * width, width), width)
        each([ref.at[rows] for ref in routed])

    @pl.when(step == steps - 1)
    def _():
        each(shared)


def gate_rows(gates, width):
    parts, columns = gates.shape
    return jnp.concatenate(
        [jnp.broadcast_to(gates[i : i + 1], (width // parts, columns)) for i in range(parts)],
        axis=0,
    )


def own_experts(rows, upstream, gates, weights):
    count, model = rows.shape
    steps, parts, _ = gates.shape
    width = weights[3].shape[0]
    unit = width // parts
    wide = 512

    def kernel(x_ref, c_ref, g_ref, gw, uw, dw, sg, su, sd, out, back, kept_h, kept_g, kept_u, dots, held, sems):
        step = pl.program_id(0)
        slot = lax.rem(step, 2)
        routed, shared = (gw, uw, dw), (sg, su, sd)

        @pl.when(step == 0)
        def _():
            weight_copies(routed, shared, held, sems, step, slot, steps, width, True)
            out[...] = jnp.zeros_like(out)
            back[...] = jnp.zeros_like(back)

        weight_copies(routed, shared, held, sems, step, slot, steps, width, False)

        @pl.when(step < steps - 1)
        def _():
            weight_copies(routed, shared, held, sems, step + 1, 1 - slot, steps, width, True)

        both = nt(held[slot, : 2 * width], x_ref[...])
        hidden_grad = nt(held[slot, 2 * width :], c_ref[...])
        hidden, d_gate, d_up, products = expert_unit(
            both[:width], both[width:], hidden_grad, gate_rows(g_ref[0], width)
        )
        kept_h[0] = hidden
        kept_g[0] = d_gate
        kept_u[0] = d_up
        dots[0] = jnp.concatenate(
            [
                jnp.sum(products[i * unit : (i + 1) * unit], axis=0, keepdims=True)
                for i in range(parts)
            ],
            axis=0,
        )
        turned = hidden.T
        turned_back = jnp.concatenate([d_gate, d_up], axis=0).T
        for at in range(0, model, wide):
            columns = slice(at, at + wide)
            out[:, columns] += nn(turned, held[slot, 2 * width :, columns])
            back[:, columns] += nn(turned_back, held[slot, : 2 * width, columns])

    def whole(shape):
        return pl.BlockSpec(shape, lambda p: (0,) * len(shape), pipeline_mode=pl.Buffered(1))

    def one(shape):
        return pl.BlockSpec((1,) + shape, lambda p: (p, 0, 0))

    kept = jax.ShapeDtypeStruct((steps, width, count), BF)
    total = jax.ShapeDtypeStruct((count, model), F32)
    return pl.pallas_call(
        kernel,
        name="own_experts",
        grid=(steps,),
        in_specs=[whole(rows.shape), whole(upstream.shape), one((parts, count))]
        + [pl.BlockSpec(memory_space=pl.ANY)] * 6,
        out_specs=[whole((count, model))] * 2 + [one((width, count))] * 3 + [one((parts, count))],
        out_shape=[total, total, kept, kept, kept, jax.ShapeDtypeStruct((steps, parts, count), F32)],
        scratch_shapes=[
            pltpu.VMEM((2, 3 * width, model), BF),
            pltpu.SemaphoreType.DMA((2, 3)),
        ],
        cost_estimate=pl.CostEstimate(
            flops=steps * 12 * count * model * width,
            bytes_accessed=steps * 6 * width * model + 24 * count * model,
            transcendentals=0,
        ),
        compiler_params=pltpu.CompilerParams(
            vmem_limit_bytes=VMEM_LIMIT, dimension_semantics=("arbitrary",)
        ),
    )(rows, upstream, gates, *weights)


def group_gradients(place, rows, upstream, row_cols, up_cols, gates, kept, weights):
    chips, count, model = rows.shape
    steps, _, parts, _ = gates.shape
    width = weights[3].shape[0]
    half = row_cols.shape[2] // 2

    def kernel(place_ref, x_ref, c_ref, xc, cc, g_ref, kept_h, kept_g, kept_u, gw, uw, dw, sg, su, sd,
               own_g, own_u, own_d, far_g, far_u, far_d, held, sems, sum_g, sum_u, sum_d):
        step = pl.program_id(0)
        turn = pl.program_id(1)
        slot = lax.rem(step, 2)
        routed, shared = (gw, uw, dw), (sg, su, sd)

        @pl.when(turn == 0)
        def _():
            @pl.when(step == 0)
            def _():
                weight_copies(routed, shared, held, sems, step, slot, steps, width, True)

            sum_g[...] = nn(kept_g[0], xc[0])
            sum_u[...] = nn(kept_u[0], xc[0])
            sum_d[...] = nn(kept_h[0], cc[0])
            weight_copies(routed, shared, held, sems, step, slot, steps, width, False)

            @pl.when(step < steps - 1)
            def _():
                weight_copies(routed, shared, held, sems, step + 1, 1 - slot, steps, width, True)

        @pl.when(turn > 0)
        def _():
            unit = width // 2
            x = x_ref[0]
            c = c_ref[0]
            gate = gate_rows(g_ref[0, 0], width)
            for at in range(0, width, unit):
                gate_pre = nt(held[slot, at : at + unit], x)
                up_pre = nt(held[slot, width + at : width + at + unit], x)
                hidden_grad = nt(held[slot, 2 * width + at : 2 * width + at + unit], c)
                hidden, d_gate, d_up, _ = expert_unit(
                    gate_pre, up_pre, hidden_grad, gate[at : at + unit]
                )
                sum_g[at : at + unit] += nn(d_gate, xc[0])
                sum_u[at : at + unit] += nn(d_up, xc[0])
                sum_d[at : at + unit] += nn(hidden, cc[0])

        @pl.when(turn == chips - 1)
        def _():
            for total, near, far in ((sum_g, own_g, far_g), (sum_u, own_u, far_u), (sum_d, own_d, far_d)):
                near[...] = total[:, :half]
                far[...] = total[:, half:].astype(BF)

    def at_chip(shape):
        return pl.BlockSpec((1,) + shape, lambda p, k, z: (lax.rem(z[0] + k, chips), 0, 0))

    def one(shape):
        return pl.BlockSpec((1,) + shape, lambda p, k, z: (p, 0, 0))

    block = pl.BlockSpec((width, half), lambda p, k, z: (p, 0))
    flops = steps * 2 * width * count * (3 * (chips - 1) * model + 6 * chips * half)
    return pl.pallas_call(
        kernel,
        name="group_gradients",
        grid_spec=pltpu.PrefetchScalarGridSpec(
            num_scalar_prefetch=1,
            grid=(steps, chips),
            in_specs=[at_chip((count, model))] * 2
            + [at_chip((count, 2 * half))] * 2
            + [pl.BlockSpec((1, 1, parts, count), lambda p, k, z: (p, lax.rem(z[0] + k, chips), 0, 0))]
            + [one((width, count))] * 3
            + [pl.BlockSpec(memory_space=pl.ANY)] * 6,
            out_specs=[block] * 6,
            scratch_shapes=[
                pltpu.VMEM((2, 3 * width, model), BF),
                pltpu.SemaphoreType.DMA((2, 3)),
            ]
            + [pltpu.VMEM((width, 2 * half), F32)] * 3,
        ),
        out_shape=[jax.ShapeDtypeStruct((steps * width, half), F32)] * 3
        + [jax.ShapeDtypeStruct((steps * width, half), BF)] * 3,
        cost_estimate=pl.CostEstimate(
            flops=flops, bytes_accessed=steps * (6 * width * model + 4 * chips * count * model), transcendentals=0
        ),
        compiler_params=pltpu.CompilerParams(
            vmem_limit_bytes=VMEM_LIMIT, dimension_semantics=("arbitrary", "arbitrary")
        ),
    )(place, rows, upstream, row_cols, up_cols, gates, *kept, *weights)


def attention_forward(place, queries, latents, latent_up, key_ids, query_ids):
    count = queries.shape[0]
    heads = queries.shape[1] // 256
    scale = (ND + RD) ** (-0.5) * LOG2E

    def kernel(place_ref, q_ref, lat_ref, up_ref, kid_ref, qid_ref, att_ref, lse_ref, keys, top, low, mix):
        top[...] = jnp.full_like(top, -1e30)
        low[...] = jnp.zeros_like(low)
        mix[...] = jnp.zeros_like(mix)

        def chunk(at, masked):
            rows = pl.ds(pl.multiple_of(at * count, count), count)
            lat = lat_ref[rows, :KVL]
            rope = lat_ref[rows, KVL:]
            for h in range(heads):
                keys[h, :, ND:] = rope
                both = nn(lat, up_ref[:, h * 256 : (h + 1) * 256]).astype(BF)
                keys[h, :, :ND] = both[:, :ND]
                values = both[:, ND:].T
                scores = nt(keys[h], q_ref[:, h * 256 : (h + 1) * 256]) * scale
                if masked:
                    scores = jnp.where(kid_ref[...] <= qid_ref[...], scores, -1e30)
                before = top[h]
                highest = jnp.maximum(before, jnp.max(scores, axis=0, keepdims=True))
                weights = jnp.exp2(scores - highest)
                decay = jnp.exp2(before - highest)
                top[h] = highest
                low[h] = low[h] * decay + jnp.sum(weights, axis=0, keepdims=True)
                mix[h] = mix[h] * decay + nn(values, weights.astype(BF))

        place_at = place_ref[0]
        lax.fori_loop(0, place_at, lambda at, carry: (chunk(at, False), carry)[1], 0)
        chunk(place_at, True)
        for h in range(heads):
            att_ref[:, h * VD : (h + 1) * VD] = (mix[h] / low[h]).T.astype(BF)
            lse_ref[h] = top[h] + jnp.log2(low[h])

    def whole(shape):
        return pl.BlockSpec(shape, lambda i, z: (0,) * len(shape), pipeline_mode=pl.Buffered(1))

    return pl.pallas_call(
        kernel,
        name="attention_forward",
        grid_spec=pltpu.PrefetchScalarGridSpec(
            num_scalar_prefetch=1,
            grid=(1,),
            in_specs=[whole(a.shape) for a in (queries, latents, latent_up, key_ids, query_ids)],
            out_specs=[whole((count, heads * VD)), whole((heads, 1, count))],
            scratch_shapes=[
                pltpu.VMEM((heads, count, 256), BF),
                pltpu.VMEM((heads, 1, count), F32),
                pltpu.VMEM((heads, 1, count), F32),
                pltpu.VMEM((heads, VD, count), F32),
            ],
        ),
        out_shape=[
            jax.ShapeDtypeStruct((count, heads * VD), BF),
            jax.ShapeDtypeStruct((heads, 1, count), F32),
        ],
        cost_estimate=pl.CostEstimate(
            flops=heads * count * latents.shape[0] * 2 * 640, bytes_accessed=12_000_000, transcendentals=0
        ),
        compiler_params=pltpu.CompilerParams(
            vmem_limit_bytes=VMEM_LIMIT, dimension_semantics=("arbitrary",)
        ),
    )(place, queries, latents, latent_up, key_ids, query_ids)


def attention_backward(place, queries, latents, latent_up, key_ids, query_ids, mix_grad, lse, delta):
    count = queries.shape[0]
    heads = queries.shape[1] // 256
    total = latents.shape[0]
    factor = (ND + RD) ** (-0.5)
    scale = factor * LOG2E

    def kernel(place_ref, q_ref, lat_ref, up_ref, kid_ref, qid_ref, do_ref, lse_ref, delta_ref,
               dq_ref, dup_ref, dlat_ref, keys, dq, dlat):
        dq[...] = jnp.zeros_like(dq)
        dup_ref[...] = jnp.zeros_like(dup_ref)

        def chunk(at, masked):
            rows = pl.ds(pl.multiple_of(at * count, count), count)
            lat = lat_ref[rows, :KVL]
            turned = lat.T
            rope = lat_ref[rows, KVL:]
            dlat[...] = jnp.zeros_like(dlat)
            for h in range(heads):
                up = up_ref[:, h * 256 : (h + 1) * 256]
                query = q_ref[:, h * 256 : (h + 1) * 256]
                upstream = do_ref[:, h * VD : (h + 1) * VD]
                keys[h, :, ND:] = rope
                both = nn(lat, up).astype(BF)
                keys[h, :, :ND] = both[:, :ND]
                scores = nt(keys[h], query) * scale
                chances = jnp.exp2(scores - lse_ref[h])
                if masked:
                    chances = jnp.where(kid_ref[...] <= qid_ref[...], chances, 0.0)
                chance_grad = nt(both[:, ND:], upstream)
                score_grad = (chances * (chance_grad - delta_ref[h])).astype(BF)
                value_grad = nn(chances.astype(BF), upstream)
                key_grad = nn(score_grad, query) * factor
                dq[h] += nn(keys[h].T, score_grad)
                both_grad = jnp.concatenate([key_grad[:, :ND], value_grad], axis=1).astype(BF)
                dlat[:, :KVL] += nt(both_grad, up)
                dlat[:, KVL:] += key_grad[:, ND:]
                dup_ref[:, h * 256 : (h + 1) * 256] += nn(turned, both_grad)
            dlat_ref[rows, :] = dlat[...].astype(BF)

        place_at = place_ref[0]
        lax.fori_loop(0, place_at, lambda at, carry: (chunk(at, False), carry)[1], 0)
        chunk(place_at, True)

        def clear(at, carry):
            rows = pl.ds(pl.multiple_of(at * count, count), count)
            dlat_ref[rows, :] = jnp.zeros((count, LAT), BF)
            return carry

        lax.fori_loop(place_at + 1, total // count, clear, 0)
        for h in range(heads):
            dq_ref[:, h * 256 : (h + 1) * 256] = dq[h].T * factor

    def whole(shape):
        return pl.BlockSpec(shape, lambda i, z: (0,) * len(shape), pipeline_mode=pl.Buffered(1))

    ins = (queries, latents, latent_up, key_ids, query_ids, mix_grad, lse, delta)
    outs = [
        jax.ShapeDtypeStruct((count, heads * 256), F32),
        jax.ShapeDtypeStruct((KVL, heads * 256), F32),
        jax.ShapeDtypeStruct((total, LAT), BF),
    ]
    return pl.pallas_call(
        kernel,
        name="attention_backward",
        grid_spec=pltpu.PrefetchScalarGridSpec(
            num_scalar_prefetch=1,
            grid=(1,),
            in_specs=[whole(a.shape) for a in ins],
            out_specs=[whole(o.shape) for o in outs],
            scratch_shapes=[
                pltpu.VMEM((heads, count, 256), BF),
                pltpu.VMEM((heads, 256, count), F32),
                pltpu.VMEM((count, LAT), F32),
            ],
        ),
        out_shape=outs,
        cost_estimate=pl.CostEstimate(
            flops=heads * count * total * 2 * 1400, bytes_accessed=24_000_000, transcendentals=0
        ),
        compiler_params=pltpu.CompilerParams(
            vmem_limit_bytes=VMEM_LIMIT, dimension_semantics=("arbitrary",)
        ),
    )(place, *ins)


def router_of(rows, router_weight, route_rows):
    logits = lax.dot_general(
        router_weight, rows, (((0,), (1,)), ((), ())), preferred_element_type=F32
    )
    named = jnp.any(
        route_rows.T[None, :, :] == jnp.arange(EXPERTS, dtype=jnp.int32)[:, None, None], axis=1
    )
    return jax.nn.softmax(logits, axis=0), named


def grouped(gates, steps):
    parts = EXPERTS // (steps - 1)
    gates = gates.reshape((steps - 1, parts) + gates.shape[1:])
    return jnp.concatenate([gates, jnp.ones((1,) + gates.shape[1:], F32)], axis=0)


def shards(
    tokens,
    cotangent,
    block_ids,
    routes,
    first_gain,
    query_weight,
    latent_down,
    latent_gain,
    latent_up,
    output_weight,
    second_gain,
    router_weight,
    gate_weight,
    up_weight,
    down_weight,
    shared_gate,
    shared_up,
    shared_down,
):
    count, model = tokens.shape
    key_count = block_ids.shape[0]
    heads = query_weight.shape[1] // (ND + RD)
    unit = gate_weight.shape[2]
    width = shared_down.shape[0]
    steps = EXPERTS * unit // width + 1
    chips = lax.axis_size("dpo")
    ranks = lax.axis_size("tensor")
    devices = chips * 2 * ranks
    chip, core, rank = lax.axis_index("dpo"), lax.axis_index("core"), lax.axis_index("tensor")
    place = chip * 2 + core
    quarter = count // ranks
    half = model // (2 * chips)
    routed_rows = EXPERTS * unit

    def mine(array):
        return lax.dynamic_slice_in_dim(array, rank * quarter, quarter, 0)

    weights = (
        jnp.swapaxes(gate_weight, 1, 2).reshape(routed_rows, model),
        jnp.swapaxes(up_weight, 1, 2).reshape(routed_rows, model),
        down_weight.reshape(routed_rows, model),
        shared_gate.T,
        shared_up.T,
        shared_down,
    )

    row_start = place * count
    cosine, sine_table = rotary_tables((row_start + jnp.arange(count, dtype=jnp.int32)) % key_count)
    own_blocks = lax.dynamic_slice_in_dim(block_ids, row_start, count, 0)
    rows_float = tokens.astype(F32)
    normed_first, first_factor = norm_rows(rows_float, first_gain)
    attention_input = normed_first.astype(BF)
    compressed = nn(attention_input, latent_down)
    latent_raw = compressed[:, :KVL]
    latent_float, latent_factor = norm_rows(latent_raw, latent_gain)
    key_rope = rotate(compressed[:, KVL:], cosine, sine_table)
    latent = jnp.concatenate(
        [latent_float, key_rope, jnp.zeros((count, LAT - KVL - RD), F32)], axis=1
    ).astype(BF)
    latents = lax.all_gather(mine(latent), ALL, axis=0, tiled=True)

    upstream_quarter = mine(cotangent)
    after = lax.optimization_barrier((latents, upstream_quarter, mine(routes)))
    latents = after[0]
    all_upstream = lax.all_gather(after[1], SPREAD, axis=0, tiled=True)
    all_routes = lax.all_gather(after[2], SPREAD, axis=0, tiled=True)

    query_raw = nn(attention_input, query_weight).reshape(count, heads, ND + RD)
    queries = jnp.concatenate(
        [
            query_raw[..., :ND],
            rotate(query_raw[..., ND:], cosine[:, None], sine_table[:, None]),
            jnp.zeros((count, heads, 256 - ND - RD), F32),
        ],
        axis=-1,
    ).astype(BF).reshape(count, heads * 256)
    place_arg = place.reshape(1).astype(jnp.int32)
    key_ids, query_ids = own_blocks[:, None], own_blocks[None, :]
    attended, lse = attention_forward(place_arg, queries, latents, latent_up, key_ids, query_ids)

    attention_part = nn(attended, output_weight).astype(BF)
    residual = mine(tokens).astype(F32) + lax.psum_scatter(
        attention_part, "tensor", scatter_dimension=0, tiled=True
    ).astype(F32)
    normed_second, second_factor = norm_rows(residual, second_gain)
    input_quarter = normed_second.astype(BF)
    expert_input = lax.all_gather(input_quarter, "tensor", axis=0, tiled=True)
    after = lax.optimization_barrier((expert_input, input_quarter))
    expert_input = after[0]
    all_input = lax.all_gather(after[1], SPREAD, axis=0, tiled=True)

    router, named = router_of(expert_input, router_weight, routes)
    own_gates = grouped(jnp.where(named, router, 0.0), steps)
    expert_part, input_back, kept_h, kept_g, kept_u, dots = own_experts(
        expert_input, cotangent, own_gates, weights
    )
    expert_total = lax.psum_scatter(
        expert_part.astype(BF), "tensor", scatter_dimension=0, tiled=True
    ).astype(F32)
    pair_grad = jnp.where(named, dots[: steps - 1].reshape(EXPERTS, count), 0.0)
    logit_grad = router * (pair_grad - jnp.sum(router * pair_grad, axis=0, keepdims=True))
    logit_low = logit_grad.astype(BF)
    grad_router = lax.dot_general(
        expert_input, logit_low, (((0,), (1,)), ((), ())), preferred_element_type=F32
    )
    input_back = input_back + lax.dot_general(
        logit_low, router_weight, (((0,), (1,)), ((), ())), preferred_element_type=F32
    )
    input_grad = lax.psum_scatter(
        input_back.astype(BF), "tensor", scatter_dimension=0, tiled=True
    ).astype(F32)
    residual_back, grad_second_gain = norm_back(residual, second_factor, second_gain, input_grad)
    residual_grad = residual_back + upstream_quarter.astype(F32)
    output_grad = lax.all_gather(residual_grad.astype(BF), "tensor", axis=0, tiled=True)
    result = lax.all_gather(
        (residual + expert_total).astype(BF), "tensor", axis=0, tiled=True
    )
    early = jnp.concatenate(
        [
            grad_router.reshape(devices, -1),
            jnp.repeat(grad_second_gain.reshape(2 * chips, -1), ranks, axis=0),
        ],
        axis=1,
    )
    early = lax.psum_scatter(early, ALL, scatter_dimension=0, tiled=True).reshape(-1)
    router_size = model // devices * EXPERTS
    grad_router = early[:router_size].reshape(-1, EXPERTS)
    grad_second_gain = early[router_size:]

    all_input = all_input.reshape(chips, count, model)
    all_upstream = all_upstream.reshape(chips, count, model)
    all_router, all_named = router_of(
        all_input.reshape(chips * count, model), router_weight, all_routes
    )
    all_gates = jnp.swapaxes(
        grouped(jnp.where(all_named, all_router, 0.0), steps).reshape(steps, -1, chips, count), 1, 2
    )

    def chip_columns(array):
        return jnp.concatenate(
            [
                lax.dynamic_slice_in_dim(array, (chip * 2 + c) * half, half, 2)
                for c in (core, 1 - core)
            ],
            axis=2,
        )

    grads = group_gradients(
        chip.reshape(1).astype(jnp.int32),
        all_input,
        all_upstream,
        chip_columns(all_input),
        chip_columns(all_upstream),
        all_gates,
        (kept_h, kept_g, kept_u),
        weights,
    )
    swap = [(0, 1), (1, 0)]
    grads = [near + lax.ppermute(far, "core", swap).astype(F32) for near, far in zip(grads[:3], grads[3:])]

    grad_output = tn(attended, output_grad)
    attended_grad = nt(output_grad, output_weight).astype(BF)
    delta = jnp.sum(
        (attended.astype(F32) * attended_grad.astype(F32)).reshape(count, heads, VD), axis=2
    ).T[:, None, :]
    query_back, grad_latent_up, latent_part = attention_backward(
        place_arg, queries, latents, latent_up, key_ids, query_ids, attended_grad, lse, delta
    )
    compressed_grad = lax.psum_scatter(
        latent_part, DP, scatter_dimension=0, tiled=True
    ).astype(F32)
    query_back = query_back.reshape(count, heads, 256)
    query_grad = jnp.concatenate(
        [
            query_back[..., :ND],
            rotate(query_back[..., ND : ND + RD], cosine[:, None], -sine_table[:, None]),
        ],
        axis=-1,
    ).astype(BF).reshape(count, heads * (ND + RD))
    grad_query = tn(attention_input, query_grad)
    latent_grad, grad_latent_gain = norm_back(
        latent_raw, latent_factor, latent_gain, compressed_grad[:, :KVL]
    )
    down_grad = jnp.concatenate(
        [latent_grad, rotate(compressed_grad[:, KVL : KVL + RD], cosine, -sine_table)], axis=1
    ).astype(BF)
    grad_latent_down = tn(attention_input, down_grad)
    attention_grad = nt(query_grad, query_weight) + nt(down_grad, latent_down)
    grad_first_gain = jnp.sum(attention_grad * rows_float * first_factor, axis=0)
    attention_grad = lax.psum_scatter(
        attention_grad.astype(BF), "tensor", scatter_dimension=0, tiled=True
    ).astype(F32)
    token_back, _ = norm_back(
        mine(tokens).astype(F32), mine(first_factor), first_gain, attention_grad
    )
    token_grad = lax.all_gather(
        (token_back + residual_grad).astype(BF), "tensor", axis=0, tiled=True
    )
    late = jnp.concatenate(
        [
            grad_latent_down.reshape(devices, -1),
            jnp.repeat(grad_first_gain.reshape(2 * chips, -1), ranks, axis=0),
            grad_latent_gain.reshape(devices, -1),
        ],
        axis=1,
    ).astype(BF)
    late = lax.psum_scatter(late, ALL, scatter_dimension=0, tiled=True).astype(F32).reshape(-1)
    down_size = model // devices * (KVL + RD)
    gain_size = model // (2 * chips)

    def scattered(array, dimension):
        return lax.psum_scatter(
            array.astype(BF), DP, scatter_dimension=dimension, tiled=True
        ).astype(F32)

    def routed_of(array):
        return array[:routed_rows].reshape(EXPERTS, unit, half)

    return (
        result,
        token_grad,
        late[down_size : down_size + gain_size],
        scattered(grad_query, 0),
        late[:down_size].reshape(-1, KVL + RD),
        late[down_size + gain_size :],
        scattered(grad_latent_up, 0),
        scattered(grad_output, 1),
        grad_second_gain,
        grad_router,
        jnp.swapaxes(routed_of(grads[0]), 1, 2),
        jnp.swapaxes(routed_of(grads[1]), 1, 2),
        routed_of(grads[2]),
        grads[0][routed_rows:].T,
        grads[1][routed_rows:].T,
        grads[2][routed_rows:],
    )


def solution(mesh):
    groups, ranks = mesh.devices.shape
    fine = Mesh(mesh.devices.reshape(groups // 2, 2, ranks), ("dpo", "core", "tensor"))
    in_specs = (
        P(DP, None),
        P(DP, None),
        P(),
        P(DP, None),
        P(),
        P(None, "tensor"),
        P(),
        P(),
        P(None, "tensor"),
        P("tensor", None),
        P(),
        P(),
        P(None, None, "tensor"),
        P(None, None, "tensor"),
        P(None, "tensor", None),
        P(None, "tensor"),
        P(None, "tensor"),
        P("tensor", None),
    )
    out_specs = (
        P(DP, None),
        P(DP, None),
        P(DP),
        P(DP, "tensor"),
        P(ALL, None),
        P(ALL),
        P(DP, "tensor"),
        P("tensor", DP),
        P(DP),
        P(ALL, None),
        P(None, DP, "tensor"),
        P(None, DP, "tensor"),
        P(None, "tensor", DP),
        P(DP, "tensor"),
        P(DP, "tensor"),
        P("tensor", DP),
    )
    return jax.shard_map(shards, mesh=fine, in_specs=in_specs, out_specs=out_specs, check_vma=False)
```

time: 1910 us -> 1270 us (0.66)
  matrix products: 442 us -> 48.5 us
  Pallas kernels: 0 us -> 265 us
  other arithmetic: 287 us -> 63.1 us
  waiting for transfers between devices: 941 us -> 756 us
  local copies, waits for them, and re-layouts: 145 us -> 59 us
  blocking collectives: 75 us -> 38.8 us
    reduce_scatter x11 -> x8, waiting for transfers between devices: 779 us -> 294 us  [the longest x1 73.8 us: shards(): lax.psum_scatter(latent_part, DP, scatter_dimension=0, tiled=True)]
    dot_general x68 -> x13, matrix products: 437 us -> 48.5 us  [the longest x3 12 us: nn(): return jnp.dot(former, latter, preferred_element_type=F32)]
    all_gather x1 -> x7, waiting for transfers between devices: 15.6 us -> 337 us  [the longest x1 91.4 us: shards(): all_upstream = lax.all_gather(after[1], SPREAD, axis=0, tiled=True)]
    pallas_call x0 -> x4, Pallas kernels: none -> 265 us  [the longest x1 163 us: group_gradients(): pl.pallas_call(kernel, name='group_gradients', grid_spec=pltpu.PrefetchSc...]
    scatter-add x3 -> x0, other arithmetic: 154 us -> none  [the longest x1 60.9 us: shards(): input_grad = input_grad + jnp.zeros((row_count + 1, model_width), jnp.flo...]
    psum x3 -> x0, waiting for transfers between devices: 146 us -> none  [the longest x1 69.6 us: shards(): lax.psum(input_grad.astype(jnp.bfloat16), 'tensor').astype(jnp.float32)]
    unnamed x17 -> x19, waiting for transfers between devices: 0.28 us -> 125 us
    gather x4 -> x0, local copies, waits for them, and re-layouts: 98.6 us -> none  [the longest x1 37.4 us: shards(): jnp.concatenate([expert_input, jnp.zeros((1, model_width), jnp.bfloat16)]...]
  transfers between devices with their start and end apart: 16 -> 20, of which waited for: 12 -> 15; matrix products, arithmetic and copies ran while one was open for 19% -> 9% of each run, Pallas kernels for 0% -> 13%
where the time goes in v1:
time: 1270 us; the launch traced here: 1260 us
  waiting for transfers between devices  756 us (60%)
  Pallas kernels  265 us (21%)
  other arithmetic  63.1 us (5%)
  local copies, waits for them, and re-layouts  59 us (5%)
  matrix products  48.5 us (4%)
  blocking collectives  38.8 us (3%)
  between operations  14.9 us (1%)
    pallas_call x1, Pallas kernels, group_gradients(): pl.pallas_call(kernel, name='group_gradients', grid_spec=pltpu.PrefetchSc...  163 us
    unnamed x19, waiting for transfers between devices  125 us
    all_gather x1, waiting for transfers between devices, shards(): all_upstream = lax.all_gather(after[1], SPREAD, axis=0, tiled=True)  91.4 us
    pallas_call x1, Pallas kernels, own_experts(): pl.pallas_call(kernel, name='own_experts', grid=(steps,), in_specs=[whole...  80.6 us
    reduce_scatter x1, waiting for transfers between devices, shards(): lax.psum_scatter(latent_part, DP, scatter_dimension=0, tiled=True)  73.8 us
    reduce_scatter x1, waiting for transfers between devices, shards(): lax.psum_scatter(attention_part, 'tensor', scatter_dimension=0, tiled=True)  59.1 us
    reduce_scatter x3, waiting for transfers between devices, scattered(): lax.psum_scatter(array.astype(BF), DP, scatter_dimension=dimension, tiled...  57.9 us
    all_gather x1, waiting for transfers between devices, shards(): all_input = lax.all_gather(after[1], SPREAD, axis=0, tiled=True)  56.3 us
  transfers between devices with their start and end apart: 20, of which 15 were waited for; matrix products, arithmetic and copies ran while one was open for 9% of the time, Pallas kernels for 13%

profile of v1, /device:TPU:0, one launch (start us, length us, event | category | flops | bytes accessed | tf_op | source)
XLA Modules:
  0.0 1255.4 jit_solution(8037761129425653441)
XLA Ops:
  10.2 4.2 fusion.51
  34.7 54.5 %all-gather.8.cloned.1.call-done.lat_ref = bf16[4096,640]{1,0:T(8,128)(2,1)} async-done(((bf16[128,640]{1,0:T(8,128)(2,1)}), bf16[4096,640]{1,0:T(8,128)(2,1)}) %all-gather.8.cloned.1.call-update) | async-done | bytes 5242896 | tf_op jit(solution)/shard_map/all_gather | solution.py:507
  89.1 7.9 attention_forward.1
  97.1 4.3 convolution_convert_fusion.3
  101.5 59.1 %reduce-scatter.9.cloned.1.call-done = bf16[128,2048]{1,0:T(8,128)(2,1)} async-done(((bf16[512,2048]{1,0:T(8,128)(2,1)}), bf16[128,2048]{1,0:T(8,128)(2,1)}) %reduce-scatter.9.cloned.1.call-update) | async-done | bytes 524304 | tf_op jit(solution)/shard_map/reduce_scatter | solution.py:529
  164.4 35.3 %all-gather.10.cloned.1.call-done.x_ref = bf16[512,2048]{1,0:T(8,128)(2,1)} async-done(((bf16[128,2048]{1,0:T(8,128)(2,1)}), bf16[512,2048]{1,0:T(8,128)(2,1)}) %all-gather.10.cloned.1.call-update) | async-done | bytes 2097168 | tf_op jit(solution)/shard_map/all_gather | solution.py:534
  202.7 80.6 %own_experts.1 = (f32[512,2048]{1,0:T(8,128)}, f32[512,2048]{1,0:T(8,128)}, bf16[7,704,512]{2,1,0:T(8,128)(2,1)}, bf16[7,704,512]{2,1,0:T(8,128)(2,1)}, bf16[7,7...) custom-call(bf16[512,2048]{1,0:T(8,128)(2,1)} %all-gather.10.cloned.1.call-done.x_ref, bf16[512,2048]{1,0:T(8,128)(2,1)} %c_ref.1, ...), custom_call_target="tpu_custom_call" | custom-call | flops 62008590336 | bytes 85721088 | tf_op jit(solution)/shard_map/own_experts/pallas_call | solution.py:166
  284.2 4.2 add_convert_fusion
  288.5 35.3 %reduce-scatter.13.cloned.1.call-done = bf16[128,2048]{1,0:T(8,128)(2,1)} async-done(((bf16[512,2048]{1,0:T(8,128)(2,1)}), bf16[128,2048]{1,0:T(8,128)(2,1)}) %reduce-scatter.13.cloned.1.call-update) | async-done | bytes 524304 | tf_op jit(solution)/shard_map/reduce_scatter | solution.py:556
  329.0 8.8 reduce-scatter.15.cloned.1.call-start
  337.7 26.7 %all-gather.14.cloned.1.call-done = bf16[512,2048]{1,0:T(8,128)(2,1)} async-done(((bf16[128,2048]{1,0:T(8,128)(2,1)}), bf16[512,2048]{1,0:T(8,128)(2,1)}) %all-gather.14.cloned.1.call-update) | async-done | bytes 2097168 | tf_op jit(solution)/shard_map/all_gather | solution.py:561
  364.4 4.7 convert_multiply_fusion.8
  375.6 12.8 %attention_backward.1 = (f32[512,1024]{1,0:T(8,128)}, f32[512,1024]{1,0:T(8,128)}, bf16[4096,640]{1,0:T(8,128)(2,1)}) custom-call(s32[1]{0:T(128)} %bitcast.place_ref, bf16[512,1024]{1,0:T(8,128)(2,1)} %copy.114.q_ref, bf16[4096,640]{1,0:T(8,128)(2,1)} %all-gather.8.cloned.1.call-done.lat_ref, bf16[512,1024]{1,0:T(8,128)(2,1)} %up_ref.3, ...), custom_call_target="tpu_custom_call" | custom-call | flops 23488102400 | bytes 24000000 | tf_op jit(solution)/shard_map/attention_backward/pallas_call | solution.py:407
  399.2 4.4 convolution_convert_fusion.2
  408.6 73.8 %reduce-scatter.15.cloned.1.call-done = bf16[512,640]{1,0:T(8,128)(2,1)} async-done(((bf16[4096,640]{1,0:T(8,128)(2,1)}), bf16[512,640]{1,0:T(8,128)(2,1)}) %reduce-scatter.15.cloned.1.call-update) | async-done | bytes 655376 | tf_op jit(solution)/shard_map/reduce_scatter | solution.py:616
  498.3 38.8 %all_gather.31 = s32[2048,6]{0,1:T(8,128)S(1)} all-gather(s32[128,6]{0,1:T(8,128)S(1)} %copy-done.30), channel_id=1, replica_groups=mesh['dpo'=4,'core'=2,'tensor'=4] {'dpo','tensor'}, dimensions={0}, use_global_device_ids=true | all-gather | bytes 52224 | tf_op jit(solution)/shard_map/all_gather | solution.py:513
  537.4 3.8 convert_element_type.122
  541.4 56.3 %all-gather.18.cloned.1.call-done = bf16[2048,2048]{1,0:T(8,128)(2,1)} async-done(((bf16[128,2048]{1,0:T(8,128)(2,1)}), bf16[2048,2048]{1,0:T(8,128)(2,1)}) %all-gather.18.cloned.1.call-update) | async-done | bytes 8388624 | tf_op jit(solution)/shard_map/all_gather | solution.py:537
  597.7 5.7 fusion.56
  606.5 4.4 copy.107
  610.9 5.6 reshape.291
  620.7 91.4 %all-gather.20.cloned.1.call-done = bf16[2048,2048]{1,0:T(8,128)(2,1)} async-done(((bf16[128,2048]{1,0:T(8,128)(2,1)}), bf16[2048,2048]{1,0:T(8,128)(2,1)}) %all-gather.20.cloned.1.call-update) | async-done | bytes 8388624 | tf_op jit(solution)/shard_map/all_gather | solution.py:512
  721.7 163.5 %group_gradients.1 = (f32[4928,256]{1,0:T(8,128)}, f32[4928,256]{1,0:T(8,128)}, f32[4928,256]{1,0:T(8,128)}, bf16[4928,256]{1,0:T(8,128)(2,1)}, bf16[4928,256]{1,0:T(8,128)(2,1)}, /*index=5*/bf16[4928,256]{1,0:T(8,128)(2,1)}) custom-call(s32[1]{0:T(128)} %bitcast.19.place_ref, bf16[4,512,2048]{2,1,0:T(8,128)(2,1)} %bitcast.71, ...), custom_call_target="tpu_custom_call" | custom-call | flops 124017180672 | bytes 177995776 | tf_op jit(solution)/shard_map/group_gradients/pallas_call | solution.py:248
  890.3 19.0 %reduce-scatter.23.cloned.1.call-done = bf16[512,256]{1,0:T(8,128)(2,1)} async-done(((bf16[512,2048]{1,0:T(8,128)(2,1)}), bf16[512,256]{1,0:T(8,128)(2,1)}) %reduce-scatter.23.cloned.1.call-update) | async-done | bytes 262160 | tf_op jit(solution)/shard_map/reduce_scatter | solution.py:659
  911.1 3.7 convert_add_fusion
  918.1 30.3 %reduce-scatter.17.cloned.1.call-done = bf16[128,2048]{1,0:T(8,128)(2,1)} async-done(((bf16[512,2048]{1,0:T(8,128)(2,1)}), bf16[128,2048]{1,0:T(8,128)(2,1)}) %reduce-scatter.17.cloned.1.call-update) | async-done | bytes 524304 | tf_op jit(solution)/shard_map/reduce_scatter | solution.py:637
  949.7 37.8 %reduce-scatter.11.cloned.1.call-done = bf16[128,2048]{1,0:T(8,128)(2,1)} async-done(((bf16[512,2048]{1,0:T(8,128)(2,1)}), bf16[128,2048]{1,0:T(8,128)(2,1)}) %reduce-scatter.11.cloned.1.call-update) | async-done | bytes 524304 | tf_op jit(solution)/shard_map/reduce_scatter | solution.py:544
  990.9 3.9 convert_add_fusion.2
  1004.1 123.4 %all-reduce.7.cloned.1.call-done = bf16[32,37136]{1,0:T(8,128)(2,1)} async-done(((bf16[32,37136]{1,0:T(8,128)(2,1)}), bf16[32,37136]{1,0:T(8,128)(2,1)}) %all-reduce.7.cloned.1.call-update) | async-done | bytes 2376720
  1131.0 38.9 %reduce-scatter.19.cloned.1.call-done = bf16[256,768]{1,0:T(8,128)(2,1)} async-done(((bf16[2048,768]{1,0:T(8,128)(2,1)}), bf16[256,768]{1,0:T(8,128)(2,1)}) %reduce-scatter.19.cloned.1.call-update) | async-done | bytes 393232 | tf_op jit(solution)/shard_map/reduce_scatter | solution.py:659
  1171.7 34.8 %all-gather.12.cloned.1.call-done = bf16[512,2048]{1,0:T(8,128)(2,1)} async-done(((bf16[128,2048]{1,0:T(8,128)(2,1)}), bf16[512,2048]{1,0:T(8,128)(2,1)}) %all-gather.12.cloned.1.call-update) | async-done | bytes 2097168 | tf_op jit(solution)/shard_map/all_gather | solution.py:562
  1206.5 37.6 %all-gather.16.cloned.1.call-done = bf16[512,2048]{1,0:T(8,128)(2,1)} async-done(((bf16[128,2048]{1,0:T(8,128)(2,1)}), bf16[512,2048]{1,0:T(8,128)(2,1)}) %all-gather.16.cloned.1.call-update) | async-done | bytes 2097168 | tf_op jit(solution)/shard_map/all_gather | solution.py:643
  (236 shorter events, 125.1 us)
Async XLA Ops:
  7.2 81.9 %all-gather.8.cloned.1.call-start = ((), (), s32[]{:S(2)}) async-start(), calls=%async_computation.8 | async-start | bytes 5406720 | tf_op jit(solution)/shard_map/all_gather | solution.py:507
  20.9 139.7 %reduce-scatter.9.cloned.1.call-start = ((), (), s32[]{:S(2)}) async-start(), calls=%async_computation.9 | async-start | bytes 2621440 | tf_op jit(solution)/shard_map/reduce_scatter | solution.py:529
  101.4 98.3 %copy-start.13 = (bf16[2048,12]{0,1:T(8,128)(2,1)S(1)}, bf16[2048,12]{0,1:T(8,128)(2,1)}, u32[]{:S(2)}) copy-start(bf16[2048,12]{0,1:T(8,128)(2,1)} %param.29) | copy-start | bytes 147460
  101.4 98.3 %all-gather.10.cloned.1.call-start = ((), (), s32[]{:S(2)}) async-start(), calls=%async_computation.10 | async-start | bytes 2621440 | tf_op jit(solution)/shard_map/all_gather | solution.py:534
  162.0 164.1 %copy-start.32 = (f32[128]{0:T(128)}, f32[128]{0:T(128)S(1)}, u32[]{:S(2)}) copy-start(f32[128]{0:T(128)S(1)} %add_rsqrt_fusion.2) | copy-start | bytes 1540
  164.3 159.5 %reduce-scatter.13.cloned.1.call-start = ((), (), s32[]{:S(2)}) async-start(), calls=%async_computation.13 | async-start | bytes 2621440 | tf_op jit(solution)/shard_map/reduce_scatter | solution.py:556
  288.4 76.0 %all-gather.14.cloned.1.call-start = ((), (), s32[]{:S(2)}) async-start(), calls=%async_computation.14 | async-start | bytes 2621440 | tf_op jit(solution)/shard_map/all_gather | solution.py:561
  329.0 153.5 %reduce-scatter.15.cloned.1.call-start = ((), (), s32[]{:S(2)}) async-start(), calls=%async_computation.15 | async-start | bytes 5898240 | tf_op jit(solution)/shard_map/reduce_scatter | solution.py:616
  388.4 209.3 %all-gather.18.cloned.1.call-start = ((), (), s32[]{:S(2)}) async-start(), calls=%async_computation.21 | async-start | bytes 8912896 | tf_op jit(solution)/shard_map/all_gather | solution.py:537
  389.2 322.9 %all-gather.20.cloned.1.call-start = ((), (), s32[]{:S(2)}) async-start(), calls=%async_computation.22 | async-start | bytes 8912896 | tf_op jit(solution)/shard_map/all_gather | solution.py:512
  389.9 495.9 %all-reduce.9.cloned.1.call-start = ((), (), s32[]{:S(2)}) async-start(), calls=%async_computation.24 | async-start | bytes 262144
  396.3 492.4 %reduce-scatter.21.cloned.1.call-start = ((), (), s32[]{:S(2)}) async-start(), calls=%async_computation.19 | async-start | bytes 1179648 | tf_op jit(solution)/shard_map/reduce_scatter | solution.py:659
  399.2 510.1 %reduce-scatter.23.cloned.1.call-start = ((), (), s32[]{:S(2)}) async-start(), calls=%async_computation.20 | async-start | bytes 2359296 | tf_op jit(solution)/shard_map/reduce_scatter | solution.py:659
  403.6 544.8 %reduce-scatter.17.cloned.1.call-start = ((), (), s32[]{:S(2)}) async-start(), calls=%async_computation.16 | async-start | bytes 2621440 | tf_op jit(solution)/shard_map/reduce_scatter | solution.py:637
  406.5 78.2 %copy-start.28 = (f32[512]{0:T(512)S(1)}, f32[512]{0:T(512)}, u32[]{:S(2)}) copy-start(f32[512]{0:T(512)} %copy-done.27) | copy-start | bytes 6148
  406.5 78.2 %copy-start.35 = (f32[32]{0:T(128)S(1)}, f32[32]{0:T(128)}, u32[]{:S(2)}) copy-start(f32[32]{0:T(128)} %multiply_power_fusion) | copy-start | bytes 388
  498.2 489.2 %reduce-scatter.11.cloned.1.call-start = ((), (), s32[]{:S(2)}) async-start(), calls=%async_computation.11 | async-start | bytes 2621440 | tf_op jit(solution)/shard_map/reduce_scatter | solution.py:544
  541.3 62.1 %copy-start.5 = (bf16[512,2048]{1,0:T(8,128)(2,1)S(1)}, bf16[512,2048]{1,0:T(8,128)(2,1)}, u32[]{:S(2)}) copy-start(bf16[512,2048]{1,0:T(8,128)(2,1)} %param.18) | copy-start | bytes 6291460
  541.3 62.1 %copy-start.15 = (bf16[512,512]{1,0:T(8,128)(2,1)S(1)}, bf16[512,512]{1,0:T(8,128)(2,1)}, u32[]{:S(2)}) copy-start(bf16[512,512]{1,0:T(8,128)(2,1)} %copy-done.14) | copy-start | bytes 1572868
  541.3 62.1 %copy-start.20 = (bf16[512,32]{1,0:T(8,128)(2,1)S(1)}, bf16[512,32]{1,0:T(8,128)(2,1)}, u32[]{:S(2)}) copy-start(bf16[512,32]{1,0:T(8,128)(2,1)} %get-tuple-element.141) | copy-start | bytes 98308
  541.3 586.2 %all-reduce.7.cloned.1.call-start = ((), (), s32[]{:S(2)}) async-start(), calls=%async_computation.23 | async-start | bytes 4767744
  619.8 550.0 %reduce-scatter.19.cloned.1.call-start = ((), (), s32[]{:S(2)}) async-start(), calls=%async_computation.18 | async-start | bytes 3538944 | tf_op jit(solution)/shard_map/reduce_scatter | solution.py:659
  721.4 485.0 %all-gather.12.cloned.1.call-start = ((), (), s32[]{:S(2)}) async-start(), calls=%async_computation.12 | async-start | bytes 2621440 | tf_op jit(solution)/shard_map/all_gather | solution.py:562
  885.1 25.9 %collective-permute-start.2 = (bf16[4928,256]{1,0:T(8,128)(2,1)}, bf16[4928,256]{1,0:T(8,128)(2,1)}, u32[]{:S(2)}, u32[]{:S(2)}) collective-permute-start(bf16[4928,256]{1,0:T(8,128)(2,1)} %get-tuple-element.59), channel_id=1, source_target_pairs={{0,4},{4,0},{1,5},{5,1},{2,6},{6,2},{3,7},{7,3},{8,12},{12,8},{9,1... | collective-permute-start | bytes 7569416 | tf_op jit(solution)/shard_map/ppermute | solution.py:606
  885.2 105.6 %collective-permute-start = (bf16[4928,256]{1,0:T(8,128)(2,1)}, bf16[4928,256]{1,0:T(8,128)(2,1)}, u32[]{:S(2)}, u32[]{:S(2)}) collective-permute-start(bf16[4928,256]{1,0:T(8,128)(2,1)} %get-tuple-element.55), channel_id=1, source_target_pairs={{0,4},{4,0},{1,5},{5,1},{2,6},{6,2},{3,7},{7,3},{8,12},{12,8},{9,1... | collective-permute-start | bytes 7569416 | tf_op jit(solution)/shard_map/ppermute | solution.py:606
  911.1 86.1 %collective-permute-start.1 = (bf16[4928,256]{1,0:T(8,128)(2,1)}, bf16[4928,256]{1,0:T(8,128)(2,1)}, u32[]{:S(2)}, u32[]{:S(2)}) collective-permute-start(bf16[4928,256]{1,0:T(8,128)(2,1)} %get-tuple-element.57), channel_id=1, source_target_pairs={{0,4},{4,0},{1,5},{5,1},{2,6},{6,2},{3,7},{7,3},{8,12},{12,8},{9,1... | collective-permute-start | bytes 7569416 | tf_op jit(solution)/shard_map/ppermute | solution.py:606
  917.1 70.3 %copy-start.6 = (bf16[128,2048]{1,0:T(8,128)(2,1)S(1)}, bf16[128,2048]{1,0:T(8,128)(2,1)}, u32[]{:S(2)}) copy-start(bf16[128,2048]{1,0:T(8,128)(2,1)} %reduce-scatter.9.cloned.1.call-done) | copy-start | bytes 1572868
  917.1 70.3 %copy-start.9 = (bf16[128,2048]{1,0:T(8,128)(2,1)S(1)}, bf16[128,2048]{1,0:T(8,128)(2,1)}, u32[]{:S(2)}) copy-start(bf16[128,2048]{1,0:T(8,128)(2,1)} %reduce-scatter.13.cloned.1.call-done) | copy-start | bytes 1572868
  917.1 70.3 %copy-start.17 = (f32[2048]{0:T(1024)S(1)}, f32[2048]{0:T(1024)}, u32[]{:S(2)}) copy-start(f32[2048]{0:T(1024)} %param.28) | copy-start | bytes 24580
  917.1 70.3 %copy-start.33 = (f32[128]{0:T(128)S(1)}, f32[128]{0:T(128)}, u32[]{:S(2)}) copy-start(f32[128]{0:T(128)} %copy-done.32) | copy-start | bytes 1540
  917.2 70.3 %copy-start.40 = (f32[128]{0:T(128)S(1)}, f32[128]{0:T(128)}, u32[]{:S(2)}) copy-start(f32[128]{0:T(128)} %copy-done.39) | copy-start | bytes 1540
  990.8 253.3 %all-gather.16.cloned.1.call-start = ((), (), s32[]{:S(2)}) async-start(), calls=%async_computation.17 | async-start | bytes 2621440 | tf_op jit(solution)/shard_map/all_gather | solution.py:643
  (34 other events, 354.7 us)
Sparse Core Ops, SparseCore 0:
  21.0 68.0 all-gather.7
  101.6 58.9 reduce-scatter.8
  164.4 35.3 all-gather.9
  288.6 35.1 reduce-scatter.12
  329.1 35.2 all-gather.13
  388.5 93.9 reduce-scatter.14
  485.8 111.7 all-gather.17
  601.0 111.0 all-gather.19
  718.2 120.6 all-reduce.8
  841.0 31.4 reduce-scatter.20
  875.3 33.9 reduce-scatter.22
  912.7 35.6 reduce-scatter.16
  952.2 35.2 reduce-scatter.10
  992.8 134.6 all-reduce.6
  1129.7 40.0 reduce-scatter.18
  1172.1 34.3 all-gather.11
  1208.7 35.2 all-gather.15

commit v2 on v1

--- a/solution.py
+++ b/solution.py
@@ -20,6 +20,7 @@
 DP = ("dpo", "core")
 SPREAD = ("dpo", "tensor")
 ALL = ("dpo", "core", "tensor")
+MESH = pl.DeviceIdType.MESH
 
 
 def nn(former, latter):
@@ -186,22 +187,265 @@
     )(rows, upstream, gates, *weights)
 
 
-def group_gradients(place, rows, upstream, row_cols, up_cols, gates, kept, weights):
+def ring_of(axis):
+    here = lax.axis_index(axis)
+    size = lax.axis_size(axis)
+    return here, [lax.rem(here + i, size) for i in range(size)]
+
+
+def greet(devices):
+    barrier = pltpu.get_barrier_semaphore()
+    for device in devices:
+        pl.semaphore_signal(barrier, inc=1, device_id=device, device_id_type=MESH)
+    pl.semaphore_wait(barrier, len(devices))
+
+
+def remote(source, target, send, receive, device):
+    return pltpu.make_async_remote_copy(
+        src_ref=source, dst_ref=target, send_sem=send, recv_sem=receive,
+        device_id=device, device_id_type=MESH,
+    )
+
+
+class Scatter:
+    def __init__(self, rows):
+        ranks = lax.axis_size("tensor")
+        quarter = rows.shape[0] // ranks
+        self.ins = [rows.reshape(ranks, quarter, rows.shape[1])]
+        self.in_specs = [pl.BlockSpec(memory_space=pl.ANY)]
+        self.outs = [jax.ShapeDtypeStruct((ranks - 1, quarter, rows.shape[1]), rows.dtype)]
+        self.out_specs = [pl.BlockSpec(memory_space=pl.ANY)]
+        self.scratch = [pltpu.SemaphoreType.DMA((ranks,)), pltpu.SemaphoreType.DMA((ranks,))]
+
+    def copies(self, refs):
+        source, target, sends, receives = refs
+        _, peers = ring_of("tensor")
+        return [
+            remote(source.at[peer], target.at[d - 1], sends.at[d], receives.at[d], {"tensor": peer})
+            for d, peer in enumerate(peers)
+            if d
+        ]
+
+    def begin(self, refs):
+        _, peers = ring_of("tensor")
+        greet([{"tensor": peer} for peer in peers[1:]])
+        for copy in self.copies(refs):
+            copy.start()
+
+    def middle(self, refs, step, last):
+        pass
+
+    def end(self, refs):
+        for copy in self.copies(refs):
+            copy.wait()
+
+
+class Gather(Scatter):
+    def __init__(self, rows):
+        ranks = lax.axis_size("tensor")
+        self.ins = [rows]
+        self.in_specs = [pl.BlockSpec(memory_space=pl.ANY)]
+        self.outs = [jax.ShapeDtypeStruct((ranks,) + rows.shape, rows.dtype)]
+        self.out_specs = [pl.BlockSpec(memory_space=pl.ANY)]
+        self.scratch = [pltpu.SemaphoreType.DMA((ranks,)), pltpu.SemaphoreType.DMA((ranks,))]
+
+    def copies(self, refs):
+        source, target, sends, receives = refs
+        rank, peers = ring_of("tensor")
+        return [pltpu.make_async_copy(source, target.at[rank], sends.at[0])] + [
+            remote(source, target.at[rank], sends.at[d], receives.at[d], {"tensor": peer})
+            for d, peer in enumerate(peers)
+            if d
+        ]
+
+
+class LineSum:
+    def __init__(self, blocks):
+        chips = lax.axis_size("dpo")
+        self.chips = chips
+        shape = blocks.shape[1:]
+        self.ins = [blocks]
+        self.in_specs = [pl.BlockSpec(memory_space=pl.ANY)]
+        self.outs = [jax.ShapeDtypeStruct(shape, F32)]
+        self.out_specs = [pl.BlockSpec(shape, lambda *_: (0, 0), pipeline_mode=pl.Buffered(1))]
+        self.scratch = [
+            pltpu.VMEM((chips,) + shape, blocks.dtype),
+            pltpu.VMEM((chips,) + shape, blocks.dtype),
+            pltpu.VMEM(shape, blocks.dtype),
+        ] + [pltpu.SemaphoreType.DMA((chips,))] * 4 + [pltpu.SemaphoreType.DMA]
+
+    def swap(self, refs, i):
+        source, _, mate, _, _, sends, receives, _, _, _ = refs
+        core = lax.axis_index("core")
+        return remote(source.at[2 * i + 1 - core], mate.at[i], sends.at[i], receives.at[i], {"core": 1 - core})
+
+    def onward(self, refs, i):
+        _, _, mate, inbox, _, _, _, sends, receives, _ = refs
+        chip = lax.axis_index("dpo")
+        return remote(mate.at[i], inbox.at[i], sends.at[i], receives.at[i], {"dpo": lax.rem(chip + self.chips - 1, self.chips)})
+
+    def begin(self, refs):
+        chip, core = lax.axis_index("dpo"), lax.axis_index("core")
+        barrier = pltpu.get_barrier_semaphore()
+        pl.semaphore_signal(barrier, inc=1, device_id={"core": 1 - core}, device_id_type=MESH)
+
+        @pl.when(chip < self.chips - 1)
+        def _():
+            pl.semaphore_signal(barrier, inc=1, device_id={"dpo": chip + 1}, device_id_type=MESH)
+
+        pl.semaphore_wait(barrier, 1 + jnp.where(chip > 0, 1, 0))
+
+        for i in range(self.chips):
+            @pl.when(i <= chip)
+            def _():
+                self.swap(refs, i).start()
+
+    def middle(self, refs, step, last):
+        source, out, mate, inbox, mine, _, _, _, _, sem = refs
+        chip, core = lax.axis_index("dpo"), lax.axis_index("core")
+        for i in range(self.chips):
+            due = jnp.minimum(1 + 3 * (self.chips - 1 - chip) + i, last)
+
+            @pl.when((i <= chip) & (step == due))
+            def _():
+                local = pltpu.make_async_copy(source.at[2 * i + core], mine, sem)
+                local.start()
+                self.swap(refs, i).wait()
+                local.wait()
+
+                @pl.when(chip < self.chips - 1)
+                def _():
+                    self.onward(refs, i).wait_recv()
+                    mate[i] = (
+                        mate[i].astype(F32) + mine[...].astype(F32) + inbox[i].astype(F32)
+                    ).astype(mate.dtype)
+
+                @pl.when(chip == self.chips - 1)
+                def _():
+                    mate[i] = (mate[i].astype(F32) + mine[...].astype(F32)).astype(mate.dtype)
+
+                @pl.when(chip > i)
+                def _():
+                    self.onward(refs, i).start()
+
+                @pl.when(chip == i)
+                def _():
+                    out[...] = mate[i].astype(F32)
+
+    def end(self, refs):
+        chip = lax.axis_index("dpo")
+        for i in range(self.chips):
+            @pl.when(chip > i)
+            def _():
+                self.onward(refs, i).wait_send()
+
+
+def settle(part, more, gain, finish, extra, collective):
+    count, model = part.shape
+    ranks = lax.axis_size("tensor")
+    quarter = count // ranks
+    n_more, n_extra = len(more), len(extra)
+
+    def kernel(*refs):
+        part_ref, gain_ref = refs[:2]
+        more_refs = refs[2 : 2 + n_more]
+        out_ref = refs[2 + n_more]
+        extra_refs = refs[3 + n_more : 3 + n_more + n_extra]
+        inbox, block, gathered, send, receive, send_on, receive_on = refs[3 + n_more + n_extra :]
+        rank, peers = ring_of("tensor")
+
+        def rows_of(i):
+            return pl.ds(pl.multiple_of(i * quarter, quarter), quarter)
+
+        greet([{"tensor": peer} for peer in peers[1:]])
+        copies = [
+            remote(part_ref.at[rows_of(peer)], inbox.at[d], send.at[d], receive.at[d], {"tensor": peer})
+            for d, peer in enumerate(peers)
+            if d
+        ]
+        for copy in copies:
+            copy.start()
+        total = part_ref[rows_of(rank)].astype(F32)
+        for d, copy in enumerate(copies):
+            copy.wait()
+            total = total + inbox[d + 1].astype(F32)
+        results = finish(total, gain_ref[...], [r[...] for r in more_refs])
+        for ref, value in zip(extra_refs, results):
+            ref[...] = value
+        block[...] = results[-1]
+        copies = [
+            remote(block, gathered.at[d], send_on.at[d], receive_on.at[d], {"tensor": peer})
+            for d, peer in enumerate(peers)
+            if d
+        ]
+        for copy in copies:
+            copy.start()
+        out_ref[rows_of(rank)] = block[...]
+        for d, copy in enumerate(copies):
+            copy.wait()
+            out_ref[rows_of(lax.rem(rank + ranks - d - 1, ranks))] = gathered[d + 1]
+
+    vmem = pl.BlockSpec(memory_space=pltpu.VMEM)
+    sems = [pltpu.SemaphoreType.DMA((ranks,))] * 4
+    return pl.pallas_call(
+        kernel,
+        name="settle",
+        in_specs=[vmem] * (2 + n_more),
+        out_specs=[vmem] * (1 + n_extra),
+        out_shape=[jax.ShapeDtypeStruct((count, model), BF)] + extra,
+        scratch_shapes=[
+            pltpu.VMEM((ranks, quarter, model), BF),
+            pltpu.VMEM((quarter, model), BF),
+            pltpu.VMEM((ranks, quarter, model), BF),
+        ]
+        + sems,
+        cost_estimate=pl.CostEstimate(flops=1000, bytes_accessed=150_000_000, transcendentals=0),
+        compiler_params=pltpu.CompilerParams(
+            vmem_limit_bytes=VMEM_LIMIT, collective_id=collective, has_side_effects=True
+        ),
+    )(part, gain, *more)
+
+
+def group_gradients(rows, upstream, row_cols, up_cols, gates, kept, weights, first, groups, held_back, beside, collective):
     chips, count, model = rows.shape
     steps, _, parts, _ = gates.shape
     width = weights[3].shape[0]
     half = row_cols.shape[2] // 2
-
-    def kernel(place_ref, x_ref, c_ref, xc, cc, g_ref, kept_h, kept_g, kept_u, gw, uw, dw, sg, su, sd,
-               own_g, own_u, own_d, far_g, far_u, far_d, held, sems, sum_g, sum_u, sum_d):
-        step = pl.program_id(0)
+    n_ins = len(beside.ins) if beside else 0
+    n_outs = len(beside.outs) if beside else 0
+    n_held = len(held_back)
+    last = groups * chips - 1
+
+    def kernel(*refs):
+        refs = list(refs)
+
+        def take(n):
+            taken = refs[:n]
+            del refs[:n]
+            return taken
+
+        x_ref, c_ref, xc, cc, g_ref, kept_h, kept_g, kept_u = take(8)
+        routed, shared = take(3), take(3)
+        take(n_held)
+        link_refs = take(n_ins)
+        own_g, own_u, own_d, far_g, far_u, far_d = take(6)
+        link_refs += take(n_outs)
+        held, sems, sum_g, sum_u, sum_d = take(5)
+        link_refs += refs
+        at_group = pl.program_id(0)
         turn = pl.program_id(1)
-        slot = lax.rem(step, 2)
-        routed, shared = (gw, uw, dw), (sg, su, sd)
+        step = at_group + first
+        slot = lax.rem(at_group, 2)
+        tick = at_group * chips + turn
+
+        if beside:
+            @pl.when(tick == 0)
+            def _():
+                beside.begin(link_refs)
 
         @pl.when(turn == 0)
         def _():
-            @pl.when(step == 0)
+            @pl.when(at_group == 0)
             def _():
                 weight_copies(routed, shared, held, sems, step, slot, steps, width, True)
 
@@ -210,7 +454,7 @@
             sum_d[...] = nn(kept_h[0], cc[0])
             weight_copies(routed, shared, held, sems, step, slot, steps, width, False)
 
-            @pl.when(step < steps - 1)
+            @pl.when(at_group < groups - 1)
             def _():
                 weight_copies(routed, shared, held, sems, step + 1, 1 - slot, steps, width, True)
 
@@ -237,57 +481,105 @@
                 near[...] = total[:, :half]
                 far[...] = total[:, half:].astype(BF)
 
+        if beside:
+            beside.middle(link_refs, tick, last)
+
+            @pl.when(tick == last)
+            def _():
+                beside.end(link_refs)
+
+    def chip_at(turn):
+        return lax.rem(lax.axis_index("dpo") + turn, chips)
+
     def at_chip(shape):
-        return pl.BlockSpec((1,) + shape, lambda p, k, z: (lax.rem(z[0] + k, chips), 0, 0))
+        return pl.BlockSpec((1,) + shape, lambda p, k: (chip_at(k), 0, 0))
 
     def one(shape):
-        return pl.BlockSpec((1,) + shape, lambda p, k, z: (p, 0, 0))
-
-    block = pl.BlockSpec((width, half), lambda p, k, z: (p, 0))
-    flops = steps * 2 * width * count * (3 * (chips - 1) * model + 6 * chips * half)
+        return pl.BlockSpec((1,) + shape, lambda p, k: (p + first, 0, 0))
+
+    anywhere = pl.BlockSpec(memory_space=pl.ANY)
+    near_block = pl.BlockSpec((width, half), lambda p, k: (p + first, 0))
+    far_block = pl.BlockSpec((width, half), lambda p, k: (p, 0))
+    flops = groups * 2 * width * count * (3 * (chips - 1) * model + 6 * chips * half)
     return pl.pallas_call(
         kernel,
         name="group_gradients",
         grid_spec=pltpu.PrefetchScalarGridSpec(
-            num_scalar_prefetch=1,
-            grid=(steps, chips),
+            num_scalar_prefetch=0,
+            grid=(groups, chips),
             in_specs=[at_chip((count, model))] * 2
             + [at_chip((count, 2 * half))] * 2
-            + [pl.BlockSpec((1, 1, parts, count), lambda p, k, z: (p, lax.rem(z[0] + k, chips), 0, 0))]
+            + [pl.BlockSpec((1, 1, parts, count), lambda p, k: (p + first, chip_at(k), 0, 0))]
             + [one((width, count))] * 3
-            + [pl.BlockSpec(memory_space=pl.ANY)] * 6,
-            out_specs=[block] * 6,
+            + [anywhere] * (6 + n_held)
+            + (beside.in_specs if beside else []),
+            out_specs=[near_block] * 3 + [far_block] * 3 + (beside.out_specs if beside else []),
             scratch_shapes=[
                 pltpu.VMEM((2, 3 * width, model), BF),
                 pltpu.SemaphoreType.DMA((2, 3)),
             ]
-            + [pltpu.VMEM((width, 2 * half), F32)] * 3,
+            + [pltpu.VMEM((width, 2 * half), F32)] * 3
+            + (beside.scratch if beside else []),
         ),
         out_shape=[jax.ShapeDtypeStruct((steps * width, half), F32)] * 3
-        + [jax.ShapeDtypeStruct((steps * width, half), BF)] * 3,
+        + [jax.ShapeDtypeStruct((groups * width, half), BF)] * 3
+        + (beside.outs if beside else []),
+        input_output_aliases={14 + i: i for i in range(n_held)},
         cost_estimate=pl.CostEstimate(
-            flops=flops, bytes_accessed=steps * (6 * width * model + 4 * chips * count * model), transcendentals=0
+            flops=flops, bytes_accessed=groups * (6 * width * model + 4 * chips * count * model), transcendentals=0
         ),
         compiler_params=pltpu.CompilerParams(
-            vmem_limit_bytes=VMEM_LIMIT, dimension_semantics=("arbitrary", "arbitrary")
-        ),
-    )(place, rows, upstream, row_cols, up_cols, gates, *kept, *weights)
-
-
-def attention_forward(place, queries, latents, latent_up, key_ids, query_ids):
+            vmem_limit_bytes=VMEM_LIMIT,
+            dimension_semantics=("arbitrary", "arbitrary"),
+            **(dict(collective_id=collective, has_side_effects=True) if beside else {}),
+        ),
+    )(
+        rows, upstream, row_cols, up_cols, gates, *kept, *weights, *held_back,
+        *(beside.ins if beside else []),
+    )
+
+
+def attention_forward(queries, latent, latent_up, key_ids, query_ids, collective):
     count = queries.shape[0]
     heads = queries.shape[1] // 256
+    chips = lax.axis_size("dpo")
     scale = (ND + RD) ** (-0.5) * LOG2E
 
-    def kernel(place_ref, q_ref, lat_ref, up_ref, kid_ref, qid_ref, att_ref, lse_ref, keys, top, low, mix):
+    def kernel(q_ref, lat_ref, up_ref, kid_ref, qid_ref, att_ref, lse_ref, all_ref, keys, top, low, mix,
+               local, send_right, take_left, send_mate, take_mate):
+        chip, core = lax.axis_index("dpo"), lax.axis_index("core")
+        place = chip * 2 + core
+        right = lax.rem(chip + 1, chips)
+        left = lax.rem(chip + chips - 1, chips)
+        barrier = pltpu.get_barrier_semaphore()
+        pl.semaphore_signal(barrier, inc=1, device_id={"core": 1 - core}, device_id_type=MESH)
+
+        @pl.when(chip > 0)
+        def _():
+            pl.semaphore_signal(barrier, inc=1, device_id={"dpo": left}, device_id_type=MESH)
+
+        pl.semaphore_wait(barrier, 1 + jnp.where(chip < chips - 1, 1, 0))
+
+        def to_right(source, i):
+            return remote(source, all_ref.at[2 * i + core], send_right.at[i], take_left.at[i], {"dpo": right})
+
+        def to_mate(source, i):
+            return remote(source, all_ref.at[2 * i + core], send_mate.at[i], take_mate.at[i], {"core": 1 - core})
+
+        @pl.when(chip < chips - 1)
+        def _():
+            to_right(lat_ref, chip).start()
+
+        to_mate(lat_ref, chip).start()
+        keep = pltpu.make_async_copy(lat_ref, all_ref.at[place], local)
+        keep.start()
         top[...] = jnp.full_like(top, -1e30)
         low[...] = jnp.zeros_like(low)
         mix[...] = jnp.zeros_like(mix)
 
-        def chunk(at, masked):
-            rows = pl.ds(pl.multiple_of(at * count, count), count)
-            lat = lat_ref[rows, :KVL]
-            rope = lat_ref[rows, KVL:]
+        def chunk(source, masked):
+            lat = source[:, :KVL]
+            rope = source[:, KVL:]
             for h in range(heads):
                 keys[h, :, ND:] = rope
                 both = nn(lat, up_ref[:, h * 256 : (h + 1) * 256]).astype(BF)
@@ -304,42 +596,78 @@
                 low[h] = low[h] * decay + jnp.sum(weights, axis=0, keepdims=True)
                 mix[h] = mix[h] * decay + nn(values, weights.astype(BF))
 
-        place_at = place_ref[0]
-        lax.fori_loop(0, place_at, lambda at, carry: (chunk(at, False), carry)[1], 0)
-        chunk(place_at, True)
+        chunk(lat_ref, True)
+        keep.wait()
+        to_mate(lat_ref, chip).wait()
+
+        @pl.when(core == 1)
+        def _():
+            chunk(all_ref.at[place - 1], False)
+
+        def earlier(i, carry):
+            at = chip - 1 - i
+            arrived = all_ref.at[2 * at + core]
+            to_right(arrived, at).wait_recv()
+
+            @pl.when(chip < chips - 1)
+            def _():
+                to_right(arrived, at).start()
+
+            to_mate(arrived, at).start()
+            chunk(arrived, False)
+            to_mate(arrived, at).wait_recv()
+            chunk(all_ref.at[2 * at + 1 - core], False)
+            return carry
+
+        lax.fori_loop(0, chip, earlier, 0)
         for h in range(heads):
             att_ref[:, h * VD : (h + 1) * VD] = (mix[h] / low[h]).T.astype(BF)
             lse_ref[h] = top[h] + jnp.log2(low[h])
 
-    def whole(shape):
-        return pl.BlockSpec(shape, lambda i, z: (0,) * len(shape), pipeline_mode=pl.Buffered(1))
-
+        def sent(i, carry):
+            to_mate(lat_ref, i).wait_send()
+            return carry
+
+        lax.fori_loop(0, chip, sent, 0)
+
+        @pl.when(chip < chips - 1)
+        def _():
+            def sent_right(i, carry):
+                to_right(lat_ref, i).wait_send()
+                return carry
+
+            lax.fori_loop(0, chip + 1, sent_right, 0)
+
+    vmem = pl.BlockSpec(memory_space=pltpu.VMEM)
+    sems = pltpu.SemaphoreType.DMA((chips,))
     return pl.pallas_call(
         kernel,
         name="attention_forward",
-        grid_spec=pltpu.PrefetchScalarGridSpec(
-            num_scalar_prefetch=1,
-            grid=(1,),
-            in_specs=[whole(a.shape) for a in (queries, latents, latent_up, key_ids, query_ids)],
-            out_specs=[whole((count, heads * VD)), whole((heads, 1, count))],
-            scratch_shapes=[
-                pltpu.VMEM((heads, count, 256), BF),
-                pltpu.VMEM((heads, 1, count), F32),
-                pltpu.VMEM((heads, 1, count), F32),
-                pltpu.VMEM((heads, VD, count), F32),
-            ],
-        ),
+        in_specs=[vmem] * 5,
+        out_specs=[vmem] * 3,
         out_shape=[
             jax.ShapeDtypeStruct((count, heads * VD), BF),
             jax.ShapeDtypeStruct((heads, 1, count), F32),
+            jax.ShapeDtypeStruct((2 * chips, count, LAT), BF),
+        ],
+        scratch_shapes=[
+            pltpu.VMEM((heads, count, 256), BF),
+            pltpu.VMEM((heads, 1, count), F32),
+            pltpu.VMEM((heads, 1, count), F32),
+            pltpu.VMEM((heads, VD, count), F32),
+            pltpu.SemaphoreType.DMA,
+            sems,
+            sems,
+            sems,
+            sems,
         ],
         cost_estimate=pl.CostEstimate(
-            flops=heads * count * latents.shape[0] * 2 * 640, bytes_accessed=12_000_000, transcendentals=0
+            flops=1000, bytes_accessed=200_000_000, transcendentals=0
         ),
         compiler_params=pltpu.CompilerParams(
-            vmem_limit_bytes=VMEM_LIMIT, dimension_semantics=("arbitrary",)
-        ),
-    )(place, queries, latents, latent_up, key_ids, query_ids)
+            vmem_limit_bytes=VMEM_LIMIT, collective_id=collective, has_side_effects=True
+        ),
+    )(queries, latent, latent_up, key_ids, query_ids)
 
 
 def attention_backward(place, queries, latents, latent_up, key_ids, query_ids, mix_grad, lse, delta):
@@ -428,14 +756,11 @@
     )(place, *ins)
 
 
-def router_of(rows, router_weight, route_rows):
+def router_of(rows, router_weight):
     logits = lax.dot_general(
         router_weight, rows, (((0,), (1,)), ((), ())), preferred_element_type=F32
     )
-    named = jnp.any(
-        route_rows.T[None, :, :] == jnp.arange(EXPERTS, dtype=jnp.int32)[:, None, None], axis=1
-    )
-    return jax.nn.softmax(logits, axis=0), named
+    return jax.nn.softmax(logits, axis=0)
 
 
 def grouped(gates, steps):
@@ -504,13 +829,18 @@
     latent = jnp.concatenate(
         [latent_float, key_rope, jnp.zeros((count, LAT - KVL - RD), F32)], axis=1
     ).astype(BF)
-    latents = lax.all_gather(mine(latent), ALL, axis=0, tiled=True)
-
+    named = jnp.any(
+        routes[:, :, None] == jnp.arange(EXPERTS, dtype=jnp.int32)[None, None, :], axis=1
+    )
     upstream_quarter = mine(cotangent)
-    after = lax.optimization_barrier((latents, upstream_quarter, mine(routes)))
-    latents = after[0]
-    all_upstream = lax.all_gather(after[1], SPREAD, axis=0, tiled=True)
-    all_routes = lax.all_gather(after[2], SPREAD, axis=0, tiled=True)
+    all_upstream = lax.all_gather(
+        jnp.concatenate(
+            [upstream_quarter, jnp.pad(mine(named).astype(BF), ((0, 0), (0, 128 - EXPERTS)))], axis=1
+        ),
+        SPREAD,
+        axis=0,
+        tiled=True,
+    ).reshape(chips, count, model + 128)
 
     query_raw = nn(attention_input, query_weight).reshape(count, heads, ND + RD)
     queries = jnp.concatenate(
@@ -521,66 +851,53 @@
         ],
         axis=-1,
     ).astype(BF).reshape(count, heads * 256)
-    place_arg = place.reshape(1).astype(jnp.int32)
     key_ids, query_ids = own_blocks[:, None], own_blocks[None, :]
-    attended, lse = attention_forward(place_arg, queries, latents, latent_up, key_ids, query_ids)
-
-    attention_part = nn(attended, output_weight).astype(BF)
-    residual = mine(tokens).astype(F32) + lax.psum_scatter(
-        attention_part, "tensor", scatter_dimension=0, tiled=True
-    ).astype(F32)
-    normed_second, second_factor = norm_rows(residual, second_gain)
-    input_quarter = normed_second.astype(BF)
-    expert_input = lax.all_gather(input_quarter, "tensor", axis=0, tiled=True)
-    after = lax.optimization_barrier((expert_input, input_quarter))
-    expert_input = after[0]
-    all_input = lax.all_gather(after[1], SPREAD, axis=0, tiled=True)
-
-    router, named = router_of(expert_input, router_weight, routes)
+    attended, lse, latents = attention_forward(
+        queries, latent, latent_up, key_ids, query_ids, 1
+    )
+    latents = latents.reshape(key_count, LAT)
+
+    def second_norm(total, gain, more):
+        residual = more[0].astype(F32) + total
+        normed, _ = norm_rows(residual, gain)
+        return residual, normed.astype(BF)
+
+    token_quarter = mine(tokens)
+    block = jax.ShapeDtypeStruct((quarter, model), F32)
+    expert_input, residual = settle(
+        nn(attended, output_weight).astype(BF),
+        [token_quarter],
+        second_gain[None],
+        second_norm,
+        [block],
+        2,
+    )
+    all_input = lax.all_gather(mine(expert_input), SPREAD, axis=0, tiled=True)
+
+    named = named.T
+    router = router_of(expert_input, router_weight)
     own_gates = grouped(jnp.where(named, router, 0.0), steps)
     expert_part, input_back, kept_h, kept_g, kept_u, dots = own_experts(
         expert_input, cotangent, own_gates, weights
     )
-    expert_total = lax.psum_scatter(
-        expert_part.astype(BF), "tensor", scatter_dimension=0, tiled=True
-    ).astype(F32)
     pair_grad = jnp.where(named, dots[: steps - 1].reshape(EXPERTS, count), 0.0)
     logit_grad = router * (pair_grad - jnp.sum(router * pair_grad, axis=0, keepdims=True))
     logit_low = logit_grad.astype(BF)
     grad_router = lax.dot_general(
         expert_input, logit_low, (((0,), (1,)), ((), ())), preferred_element_type=F32
     )
-    input_back = input_back + lax.dot_general(
-        logit_low, router_weight, (((0,), (1,)), ((), ())), preferred_element_type=F32
-    )
-    input_grad = lax.psum_scatter(
-        input_back.astype(BF), "tensor", scatter_dimension=0, tiled=True
-    ).astype(F32)
-    residual_back, grad_second_gain = norm_back(residual, second_factor, second_gain, input_grad)
-    residual_grad = residual_back + upstream_quarter.astype(F32)
-    output_grad = lax.all_gather(residual_grad.astype(BF), "tensor", axis=0, tiled=True)
-    result = lax.all_gather(
-        (residual + expert_total).astype(BF), "tensor", axis=0, tiled=True
-    )
-    early = jnp.concatenate(
-        [
-            grad_router.reshape(devices, -1),
-            jnp.repeat(grad_second_gain.reshape(2 * chips, -1), ranks, axis=0),
-        ],
-        axis=1,
-    )
-    early = lax.psum_scatter(early, ALL, scatter_dimension=0, tiled=True).reshape(-1)
-    router_size = model // devices * EXPERTS
-    grad_router = early[:router_size].reshape(-1, EXPERTS)
-    grad_second_gain = early[router_size:]
+    input_back = (
+        input_back
+        + lax.dot_general(
+            logit_low, router_weight, (((0,), (1,)), ((), ())), preferred_element_type=F32
+        )
+    ).astype(BF)
 
     all_input = all_input.reshape(chips, count, model)
-    all_upstream = all_upstream.reshape(chips, count, model)
-    all_router, all_named = router_of(
-        all_input.reshape(chips * count, model), router_weight, all_routes
-    )
+    all_named = all_upstream[:, :, model : model + EXPERTS].reshape(chips * count, EXPERTS).T
+    all_router = router_of(all_input.reshape(chips * count, model), router_weight)
     all_gates = jnp.swapaxes(
-        grouped(jnp.where(all_named, all_router, 0.0), steps).reshape(steps, -1, chips, count), 1, 2
+        grouped(all_router * all_named.astype(F32), steps).reshape(steps, -1, chips, count), 1, 2
     )
 
     def chip_columns(array):
@@ -592,30 +909,39 @@
             axis=2,
         )
 
-    grads = group_gradients(
-        chip.reshape(1).astype(jnp.int32),
-        all_input,
-        all_upstream,
-        chip_columns(all_input),
-        chip_columns(all_upstream),
-        all_gates,
-        (kept_h, kept_g, kept_u),
-        weights,
-    )
-    swap = [(0, 1), (1, 0)]
-    grads = [near + lax.ppermute(far, "core", swap).astype(F32) for near, far in zip(grads[:3], grads[3:])]
-
-    grad_output = tn(attended, output_grad)
+    input_cols, upstream_cols = chip_columns(all_input), chip_columns(all_upstream)
+    near, far = [], []
+
+    def piece(first, groups, beside, collective):
+        made = group_gradients(
+            all_input, all_upstream, input_cols, upstream_cols, all_gates,
+            (kept_h, kept_g, kept_u), weights, first, groups, near, beside, collective,
+        )
+        near[:] = made[:3]
+        far.append([lax.ppermute(f, "core", [(0, 1), (1, 0)]) for f in made[3:6]])
+        return made[6:]
+
+    def summed(rows, got):
+        return mine(rows).astype(F32) + jnp.sum(got.astype(F32), axis=0)
+
+    (got,) = piece(0, 1, Scatter(input_back), 3)
+    second_factor = lax.rsqrt(jnp.mean(residual * residual, axis=-1, keepdims=True) + EPSILON)
+    residual_back, grad_second_gain = norm_back(
+        residual, second_factor, second_gain, summed(input_back, got)
+    )
+    residual_grad = residual_back + upstream_quarter.astype(F32)
+    (output_grad,) = piece(1, 1, Gather(residual_grad.astype(BF)), 4)
+    output_grad = output_grad.reshape(count, model)
+
     attended_grad = nt(output_grad, output_weight).astype(BF)
     delta = jnp.sum(
         (attended.astype(F32) * attended_grad.astype(F32)).reshape(count, heads, VD), axis=2
     ).T[:, None, :]
+    place_arg = place.reshape(1).astype(jnp.int32)
     query_back, grad_latent_up, latent_part = attention_backward(
         place_arg, queries, latents, latent_up, key_ids, query_ids, attended_grad, lse, delta
     )
-    compressed_grad = lax.psum_scatter(
-        latent_part, DP, scatter_dimension=0, tiled=True
-    ).astype(F32)
+    (compressed_grad,) = piece(2, steps - 4, LineSum(latent_part.reshape(2 * chips, count, LAT)), 5)
     query_back = query_back.reshape(count, heads, 256)
     query_grad = jnp.concatenate(
         [
@@ -624,36 +950,53 @@
         ],
         axis=-1,
     ).astype(BF).reshape(count, heads * (ND + RD))
-    grad_query = tn(attention_input, query_grad)
     latent_grad, grad_latent_gain = norm_back(
         latent_raw, latent_factor, latent_gain, compressed_grad[:, :KVL]
     )
     down_grad = jnp.concatenate(
         [latent_grad, rotate(compressed_grad[:, KVL : KVL + RD], cosine, -sine_table)], axis=1
     ).astype(BF)
-    grad_latent_down = tn(attention_input, down_grad)
     attention_grad = nt(query_grad, query_weight) + nt(down_grad, latent_down)
     grad_first_gain = jnp.sum(attention_grad * rows_float * first_factor, axis=0)
-    attention_grad = lax.psum_scatter(
-        attention_grad.astype(BF), "tensor", scatter_dimension=0, tiled=True
+    attention_grad = attention_grad.astype(BF)
+    (got,) = piece(steps - 2, 1, Scatter(attention_grad), 6)
+    token_back, _ = norm_back(
+        token_quarter.astype(F32), mine(first_factor), first_gain, summed(attention_grad, got)
+    )
+    (token_grad,) = piece(steps - 1, 1, Gather((token_back + residual_grad).astype(BF)), 7)
+    token_grad = token_grad.reshape(count, model)
+    grads = [
+        n + jnp.concatenate([f[i] for f in far], axis=0).astype(F32) for i, n in enumerate(near)
+    ]
+
+    expert_total = lax.psum_scatter(
+        expert_part.astype(BF), "tensor", scatter_dimension=0, tiled=True
     ).astype(F32)
-    token_back, _ = norm_back(
-        mine(tokens).astype(F32), mine(first_factor), first_gain, attention_grad
-    )
-    token_grad = lax.all_gather(
-        (token_back + residual_grad).astype(BF), "tensor", axis=0, tiled=True
-    )
-    late = jnp.concatenate(
-        [
-            grad_latent_down.reshape(devices, -1),
-            jnp.repeat(grad_first_gain.reshape(2 * chips, -1), ranks, axis=0),
-            grad_latent_gain.reshape(devices, -1),
-        ],
-        axis=1,
-    ).astype(BF)
-    late = lax.psum_scatter(late, ALL, scatter_dimension=0, tiled=True).astype(F32).reshape(-1)
+    result = lax.all_gather(
+        (residual + expert_total).astype(BF), "tensor", axis=0, tiled=True
+    )
+    grad_output = tn(attended, output_grad)
+    grad_query = tn(attention_input, query_grad)
+    grad_latent_down = tn(attention_input, down_grad)
+
+    def packed(arrays, dtype):
+        rows = jnp.concatenate([a.reshape(devices, -1).astype(dtype) for a in arrays], axis=1)
+        rows = jnp.pad(rows, ((0, 0), (0, -rows.shape[1] % 2048)))
+        return lax.psum_scatter(
+            rows.reshape(-1, 128), ALL, scatter_dimension=0, tiled=True
+        ).astype(F32).reshape(-1)
+
+    def for_ranks(gain):
+        return jnp.repeat(gain.reshape(2 * chips, -1), ranks, axis=0)
+
+    gain_size = model // (2 * chips)
+    early = packed([grad_router, for_ranks(grad_second_gain)], F32)
+    router_size = model // devices * EXPERTS
+    grad_router = early[:router_size].reshape(-1, EXPERTS)
+    grad_second_gain = early[router_size : router_size + gain_size]
+    late = packed([grad_latent_down, for_ranks(grad_first_gain), grad_latent_gain], BF)
     down_size = model // devices * (KVL + RD)
-    gain_size = model // (2 * chips)
+    latent_size = KVL // devices
 
     def scattered(array, dimension):
         return lax.psum_scatter(
@@ -669,7 +1012,7 @@
         late[down_size : down_size + gain_size],
         scattered(grad_query, 0),
         late[:down_size].reshape(-1, KVL + RD),
-        late[down_size + gain_size :],
+        late[down_size + gain_size : down_size + gain_size + latent_size],
         scattered(grad_latent_up, 0),
         scattered(grad_output, 1),
         grad_second_gain,

time: 1270 us -> 891 us (0.70)
  waiting for transfers between devices: 756 us -> 249 us
  Pallas kernels: 265 us -> 407 us
  blocking collectives: 38.8 us -> 0 us
  local copies, waits for them, and re-layouts: 59 us -> 88.5 us
    reduce_scatter x4 -> x2, waiting for transfers between devices: 199 us -> 53.5 us  [packed(): lax.psum_scatter(rows.reshape(-1, 128), ALL, scatter_dimension=0, tiled=T...]
    all_gather x6 -> x2, waiting for transfers between devices: 302 us -> 158 us  [the longest x1 111 us: shards(): lax.all_gather(jnp.concatenate([upstream_quarter, jnp.pad(mine(named).ast...]
    unnamed x19 -> x9, waiting for transfers between devices: 125 us -> 0.15 us
    pallas_call x1 -> x5, Pallas kernels: 163 us -> 239 us  [group_gradients(): pl.pallas_call(kernel, name='group_gradients', grid_spec=pltpu.PrefetchSc...]
    pallas_call x1 -> x2, Pallas kernels: 7.91 us -> 74.1 us  [the longest x1 52.7 us: settle(): pl.pallas_call(kernel, name='settle', in_specs=[vmem] * (2 + n_more), out...]
    all_gather x1 -> x0, blocking collectives: 38.8 us -> none  [shards(): all_routes = lax.all_gather(after[2], SPREAD, axis=0, tiled=True)]
    reduce_scatter x1, waiting for transfers between devices: 37.8 us -> 0.03 us  [shards(): lax.psum_scatter(expert_part.astype(BF), 'tensor', scatter_dimension=0, t...]
    all_gather x1, waiting for transfers between devices: 34.8 us -> 0.01 us  [shards(): lax.all_gather((residual + expert_total).astype(BF), 'tensor', axis=0, ti...]
  transfers between devices with their start and end apart: 20 -> 24, of which waited for: 15 -> 4; matrix products, arithmetic and copies ran while one was open for 9% -> 17% of each run, Pallas kernels for 13% -> 34%
where the time goes in v2:
time: 891 us; the launch traced here: 882 us
  Pallas kernels  407 us (46%)
  waiting for transfers between devices  249 us (28%)
  local copies, waits for them, and re-layouts  88.5 us (10%)
  other arithmetic  65 us (7%)
  matrix products  50.8 us (6%)
  between operations  16.7 us (2%)
    pallas_call x5, Pallas kernels, group_gradients(): pl.pallas_call(kernel, name='group_gradients', grid_spec=pltpu.PrefetchSc...  239 us
    all_gather x1, waiting for transfers between devices, shards(): lax.all_gather(jnp.concatenate([upstream_quarter, jnp.pad(mine(named).ast...  111 us
    pallas_call x1, Pallas kernels, own_experts(): pl.pallas_call(kernel, name='own_experts', grid=(steps,), in_specs=[whole...  80.6 us
    reduce_scatter x2, waiting for transfers between devices, packed(): lax.psum_scatter(rows.reshape(-1, 128), ALL, scatter_dimension=0, tiled=T...  53.5 us
    pallas_call x1, Pallas kernels, settle(): pl.pallas_call(kernel, name='settle', in_specs=[vmem] * (2 + n_more), out...  52.7 us
    all_gather x1, waiting for transfers between devices, shards(): all_input = lax.all_gather(mine(expert_input), SPREAD, axis=0, tiled=True)  47.8 us
    reduce_scatter x3, waiting for transfers between devices, scattered(): lax.psum_scatter(array.astype(BF), DP, scatter_dimension=dimension, tiled...  37.3 us
    unnamed x112, local copies, waits for them, and re-layouts  25.3 us
  transfers between devices with their start and end apart: 24, of which 4 were waited for; matrix products, arithmetic and copies ran while one was open for 17% of the time, Pallas kernels for 34%

profile of v2, /device:TPU:0, one launch (start us, length us, event | category | flops | bytes accessed | tf_op | source)
XLA Modules:
  0.0 881.8 jit_solution(16997928078391295801)
XLA Ops:
  10.6 4.8 fusion.46
  33.3 21.5 %attention_forward.1 = (bf16[512,512]{1,0:T(8,128)(2,1)}, f32[4,1,512]{2,1,0:T(1,128)}, bf16[8,512,640]{2,1,0:T(8,128)(2,1)}) custom-call(bf16[512,1024]{1,0:T(8,128)(2,1)} %copy.145.q_ref, bf16[512,640]{1,0:T(8,128)(2,1)} %maximum_maximum_fusion.1.lat_ref, bf16[512,1024]{1,0:T(8,128)(2,1)} %up_ref.3, s32[512,1]{1,0:T(8,128)} %copy.128.kid_ref, ...), custom_call_target="tpu_custom_call" | custom-call | flops 1000 | bytes 200000000 | tf_op jit(solution)/shard_map/attention_forward/pallas_call | solution.py:643
  54.8 4.3 convolution_convert_fusion.3.refs_0_
  59.1 52.7 %settle.1 = (bf16[512,2048]{1,0:T(8,128)(2,1)}, f32[128,2048]{1,0:T(8,128)}) custom-call(bf16[512,2048]{1,0:T(8,128)(2,1)} %convolution_convert_fusion.3.refs_0_, f32[1,2048]{1,0:T(1,128)} %bitcast.151, bf16[128,2048]{1,0:T(8,128)(2,1)} %constant_dynamic-slice_fusion.7.refs_2_), custom_call_target="tpu_custom_call" | custom-call | flops 1000 | bytes 150000000 | tf_op jit(solution)/shard_map/settle/pallas_call | solution.py:390
  119.2 80.6 %own_experts.1 = (f32[512,2048]{1,0:T(8,128)}, f32[512,2048]{1,0:T(8,128)}, bf16[7,704,512]{2,1,0:T(8,128)(2,1)}, bf16[7,704,512]{2,1,0:T(8,128)(2,1)}, bf16[7,7...) custom-call(bf16[512,2048]{1,0:T(8,128)(2,1)} %get-tuple-element.67.x_ref, bf16[512,2048]{1,0:T(8,128)(2,1)} %c_ref.1, ...), custom_call_target="tpu_custom_call" | custom-call | flops 62008590336 | bytes 85721088 | tf_op jit(solution)/shard_map/own_experts/pallas_call | solution.py:167
  199.8 3.8 convert_element_type.150
  205.9 3.3 fusion.52
  209.3 4.3 add_convert_fusion
  216.4 47.8 %all-gather.6.cloned.1.call-done = bf16[2048,2048]{1,0:T(8,128)(2,1)} async-done(((bf16[128,2048]{1,0:T(8,128)(2,1)}), bf16[2048,2048]{1,0:T(8,128)(2,1)}) %all-gather.6.cloned.1.call-update) | async-done | bytes 8388624 | tf_op jit(solution)/shard_map/all_gather | solution.py:875
  264.2 5.7 fusion.49
  273.1 110.6 %all-gather.8.cloned.1.call-done = bf16[2048,2176]{1,0:T(8,128)(2,1)} async-done(((bf16[128,2176]{1,0:T(8,128)(2,1)}), bf16[2048,2176]{1,0:T(8,128)(2,1)}) %all-gather.8.cloned.1.call-update) | async-done | bytes 8912912 | tf_op jit(solution)/shard_map/all_gather | solution.py:836
  391.5 30.5 %group_gradients.5 = (f32[4928,256]{1,0:T(8,128)}, f32[4928,256]{1,0:T(8,128)}, f32[4928,256]{1,0:T(8,128)}, bf16[704,256]{1,0:T(8,128)(2,1)}, bf16[704,256]{1,0...) custom-call(bf16[4,512,2048]{2,1,0:T(8,128)(2,1)} %bitcast.105, bf16[4,512,2176]{2,1,0:T(8,128)(2,1)} %bitcast.112, ...), custom_call_target="tpu_custom_call" | custom-call | flops 17716740096 | bytes 25427968 | tf_op jit(solution)/shard_map/group_gradients/pallas_call | solution.py:504
  425.8 3.8 fusion.48
  429.6 30.7 %group_gradients.6 = (f32[4928,256]{1,0:T(8,128)}, f32[4928,256]{1,0:T(8,128)}, f32[4928,256]{1,0:T(8,128)}, bf16[704,256]{1,0:T(8,128)(2,1)}, bf16[704,256]{1,0...) custom-call(bf16[4,512,2048]{2,1,0:T(8,128)(2,1)} %bitcast.106, ...), custom_call_target="tpu_custom_call", output_to_operand_aliasing={{0}: (14, {}), {1}: (15, {}), {2}: (16, {})} | custom-call | flops 17716740096 | bytes 25427968 | tf_op jit(solution)/shard_map/group_gradients/pallas_call | solution.py:504
  460.3 4.7 convert_multiply_fusion.5
  471.0 13.0 %attention_backward.1 = (f32[512,1024]{1,0:T(8,128)}, f32[512,1024]{1,0:T(8,128)}, bf16[4096,640]{1,0:T(8,128)(2,1)}) custom-call(s32[1]{0:T(128)} %bitcast.24.place_ref, bf16[512,1024]{1,0:T(8,128)(2,1)} %copy.145.q_ref, bf16[4096,640]{1,0:T(8,128)(2,1)} %bitcast.156, bf16[512,1024]{1,0:T(8,128)(2,1)} %up_ref.3, s32[512,1]{1,0:T(8,128)} %copy.128.kid_ref, ...), custom_call_target="tpu_custom_call" | custom-call | flops 23488102400 | bytes 24000000 | tf_op jit(solution)/shard_map/attention_backward/pallas_call | solution.py:735
  486.8 2.9 copy.146
  490.0 105.9 %group_gradients.7 = (f32[4928,256]{1,0:T(8,128)}, f32[4928,256]{1,0:T(8,128)}, f32[4928,256]{1,0:T(8,128)}, bf16[2112,256]{1,0:T(8,128)(2,1)}, bf16[2112,256]{1...) custom-call(bf16[4,512,2048]{2,1,0:T(8,128)(2,1)} %bitcast.107, ...), custom_call_target="tpu_custom_call", output_to_operand_aliasing={{0}: (14, {}), {1}: (15, {}), {2}: (16, {})} | custom-call | flops 53150220288 | bytes 76283904 | tf_op jit(solution)/shard_map/group_gradients/pallas_call | solution.py:504
  595.9 3.1 fusion.29
  610.0 3.4 fusion.7
  613.4 4.7 convolution_convert_fusion.1
  618.1 4.3 copy.138
  622.4 5.6 convert_element_type.171
  628.1 4.4 convolution_convert_fusion.2
  635.3 4.4 reshape.318
  640.9 31.4 %group_gradients.8 = (f32[4928,256]{1,0:T(8,128)}, f32[4928,256]{1,0:T(8,128)}, f32[4928,256]{1,0:T(8,128)}, bf16[704,256]{1,0:T(8,128)(2,1)}, bf16[704,256]{1,0...) custom-call(bf16[4,512,2048]{2,1,0:T(8,128)(2,1)} %bitcast.108, ...), custom_call_target="tpu_custom_call", output_to_operand_aliasing={{0}: (14, {}), {1}: (15, {}), {2}: (16, {})} | custom-call | flops 17716740096 | bytes 25427968 | tf_op jit(solution)/shard_map/group_gradients/pallas_call | solution.py:504
  678.2 40.4 %group_gradients.9 = (f32[4928,256]{1,0:T(8,128)}, f32[4928,256]{1,0:T(8,128)}, f32[4928,256]{1,0:T(8,128)}, bf16[704,256]{1,0:T(8,128)(2,1)}, bf16[704,256]{1,0...) custom-call(bf16[4,512,2048]{2,1,0:T(8,128)(2,1)} %bitcast.109, ...), custom_call_target="tpu_custom_call", output_to_operand_aliasing={{0}: (14, {}), {1}: (15, {}), {2}: (16, {})} | custom-call | flops 17716740096 | bytes 25427968 | tf_op jit(solution)/shard_map/group_gradients/pallas_call | solution.py:504
  718.6 5.3 convolution_convert_fusion
  743.4 3.9 convert_add_fusion
  773.1 53.5 %reduce-scatter.9.cloned.1.call-done = bf16[304,128]{1,0:T(8,128)(2,1)} async-done(((bf16[9728,128]{1,0:T(8,128)(2,1)}), bf16[304,128]{1,0:T(8,128)(2,1)}) %reduce-scatter.9.cloned.1.call-update) | async-done | bytes 77840 | tf_op jit(solution)/shard_map/reduce_scatter | solution.py:985
  830.3 37.3 %reduce-scatter.11.cloned.1.call-done = bf16[256,768]{1,0:T(8,128)(2,1)} async-done(((bf16[2048,768]{1,0:T(8,128)(2,1)}), bf16[256,768]{1,0:T(8,128)(2,1)}) %reduce-scatter.11.cloned.1.call-update) | async-done | bytes 393232 | tf_op jit(solution)/shard_map/reduce_scatter | solution.py:1002
  869.6 3.2 copy.174
  (270 shorter events, 129.3 us)
Async XLA Ops:
  8.0 256.2 %all-gather.6.cloned.1.call-start = ((), (), s32[]{:S(2)}) async-start(), calls=%async_computation.8 | async-start | bytes 8912896 | tf_op jit(solution)/shard_map/all_gather | solution.py:875
  27.3 27.4 %copy-start.25 = (f32[512]{0:T(512)}, f32[512]{0:T(512)S(1)}, u32[]{:S(2)}) copy-start(f32[512]{0:T(512)S(1)} %add_rsqrt_fusion) | copy-start | bytes 6148
  59.1 54.7 %copy-start.33 = (s32[512,6]{0,1:T(8,128)S(1)}, s32[512,6]{0,1:T(8,128)}, u32[]{:S(2)}) copy-start(s32[512,6]{0,1:T(8,128)} %param.21) | copy-start | bytes 36868
  113.7 270.0 %all-gather.8.cloned.1.call-start = ((), (), s32[]{:S(2)}) async-start(), calls=%async_computation.9 | async-start | bytes 9469952 | tf_op jit(solution)/shard_map/all_gather | solution.py:836
  116.0 309.8 %reduce-scatter.7.cloned.1.call-start = ((), (), s32[]{:S(2)}) async-start(), calls=%async_computation.6 | async-start | bytes 2621440 | tf_op jit(solution)/shard_map/reduce_scatter | solution.py:972
  203.7 531.1 %reduce-scatter.17.cloned.1.call-start = ((), (), s32[]{:S(2)}) async-start(), calls=%async_computation.14 | async-start | bytes 270336 | tf_op jit(solution)/shard_map/reduce_scatter | solution.py:985
  429.6 30.8 %copy-start.41 = (bf16[512,512]{1,0:T(8,128)(2,1)S(1)}, bf16[512,512]{1,0:T(8,128)(2,1)}, u32[]{:S(2)}) copy-start(bf16[512,512]{1,0:T(8,128)(2,1)} %get-tuple-element.65) | copy-start | bytes 1572868
  471.0 298.8 %reduce-scatter.13.cloned.1.call-start = ((), (), s32[]{:S(2)}) async-start(), calls=%async_computation.12 | async-start | bytes 1179648 | tf_op jit(solution)/shard_map/reduce_scatter | solution.py:1002
  486.8 284.6 %all-gather.4.cloned.1.call-start = ((), (), s32[]{:S(2)}) async-start(), calls=%async_computation.7 | async-start | bytes 2621440 | tf_op jit(solution)/shard_map/all_gather | solution.py:975
  489.7 281.6 %reduce-scatter.15.cloned.1.call-start = ((), (), s32[]{:S(2)}) async-start(), calls=%async_computation.13 | async-start | bytes 2359296 | tf_op jit(solution)/shard_map/reduce_scatter | solution.py:1002
  490.0 105.9 %copy-start.29 = (f32[512]{0:T(512)S(1)}, f32[512]{0:T(512)}, u32[]{:S(2)}) copy-start(f32[512]{0:T(512)} %copy-done.28) | copy-start | bytes 6148
  490.0 105.9 %copy-start.35 = (f32[32]{0:T(128)S(1)}, f32[32]{0:T(128)}, u32[]{:S(2)}) copy-start(f32[32]{0:T(128)} %copy-done.34) | copy-start | bytes 388
  490.0 111.2 %copy-start.26 = (f32[512]{0:T(512)S(1)}, f32[512]{0:T(512)}, u32[]{:S(2)}) copy-start(f32[512]{0:T(512)} %copy-done.25) | copy-start | bytes 6148
  490.0 111.2 %copy-start.32 = (f32[512]{0:T(512)S(1)}, f32[512]{0:T(512)}, u32[]{:S(2)}) copy-start(f32[512]{0:T(512)} %param.25) | copy-start | bytes 6148
  632.4 194.2 %reduce-scatter.9.cloned.1.call-start = ((), (), s32[]{:S(2)}) async-start(), calls=%async_computation.10 | async-start | bytes 2568192 | tf_op jit(solution)/shard_map/reduce_scatter | solution.py:985
  639.8 227.8 %reduce-scatter.11.cloned.1.call-start = ((), (), s32[]{:S(2)}) async-start(), calls=%async_computation.11 | async-start | bytes 3538944 | tf_op jit(solution)/shard_map/reduce_scatter | solution.py:1002
  639.9 84.0 %collective-permute-start = (bf16[704,256]{1,0:T(8,128)(2,1)}, bf16[704,256]{1,0:T(8,128)(2,1)}, u32[]{:S(2)}, u32[]{:S(2)}) collective-permute-start(bf16[704,256]{1,0:T(8,128)(2,1)} %get-tuple-element.97), channel_id=1, source_target_pairs={{0,4},{4,0},{1,5},{5,1},{2,6},{6,2},{3,7},{7,3},{8,12},{12,8},{9,1... | collective-permute-start | bytes 1081352 | tf_op jit(solution)/shard_map/ppermute | solution.py:921
  639.9 86.3 %collective-permute-start.5 = (bf16[704,256]{1,0:T(8,128)(2,1)}, bf16[704,256]{1,0:T(8,128)(2,1)}, u32[]{:S(2)}, u32[]{:S(2)}) collective-permute-start(bf16[704,256]{1,0:T(8,128)(2,1)} %get-tuple-element.103), channel_id=1, source_target_pairs={{0,4},{4,0},{1,5},{5,1},{2,6},{6,2},{3,7},{7,3},{8,12},{12,8},{9,1... | collective-permute-start | bytes 1081352 | tf_op jit(solution)/shard_map/ppermute | solution.py:921
  640.4 87.6 %collective-permute-start.10 = (bf16[704,256]{1,0:T(8,128)(2,1)}, bf16[704,256]{1,0:T(8,128)(2,1)}, u32[]{:S(2)}, u32[]{:S(2)}) collective-permute-start(bf16[704,256]{1,0:T(8,128)(2,1)} %get-tuple-element.109), channel_id=1, source_target_pairs={{0,4},{4,0},{1,5},{5,1},{2,6},{6,2},{3,7},{7,3},{8,12},{12,8},{9,1... | collective-permute-start | bytes 1081352 | tf_op jit(solution)/shard_map/ppermute | solution.py:921
  640.5 97.1 %collective-permute-start.12 = (bf16[2112,256]{1,0:T(8,128)(2,1)}, bf16[2112,256]{1,0:T(8,128)(2,1)}, u32[]{:S(2)}, u32[]{:S(2)}) collective-permute-start(bf16[2112,256]{1,0:T(8,128)(2,1)} %get-tuple-element.111), channel_id=1, source_target_pairs={{0,4},{4,0},{1,5},{5,1},{2,6},{6,2},{3,7},{7,3},{8,12},{12,8},{9,1... | collective-permute-start | bytes 3244040 | tf_op jit(solution)/shard_map/ppermute | solution.py:921
  678.2 40.4 %copy-start.11 = (bf16[512,4,192]{0,2,1:T(8,128)(2,1)S(1)}, bf16[512,4,192]{0,2,1:T(8,128)(2,1)}, u32[]{:S(2)}) copy-start(bf16[512,4,192]{0,2,1:T(8,128)(2,1)} %copy-done.10) | copy-start | bytes 2359300
  723.9 6.4 collective-permute-start.1
  723.9 26.6 %collective-permute-start.2 = (bf16[2112,256]{1,0:T(8,128)(2,1)}, bf16[2112,256]{1,0:T(8,128)(2,1)}, u32[]{:S(2)}, u32[]{:S(2)}) collective-permute-start(bf16[2112,256]{1,0:T(8,128)(2,1)} %get-tuple-element.99), channel_id=1, source_target_pairs={{0,4},{4,0},{1,5},{5,1},{2,6},{6,2},{3,7},{7,3},{8,12},{12,8},{9,1... | collective-permute-start | bytes 3244040 | tf_op jit(solution)/shard_map/ppermute | solution.py:921
  726.3 6.5 collective-permute-start.6
  728.0 6.0 collective-permute-start.11
  731.0 21.9 %collective-permute-start.3 = (bf16[704,256]{1,0:T(8,128)(2,1)}, bf16[704,256]{1,0:T(8,128)(2,1)S(1)}, u32[]{:S(2)}, u32[]{:S(2)}) collective-permute-start(bf16[704,256]{1,0:T(8,128)(2,1)} %get-tuple-element.100), channel_id=1, source_target_pairs={{0,4},{4,0},{1,5},{5,1},{2,6},{6,2},{3,7},{7,3},{8,12},{12,8},{9,1... | collective-permute-start | bytes 1081352 | tf_op jit(solution)/shard_map/ppermute | solution.py:921
  732.8 20.9 %collective-permute-start.4 = (bf16[704,256]{1,0:T(8,128)(2,1)}, bf16[704,256]{1,0:T(8,128)(2,1)}, u32[]{:S(2)}, u32[]{:S(2)}) collective-permute-start(bf16[704,256]{1,0:T(8,128)(2,1)} %get-tuple-element.101), channel_id=1, source_target_pairs={{0,4},{4,0},{1,5},{5,1},{2,6},{6,2},{3,7},{7,3},{8,12},{12,8},{9,1... | collective-permute-start | bytes 1081352 | tf_op jit(solution)/shard_map/ppermute | solution.py:921
  734.0 6.3 collective-permute-start.13
  737.6 4.6 collective-permute-start.14
  740.4 20.1 %collective-permute-start.7 = (bf16[2112,256]{1,0:T(8,128)(2,1)}, bf16[2112,256]{1,0:T(8,128)(2,1)S(1)}, u32[]{:S(2)}, u32[]{:S(2)}) collective-permute-start(bf16[2112,256]{1,0:T(8,128)(2,1)} %get-tuple-element.105), channel_id=1, source_target_pairs={{0,4},{4,0},{1,5},{5,1},{2,6},{6,2},{3,7},{7,3},{8,12},{12,8},{9,1... | collective-permute-start | bytes 3244040 | tf_op jit(solution)/shard_map/ppermute | solution.py:921
  742.1 19.4 %collective-permute-start.8 = (bf16[704,256]{1,0:T(8,128)(2,1)S(1)}, bf16[704,256]{1,0:T(8,128)(2,1)S(1)}, u32[]{:S(2)}, u32[]{:S(2)}) collective-permute-start(bf16[704,256]{1,0:T(8,128)(2,1)S(1)} %copy-done.42), channel_id=1, source_target_pairs={{0,4},{4,0},{1,5},{5,1},{2,6},{6,2},{3,7},{7,3},{8,12},{12,8},{9,1... | collective-permute-start | bytes 1081352 | tf_op jit(solution)/shard_map/ppermute | solution.py:921
  750.6 11.7 %collective-permute-start.9 = (bf16[704,256]{1,0:T(8,128)(2,1)S(1)}, bf16[704,256]{1,0:T(8,128)(2,1)S(1)}, u32[]{:S(2)}, u32[]{:S(2)}) collective-permute-start(bf16[704,256]{1,0:T(8,128)(2,1)S(1)} %copy-done.43), channel_id=1, source_target_pairs={{0,4},{4,0},{1,5},{5,1},{2,6},{6,2},{3,7},{7,3},{8,12},{12,8},{9,1... | collective-permute-start | bytes 1081352 | tf_op jit(solution)/shard_map/ppermute | solution.py:921
  (40 other events, 178.6 us)
Sparse Core Ops, SparseCore 0:
  113.9 150.3 all-gather.5
  267.8 115.9 all-gather.7
  471.1 144.0 reduce-scatter.16
  617.3 29.1 reduce-scatter.12
  648.6 37.8 reduce-scatter.14
  688.6 137.9 reduce-scatter.8
  828.9 38.5 reduce-scatter.10
Sparse Core Ops, SparseCore 1:
  203.8 73.0 reduce-scatter.6
  489.8 67.5 all-gather.3

commit v3 on v2

--- a/solution.py
+++ b/solution.py
@@ -18,9 +18,9 @@
 F32 = jnp.float32
 VMEM_LIMIT = 60 * 1024 * 1024
 DP = ("dpo", "core")
-SPREAD = ("dpo", "tensor")
 ALL = ("dpo", "core", "tensor")
 MESH = pl.DeviceIdType.MESH
+SHORT = pl.CostEstimate(flops=1000, bytes_accessed=100_000, transcendentals=0)
 
 
 def nn(former, latter):
@@ -111,13 +111,13 @@
 
 
 def own_experts(rows, upstream, gates, weights):
-    count, model = rows.shape
+    count, model = upstream.shape
     steps, parts, _ = gates.shape
     width = weights[3].shape[0]
     unit = width // parts
     wide = 512
 
-    def kernel(x_ref, c_ref, g_ref, gw, uw, dw, sg, su, sd, out, back, kept_h, kept_g, kept_u, dots, held, sems):
+    def kernel(x_ref, c_ref, g_ref, gw, uw, dw, sg, su, sd, out_low, back, kept_h, kept_g, kept_u, dots, held, sems, out):
         step = pl.program_id(0)
         slot = lax.rem(step, 2)
         routed, shared = (gw, uw, dw), (sg, su, sd)
@@ -156,6 +156,10 @@
             out[:, columns] += nn(turned, held[slot, 2 * width :, columns])
             back[:, columns] += nn(turned_back, held[slot, : 2 * width, columns])
 
+        @pl.when(step == steps - 1)
+        def _():
+            out_low[...] = out[...].astype(BF)
+
     def whole(shape):
         return pl.BlockSpec(shape, lambda p: (0,) * len(shape), pipeline_mode=pl.Buffered(1))
 
@@ -168,19 +172,16 @@
         kernel,
         name="own_experts",
         grid=(steps,),
-        in_specs=[whole(rows.shape), whole(upstream.shape), one((parts, count))]
+        in_specs=[whole((count, model)), whole((count, model)), one((parts, count))]
         + [pl.BlockSpec(memory_space=pl.ANY)] * 6,
         out_specs=[whole((count, model))] * 2 + [one((width, count))] * 3 + [one((parts, count))],
-        out_shape=[total, total, kept, kept, kept, jax.ShapeDtypeStruct((steps, parts, count), F32)],
+        out_shape=[jax.ShapeDtypeStruct((count, model), BF), total, kept, kept, kept, jax.ShapeDtypeStruct((steps, parts, count), F32)],
         scratch_shapes=[
             pltpu.VMEM((2, 3 * width, model), BF),
             pltpu.SemaphoreType.DMA((2, 3)),
+            pltpu.VMEM((count, model), F32),
         ],
-        cost_estimate=pl.CostEstimate(
-            flops=steps * 12 * count * model * width,
-            bytes_accessed=steps * 6 * width * model + 24 * count * model,
-            transcendentals=0,
-        ),
+        cost_estimate=SHORT,
         compiler_params=pltpu.CompilerParams(
             vmem_limit_bytes=VMEM_LIMIT, dimension_semantics=("arbitrary",)
         ),
@@ -193,11 +194,38 @@
     return here, [lax.rem(here + i, size) for i in range(size)]
 
 
-def greet(devices):
+def greet(friends):
     barrier = pltpu.get_barrier_semaphore()
-    for device in devices:
-        pl.semaphore_signal(barrier, inc=1, device_id=device, device_id_type=MESH)
-    pl.semaphore_wait(barrier, len(devices))
+    total = 0
+    for device, present in friends.values():
+        if present is None:
+            pl.semaphore_signal(barrier, inc=1, device_id=device, device_id_type=MESH)
+            total = total + 1
+            continue
+
+        @pl.when(present)
+        def _():
+            pl.semaphore_signal(barrier, inc=1, device_id=device, device_id_type=MESH)
+
+        total = total + jnp.where(present, 1, 0)
+    pl.semaphore_wait(barrier, total)
+
+
+def mate_friend():
+    return {"mate": ({"core": 1 - lax.axis_index("core")}, None)}
+
+
+def rank_friends():
+    _, peers = ring_of("tensor")
+    return {f"rank{d}": ({"tensor": peer}, None) for d, peer in enumerate(peers) if d}
+
+
+def line_friends():
+    chip, chips = lax.axis_index("dpo"), lax.axis_size("dpo")
+    return {
+        "left": ({"dpo": lax.rem(chip + chips - 1, chips)}, chip > 0),
+        "right": ({"dpo": lax.rem(chip + 1, chips)}, chip < chips - 1),
+    }
 
 
 def remote(source, target, send, receive, device):
@@ -226,9 +254,10 @@
             if d
         ]
 
+    def friends(self):
+        return rank_friends()
+
     def begin(self, refs):
-        _, peers = ring_of("tensor")
-        greet([{"tensor": peer} for peer in peers[1:]])
         for copy in self.copies(refs):
             copy.start()
 
@@ -257,6 +286,24 @@
             for d, peer in enumerate(peers)
             if d
         ]
+
+
+class Many(Scatter):
+    def __init__(self, transfers):
+        self.transfers = transfers
+        self.ins = [x for t in transfers for x in t.ins]
+        self.in_specs = [x for t in transfers for x in t.in_specs]
+        self.outs = [x for t in transfers for x in t.outs]
+        self.out_specs = [x for t in transfers for x in t.out_specs]
+        self.scratch = [x for t in transfers for x in t.scratch]
+
+    def copies(self, refs):
+        n = len(self.transfers)
+        copies = []
+        for i, t in enumerate(self.transfers):
+            own = [refs[i], refs[n + i], refs[2 * n + 2 * i], refs[2 * n + 2 * i + 1]]
+            copies += t.copies(own)
+        return copies
 
 
 class LineSum:
@@ -284,17 +331,11 @@
         chip = lax.axis_index("dpo")
         return remote(mate.at[i], inbox.at[i], sends.at[i], receives.at[i], {"dpo": lax.rem(chip + self.chips - 1, self.chips)})
 
+    def friends(self):
+        return line_friends()
+
     def begin(self, refs):
-        chip, core = lax.axis_index("dpo"), lax.axis_index("core")
-        barrier = pltpu.get_barrier_semaphore()
-        pl.semaphore_signal(barrier, inc=1, device_id={"core": 1 - core}, device_id_type=MESH)
-
-        @pl.when(chip < self.chips - 1)
-        def _():
-            pl.semaphore_signal(barrier, inc=1, device_id={"dpo": chip + 1}, device_id_type=MESH)
-
-        pl.semaphore_wait(barrier, 1 + jnp.where(chip > 0, 1, 0))
-
+        chip = lax.axis_index("dpo")
         for i in range(self.chips):
             @pl.when(i <= chip)
             def _():
@@ -340,24 +381,192 @@
                 self.onward(refs, i).wait_send()
 
 
-def settle(part, more, gain, finish, extra, collective):
+class LineSpread(LineSum):
+    def __init__(self, arrays):
+        chips = lax.axis_size("dpo")
+        self.chips = chips
+        self.dimensions = [d for _, d in arrays]
+        self.shapes = [
+            tuple(n // (2 * chips) if i == d else n for i, n in enumerate(a.shape)) for a, d in arrays
+        ]
+        n = len(arrays)
+        self.ins = [a for a, _ in arrays]
+        self.in_specs = [pl.BlockSpec(memory_space=pl.ANY)] * n
+        self.outs = [jax.ShapeDtypeStruct(shape, F32) for shape in self.shapes]
+        self.out_specs = [
+            pl.BlockSpec(shape, lambda *_: (0, 0), pipeline_mode=pl.Buffered(1)) for shape in self.shapes
+        ]
+        self.scratch = []
+        for shape in self.shapes:
+            self.scratch += [
+                pltpu.VMEM((chips,) + shape, BF),
+                pltpu.VMEM((chips + 1,) + shape, BF),
+                pltpu.VMEM(shape, BF),
+            ]
+        self.scratch += [
+            pltpu.SemaphoreType.DMA((n, chips)),
+            pltpu.SemaphoreType.DMA((n, chips)),
+            pltpu.SemaphoreType.DMA((n, chips)),
+            pltpu.SemaphoreType.DMA((n, chips + 1)),
+            pltpu.SemaphoreType.DMA((n,)),
+        ]
+
+    def parts(self, refs):
+        n = len(self.shapes)
+        buffers = refs[2 * n : 5 * n]
+        return [(refs[j], refs[n + j]) + tuple(buffers[3 * j : 3 * j + 3]) for j in range(n)], refs[5 * n :]
+
+    def block(self, j, source, place):
+        size = self.shapes[j][self.dimensions[j]]
+        part = pl.ds(pl.multiple_of(place * size, size), size)
+        return source.at[part] if self.dimensions[j] == 0 else source.at[:, part]
+
+    def swaps(self, refs, i):
+        parts, sems = self.parts(refs)
+        core = lax.axis_index("core")
+        return [
+            remote(
+                self.block(j, source, 2 * i + 1 - core), mate.at[i], sems[0].at[j, i], sems[1].at[j, i],
+                {"core": 1 - core},
+            )
+            for j, (source, _, mate, _, _) in enumerate(parts)
+        ]
+
+    def onwards(self, refs, i, slot, step):
+        parts, sems = self.parts(refs)
+        chip = lax.axis_index("dpo")
+        to = lax.rem(chip + step + self.chips, self.chips)
+        return [
+            remote(mate.at[i], inbox.at[slot], sems[2].at[j, i], sems[3].at[j, slot], {"dpo": to})
+            for j, (_, _, mate, inbox, _) in enumerate(parts)
+        ]
+
+    def begin(self, refs):
+        for i in range(self.chips):
+            for copy in self.swaps(refs, i):
+                copy.start()
+
+    def middle(self, refs, step, last):
+        chip, core = lax.axis_index("dpo"), lax.axis_index("core")
+        parts, sems = self.parts(refs)
+        end = self.chips - 1
+
+        def arrive(i, slot):
+            for copy in self.onwards(refs, i, slot, 0):
+                copy.wait_recv()
+            for _, _, mate, inbox, _ in parts:
+                mate[i] = (mate[i].astype(F32) + inbox[slot].astype(F32)).astype(BF)
+
+        for i in range(self.chips):
+            due = jnp.minimum(1 + 3 * (end - jnp.abs(chip - i)), last)
+
+            @pl.when(step == due)
+            def _():
+                locals_ = [
+                    pltpu.make_async_copy(self.block(j, source, 2 * i + core), mine, sems[4].at[j])
+                    for j, (source, _, _, _, mine) in enumerate(parts)
+                ]
+                for copy in locals_:
+                    copy.start()
+                for copy in self.swaps(refs, i) + locals_:
+                    copy.wait()
+                for _, _, mate, _, mine in parts:
+                    mate[i] = (mate[i].astype(F32) + mine[...].astype(F32)).astype(BF)
+
+                @pl.when((i <= chip) & (chip < end))
+                def _():
+                    arrive(i, i)
+
+                @pl.when((i > chip) & (chip > 0))
+                def _():
+                    arrive(i, i)
+
+                @pl.when((i == chip) & (chip > 0))
+                def _():
+                    arrive(i, self.chips)
+
+                @pl.when(i < chip)
+                def _():
+                    for copy in self.onwards(refs, i, i, -1):
+                        copy.start()
+
+                @pl.when(i == chip + 1)
+                def _():
+                    for copy in self.onwards(refs, i, self.chips, 1):
+                        copy.start()
+
+                @pl.when(i > chip + 1)
+                def _():
+                    for copy in self.onwards(refs, i, i, 1):
+                        copy.start()
+
+                @pl.when(i == chip)
+                def _():
+                    for _, out, mate, _, _ in parts:
+                        out[...] = mate[i].astype(F32)
+
+    def end(self, refs):
+        chip = lax.axis_index("dpo")
+        for i in range(self.chips):
+            @pl.when(chip != i)
+            def _():
+                for copy in self.onwards(refs, i, i, 0):
+                    copy.wait_send()
+
+
+class Beside:
+    def __init__(self, former, latter):
+        self.pair = (former, latter)
+        self.ins = former.ins + latter.ins
+        self.in_specs = former.in_specs + latter.in_specs
+        self.outs = former.outs + latter.outs
+        self.out_specs = former.out_specs + latter.out_specs
+        self.scratch = former.scratch + latter.scratch
+
+    def split(self, refs):
+        refs = list(refs)
+        lists = ([], [])
+        for name in ("ins", "outs", "scratch"):
+            for t, held in zip(self.pair, lists):
+                n = len(getattr(t, name))
+                held += refs[:n]
+                del refs[:n]
+        return zip(self.pair, lists)
+
+    def friends(self):
+        return {**self.pair[0].friends(), **self.pair[1].friends()}
+
+    def begin(self, refs):
+        for t, held in self.split(refs):
+            t.begin(held)
+
+    def middle(self, refs, step, last):
+        for t, held in self.split(refs):
+            t.middle(held, step, last)
+
+    def end(self, refs):
+        for t, held in self.split(refs):
+            t.end(held)
+
+
+def settle(part, more, finish, extra, wide, collective):
     count, model = part.shape
     ranks = lax.axis_size("tensor")
     quarter = count // ranks
     n_more, n_extra = len(more), len(extra)
 
     def kernel(*refs):
-        part_ref, gain_ref = refs[:2]
-        more_refs = refs[2 : 2 + n_more]
-        out_ref = refs[2 + n_more]
-        extra_refs = refs[3 + n_more : 3 + n_more + n_extra]
-        inbox, block, gathered, send, receive, send_on, receive_on = refs[3 + n_more + n_extra :]
+        part_ref = refs[0]
+        more_refs = refs[1 : 1 + n_more]
+        out_ref = refs[1 + n_more]
+        extra_refs = refs[2 + n_more : 2 + n_more + n_extra]
+        inbox, block, gathered, send, receive, send_on, receive_on = refs[2 + n_more + n_extra :]
         rank, peers = ring_of("tensor")
 
         def rows_of(i):
             return pl.ds(pl.multiple_of(i * quarter, quarter), quarter)
 
-        greet([{"tensor": peer} for peer in peers[1:]])
+        greet(rank_friends())
         copies = [
             remote(part_ref.at[rows_of(peer)], inbox.at[d], send.at[d], receive.at[d], {"tensor": peer})
             for d, peer in enumerate(peers)
@@ -369,7 +578,7 @@
         for d, copy in enumerate(copies):
             copy.wait()
             total = total + inbox[d + 1].astype(F32)
-        results = finish(total, gain_ref[...], [r[...] for r in more_refs])
+        results = finish(total, [r[...] for r in more_refs])
         for ref, value in zip(extra_refs, results):
             ref[...] = value
         block[...] = results[-1]
@@ -390,31 +599,31 @@
     return pl.pallas_call(
         kernel,
         name="settle",
-        in_specs=[vmem] * (2 + n_more),
+        in_specs=[vmem] * (1 + n_more),
         out_specs=[vmem] * (1 + n_extra),
-        out_shape=[jax.ShapeDtypeStruct((count, model), BF)] + extra,
+        out_shape=[jax.ShapeDtypeStruct((count, wide), BF)] + extra,
         scratch_shapes=[
             pltpu.VMEM((ranks, quarter, model), BF),
-            pltpu.VMEM((quarter, model), BF),
-            pltpu.VMEM((ranks, quarter, model), BF),
+            pltpu.VMEM((quarter, wide), BF),
+            pltpu.VMEM((ranks, quarter, wide), BF),
         ]
         + sems,
-        cost_estimate=pl.CostEstimate(flops=1000, bytes_accessed=150_000_000, transcendentals=0),
+        cost_estimate=SHORT,
         compiler_params=pltpu.CompilerParams(
             vmem_limit_bytes=VMEM_LIMIT, collective_id=collective, has_side_effects=True
         ),
-    )(part, gain, *more)
+    )(part, *more)
 
 
 def group_gradients(rows, upstream, row_cols, up_cols, gates, kept, weights, first, groups, held_back, beside, collective):
-    chips, count, model = rows.shape
+    chips, count, model = upstream.shape
     steps, _, parts, _ = gates.shape
     width = weights[3].shape[0]
     half = row_cols.shape[2] // 2
-    n_ins = len(beside.ins) if beside else 0
-    n_outs = len(beside.outs) if beside else 0
-    n_held = len(held_back)
+    unit = width // 2
+    n_ins, n_outs, n_held = len(beside.ins), len(beside.outs), len(held_back)
     last = groups * chips - 1
+    ends = first + groups == steps
 
     def kernel(*refs):
         refs = list(refs)
@@ -428,20 +637,29 @@
         routed, shared = take(3), take(3)
         take(n_held)
         link_refs = take(n_ins)
-        own_g, own_u, own_d, far_g, far_u, far_d = take(6)
+        outs = take(3)
+        shared_outs = take(3) if ends else None
         link_refs += take(n_outs)
-        held, sems, sum_g, sum_u, sum_d = take(5)
+        held, sems, sum_g, sum_u, sum_d, outbox, inbox, sends, receives = take(9)
         link_refs += refs
         at_group = pl.program_id(0)
         turn = pl.program_id(1)
         step = at_group + first
         slot = lax.rem(at_group, 2)
         tick = at_group * chips + turn
-
-        if beside:
-            @pl.when(tick == 0)
-            def _():
-                beside.begin(link_refs)
+        sums = (sum_g, sum_u, sum_d)
+
+        def swap(i):
+            part = pl.ds(i * unit, unit)
+            return remote(
+                outbox.at[:, part], inbox.at[slot, :, part], sends.at[slot, i], receives.at[slot, i],
+                {"core": 1 - lax.axis_index("core")},
+            )
+
+        @pl.when(tick == 0)
+        def _():
+            greet({**mate_friend(), **beside.friends()})
+            beside.begin(link_refs)
 
         @pl.when(turn == 0)
         def _():
@@ -458,35 +676,54 @@
             def _():
                 weight_copies(routed, shared, held, sems, step + 1, 1 - slot, steps, width, True)
 
-        @pl.when(turn > 0)
-        def _():
-            unit = width // 2
+        def work(final):
             x = x_ref[0]
             c = c_ref[0]
             gate = gate_rows(g_ref[0, 0], width)
-            for at in range(0, width, unit):
+            for i in range(2):
+                at = i * unit
+                part = slice(at, at + unit)
                 gate_pre = nt(held[slot, at : at + unit], x)
                 up_pre = nt(held[slot, width + at : width + at + unit], x)
                 hidden_grad = nt(held[slot, 2 * width + at : 2 * width + at + unit], c)
-                hidden, d_gate, d_up, _ = expert_unit(
-                    gate_pre, up_pre, hidden_grad, gate[at : at + unit]
-                )
-                sum_g[at : at + unit] += nn(d_gate, xc[0])
-                sum_u[at : at + unit] += nn(d_up, xc[0])
-                sum_d[at : at + unit] += nn(hidden, cc[0])
+                hidden, d_gate, d_up, _ = expert_unit(gate_pre, up_pre, hidden_grad, gate[part])
+                sum_g[part] += nn(d_gate, xc[0])
+                sum_u[part] += nn(d_up, xc[0])
+                sum_d[part] += nn(hidden, cc[0])
+                if final:
+                    for j, total in enumerate(sums):
+                        outbox[j, part] = total[part, half:].astype(BF)
+                    swap(i).start()
+
+        @pl.when((turn > 0) & (turn < chips - 1))
+        def _():
+            work(False)
 
         @pl.when(turn == chips - 1)
         def _():
-            for total, near, far in ((sum_g, own_g, far_g), (sum_u, own_u, far_u), (sum_d, own_d, far_d)):
-                near[...] = total[:, :half]
-                far[...] = total[:, half:].astype(BF)
-
-        if beside:
-            beside.middle(link_refs, tick, last)
-
-            @pl.when(tick == last)
-            def _():
-                beside.end(link_refs)
+            work(True)
+            for i in range(2):
+                swap(i).wait()
+                part = slice(i * unit, (i + 1) * unit)
+                for j, total in enumerate(sums):
+                    value = (total[part, :half] + inbox[slot, j, part].astype(F32)).astype(BF)
+                    if not ends:
+                        outs[j][part] = value
+                        continue
+
+                    @pl.when(step < steps - 1)
+                    def _():
+                        outs[j][part] = value
+
+                    @pl.when(step == steps - 1)
+                    def _():
+                        shared_outs[j][part] = value
+
+        beside.middle(link_refs, tick, last)
+
+        @pl.when(tick == last)
+        def _():
+            beside.end(link_refs)
 
     def chip_at(turn):
         return lax.rem(lax.axis_index("dpo") + turn, chips)
@@ -498,9 +735,8 @@
         return pl.BlockSpec((1,) + shape, lambda p, k: (p + first, 0, 0))
 
     anywhere = pl.BlockSpec(memory_space=pl.ANY)
-    near_block = pl.BlockSpec((width, half), lambda p, k: (p + first, 0))
-    far_block = pl.BlockSpec((width, half), lambda p, k: (p, 0))
-    flops = groups * 2 * width * count * (3 * (chips - 1) * model + 6 * chips * half)
+    block = pl.BlockSpec((width, half), lambda p, k: (jnp.minimum(p + first, steps - 2), 0))
+    shared_block = pl.BlockSpec((width, half), lambda p, k: (0, 0))
     return pl.pallas_call(
         kernel,
         name="group_gradients",
@@ -512,30 +748,38 @@
             + [pl.BlockSpec((1, 1, parts, count), lambda p, k: (p + first, chip_at(k), 0, 0))]
             + [one((width, count))] * 3
             + [anywhere] * (6 + n_held)
-            + (beside.in_specs if beside else []),
-            out_specs=[near_block] * 3 + [far_block] * 3 + (beside.out_specs if beside else []),
+            + beside.in_specs,
+            out_specs=[block] * 3 + ([shared_block] * 3 if ends else []) + beside.out_specs,
             scratch_shapes=[
                 pltpu.VMEM((2, 3 * width, model), BF),
                 pltpu.SemaphoreType.DMA((2, 3)),
             ]
             + [pltpu.VMEM((width, 2 * half), F32)] * 3
-            + (beside.scratch if beside else []),
+            + [
+                pltpu.VMEM((3, width, half), BF),
+                pltpu.VMEM((2, 3, width, half), BF),
+                pltpu.SemaphoreType.DMA((2, 2)),
+                pltpu.SemaphoreType.DMA((2, 2)),
+            ]
+            + beside.scratch,
         ),
-        out_shape=[jax.ShapeDtypeStruct((steps * width, half), F32)] * 3
-        + [jax.ShapeDtypeStruct((groups * width, half), BF)] * 3
-        + (beside.outs if beside else []),
+        out_shape=[jax.ShapeDtypeStruct(((steps - 1) * width, half), BF)] * 3
+        + ([jax.ShapeDtypeStruct((width, half), BF)] * 3 if ends else [])
+        + beside.outs,
         input_output_aliases={14 + i: i for i in range(n_held)},
         cost_estimate=pl.CostEstimate(
-            flops=flops, bytes_accessed=groups * (6 * width * model + 4 * chips * count * model), transcendentals=0
+            flops=groups * 2 * width * count * (3 * (chips - 1) * model + 6 * chips * half),
+            bytes_accessed=groups * (6 * width * model + 4 * chips * count * model),
+            transcendentals=0,
         ),
         compiler_params=pltpu.CompilerParams(
             vmem_limit_bytes=VMEM_LIMIT,
             dimension_semantics=("arbitrary", "arbitrary"),
-            **(dict(collective_id=collective, has_side_effects=True) if beside else {}),
+            collective_id=collective,
+            has_side_effects=True,
         ),
     )(
-        rows, upstream, row_cols, up_cols, gates, *kept, *weights, *held_back,
-        *(beside.ins if beside else []),
+        rows, upstream, row_cols, up_cols, gates, *kept, *weights, *held_back, *beside.ins,
     )
 
 
@@ -550,15 +794,7 @@
         chip, core = lax.axis_index("dpo"), lax.axis_index("core")
         place = chip * 2 + core
         right = lax.rem(chip + 1, chips)
-        left = lax.rem(chip + chips - 1, chips)
-        barrier = pltpu.get_barrier_semaphore()
-        pl.semaphore_signal(barrier, inc=1, device_id={"core": 1 - core}, device_id_type=MESH)
-
-        @pl.when(chip > 0)
-        def _():
-            pl.semaphore_signal(barrier, inc=1, device_id={"dpo": left}, device_id_type=MESH)
-
-        pl.semaphore_wait(barrier, 1 + jnp.where(chip < chips - 1, 1, 0))
+        greet({**mate_friend(), **line_friends()})
 
         def to_right(source, i):
             return remote(source, all_ref.at[2 * i + core], send_right.at[i], take_left.at[i], {"dpo": right})
@@ -661,9 +897,7 @@
             sems,
             sems,
         ],
-        cost_estimate=pl.CostEstimate(
-            flops=1000, bytes_accessed=200_000_000, transcendentals=0
-        ),
+        cost_estimate=SHORT,
         compiler_params=pltpu.CompilerParams(
             vmem_limit_bytes=VMEM_LIMIT, collective_id=collective, has_side_effects=True
         ),
@@ -747,9 +981,7 @@
             ],
         ),
         out_shape=outs,
-        cost_estimate=pl.CostEstimate(
-            flops=heads * count * total * 2 * 1400, bytes_accessed=24_000_000, transcendentals=0
-        ),
+        cost_estimate=SHORT,
         compiler_params=pltpu.CompilerParams(
             vmem_limit_bytes=VMEM_LIMIT, dimension_semantics=("arbitrary",)
         ),
@@ -829,19 +1061,6 @@
     latent = jnp.concatenate(
         [latent_float, key_rope, jnp.zeros((count, LAT - KVL - RD), F32)], axis=1
     ).astype(BF)
-    named = jnp.any(
-        routes[:, :, None] == jnp.arange(EXPERTS, dtype=jnp.int32)[None, None, :], axis=1
-    )
-    upstream_quarter = mine(cotangent)
-    all_upstream = lax.all_gather(
-        jnp.concatenate(
-            [upstream_quarter, jnp.pad(mine(named).astype(BF), ((0, 0), (0, 128 - EXPERTS)))], axis=1
-        ),
-        SPREAD,
-        axis=0,
-        tiled=True,
-    ).reshape(chips, count, model + 128)
-
     query_raw = nn(attention_input, query_weight).reshape(count, heads, ND + RD)
     queries = jnp.concatenate(
         [
@@ -857,35 +1076,52 @@
     )
     latents = latents.reshape(key_count, LAT)
 
-    def second_norm(total, gain, more):
-        residual = more[0].astype(F32) + total
+    attended, upstream = lax.optimization_barrier((attended, cotangent))
+    all_upstream = lax.all_gather(upstream, "dpo", axis=0, tiled=True)
+
+    named = jnp.any(
+        routes[:, :, None] == jnp.arange(128, dtype=jnp.int32)[None, None, :], axis=1
+    ).astype(F32)
+    token_quarter = mine(tokens)
+
+    def second_norm(total, more):
+        rows, gain, router_columns, mask = more
+        residual = rows.astype(F32) + total
         normed, _ = norm_rows(residual, gain)
-        return residual, normed.astype(BF)
-
-    token_quarter = mine(tokens)
-    block = jax.ShapeDtypeStruct((quarter, model), F32)
-    expert_input, residual = settle(
+        normed = normed.astype(BF)
+        logits = nn(normed, router_columns)
+        lane = lax.broadcasted_iota(jnp.int32, logits.shape, 1)
+        logits = jnp.where(lane < EXPERTS, logits, -1e30)
+        odds = jnp.exp(logits - jnp.max(logits, axis=1, keepdims=True))
+        gates = mask * odds / jnp.sum(odds, axis=1, keepdims=True)
+        return residual, jnp.concatenate([normed, gates.astype(BF)], axis=1)
+
+    wide_input, residual = settle(
         nn(attended, output_weight).astype(BF),
-        [token_quarter],
-        second_gain[None],
+        [
+            token_quarter,
+            second_gain[None],
+            jnp.pad(router_weight, ((0, 0), (0, 128 - EXPERTS))),
+            mine(named),
+        ],
         second_norm,
-        [block],
+        [jax.ShapeDtypeStruct((quarter, model), F32)],
+        model + 128,
         2,
     )
-    all_input = lax.all_gather(mine(expert_input), SPREAD, axis=0, tiled=True)
-
-    named = named.T
+    expert_input = wide_input[:, :model]
+    all_input = lax.all_gather(wide_input, "dpo", axis=0, tiled=True)
+    all_input = all_input.reshape(chips, count, model + 128)
+
+    named = named[:, :EXPERTS].T
     router = router_of(expert_input, router_weight)
-    own_gates = grouped(jnp.where(named, router, 0.0), steps)
+    own_gates = grouped(named * router, steps)
     expert_part, input_back, kept_h, kept_g, kept_u, dots = own_experts(
-        expert_input, cotangent, own_gates, weights
-    )
-    pair_grad = jnp.where(named, dots[: steps - 1].reshape(EXPERTS, count), 0.0)
+        wide_input, cotangent, own_gates, weights
+    )
+    pair_grad = named * dots[: steps - 1].reshape(EXPERTS, count)
     logit_grad = router * (pair_grad - jnp.sum(router * pair_grad, axis=0, keepdims=True))
     logit_low = logit_grad.astype(BF)
-    grad_router = lax.dot_general(
-        expert_input, logit_low, (((0,), (1,)), ((), ())), preferred_element_type=F32
-    )
     input_back = (
         input_back
         + lax.dot_general(
@@ -893,12 +1129,31 @@
         )
     ).astype(BF)
 
-    all_input = all_input.reshape(chips, count, model)
-    all_named = all_upstream[:, :, model : model + EXPERTS].reshape(chips * count, EXPERTS).T
-    all_router = router_of(all_input.reshape(chips * count, model), router_weight)
-    all_gates = jnp.swapaxes(
-        grouped(all_router * all_named.astype(F32), steps).reshape(steps, -1, chips, count), 1, 2
-    )
+    def second_norm_back(total, more):
+        rows, gain, upstream_rows = more
+        factor = lax.rsqrt(jnp.mean(rows * rows, axis=-1, keepdims=True) + EPSILON)
+        back, gain_grad = norm_back(rows, factor, gain, total)
+        back = back + upstream_rows.astype(F32)
+        return back, gain_grad[None], back.astype(BF)
+
+    input_back, all_upstream = lax.optimization_barrier((input_back, all_upstream))
+    output_grad, residual_grad, grad_second_gain = settle(
+        input_back,
+        [residual, second_gain[None], mine(cotangent)],
+        second_norm_back,
+        [
+            jax.ShapeDtypeStruct((quarter, model), F32),
+            jax.ShapeDtypeStruct((1, model), F32),
+        ],
+        model,
+        3,
+    )
+    grad_second_gain = grad_second_gain[0]
+
+    all_gates = grouped(
+        jnp.transpose(all_input[:, :, model : model + EXPERTS].astype(F32), (2, 0, 1)), steps
+    )
+    all_gates = jnp.swapaxes(all_gates, 1, 2)
 
     def chip_columns(array):
         return jnp.concatenate(
@@ -909,31 +1164,23 @@
             axis=2,
         )
 
+    all_upstream = all_upstream.reshape(chips, count, model)
     input_cols, upstream_cols = chip_columns(all_input), chip_columns(all_upstream)
-    near, far = [], []
+    routed_grads = []
 
     def piece(first, groups, beside, collective):
         made = group_gradients(
             all_input, all_upstream, input_cols, upstream_cols, all_gates,
-            (kept_h, kept_g, kept_u), weights, first, groups, near, beside, collective,
+            (kept_h, kept_g, kept_u), weights, first, groups, routed_grads, beside, collective,
         )
-        near[:] = made[:3]
-        far.append([lax.ppermute(f, "core", [(0, 1), (1, 0)]) for f in made[3:6]])
-        return made[6:]
+        routed_grads[:] = made[:3]
+        return made[3:]
 
     def summed(rows, got):
         return mine(rows).astype(F32) + jnp.sum(got.astype(F32), axis=0)
 
-    (got,) = piece(0, 1, Scatter(input_back), 3)
-    second_factor = lax.rsqrt(jnp.mean(residual * residual, axis=-1, keepdims=True) + EPSILON)
-    residual_back, grad_second_gain = norm_back(
-        residual, second_factor, second_gain, summed(input_back, got)
-    )
-    residual_grad = residual_back + upstream_quarter.astype(F32)
-    (output_grad,) = piece(1, 1, Gather(residual_grad.astype(BF)), 4)
-    output_grad = output_grad.reshape(count, model)
-
     attended_grad = nt(output_grad, output_weight).astype(BF)
+    grad_output = tn(attended, output_grad).astype(BF)
     delta = jnp.sum(
         (attended.astype(F32) * attended_grad.astype(F32)).reshape(count, heads, VD), axis=2
     ).T[:, None, :]
@@ -941,7 +1188,6 @@
     query_back, grad_latent_up, latent_part = attention_backward(
         place_arg, queries, latents, latent_up, key_ids, query_ids, attended_grad, lse, delta
     )
-    (compressed_grad,) = piece(2, steps - 4, LineSum(latent_part.reshape(2 * chips, count, LAT)), 5)
     query_back = query_back.reshape(count, heads, 256)
     query_grad = jnp.concatenate(
         [
@@ -950,79 +1196,106 @@
         ],
         axis=-1,
     ).astype(BF).reshape(count, heads * (ND + RD))
+    grad_query = tn(attention_input, query_grad).astype(BF)
+    query_part = nt(query_grad, query_weight)
+    latent_part, grad_query, query_part = lax.optimization_barrier(
+        (latent_part, grad_query, query_part)
+    )
+    (compressed_grad,) = piece(0, 2, LineSum(latent_part.reshape(2 * chips, count, LAT)), 5)
     latent_grad, grad_latent_gain = norm_back(
         latent_raw, latent_factor, latent_gain, compressed_grad[:, :KVL]
     )
     down_grad = jnp.concatenate(
         [latent_grad, rotate(compressed_grad[:, KVL : KVL + RD], cosine, -sine_table)], axis=1
     ).astype(BF)
-    attention_grad = nt(query_grad, query_weight) + nt(down_grad, latent_down)
+    attention_grad = query_part + nt(down_grad, latent_down)
     grad_first_gain = jnp.sum(attention_grad * rows_float * first_factor, axis=0)
     attention_grad = attention_grad.astype(BF)
-    (got,) = piece(steps - 2, 1, Scatter(attention_grad), 6)
+    grad_latent_down = lax.psum_scatter(
+        tn(attention_input, down_grad).astype(BF), DP, scatter_dimension=0, tiled=True
+    )
+    grad_query, grad_latent_up, grad_output, got, got_result = piece(
+        2,
+        steps - 4,
+        Beside(
+            LineSpread([(grad_query, 0), (grad_latent_up.astype(BF), 0), (grad_output, 1)]),
+            Many([Scatter(attention_grad), Scatter(expert_part)]),
+        ),
+        6,
+    )
     token_back, _ = norm_back(
         token_quarter.astype(F32), mine(first_factor), first_gain, summed(attention_grad, got)
     )
-    (token_grad,) = piece(steps - 1, 1, Gather((token_back + residual_grad).astype(BF)), 7)
-    token_grad = token_grad.reshape(count, model)
-    grads = [
-        n + jnp.concatenate([f[i] for f in far], axis=0).astype(F32) for i, n in enumerate(near)
-    ]
-
-    expert_total = lax.psum_scatter(
-        expert_part.astype(BF), "tensor", scatter_dimension=0, tiled=True
-    ).astype(F32)
-    result = lax.all_gather(
-        (residual + expert_total).astype(BF), "tensor", axis=0, tiled=True
-    )
-    grad_output = tn(attended, output_grad)
-    grad_query = tn(attention_input, query_grad)
-    grad_latent_down = tn(attention_input, down_grad)
-
-    def packed(arrays, dtype):
-        rows = jnp.concatenate([a.reshape(devices, -1).astype(dtype) for a in arrays], axis=1)
-        rows = jnp.pad(rows, ((0, 0), (0, -rows.shape[1] % 2048)))
-        return lax.psum_scatter(
-            rows.reshape(-1, 128), ALL, scatter_dimension=0, tiled=True
-        ).astype(F32).reshape(-1)
+    *shared_grads, token_grad, result = piece(
+        steps - 2,
+        2,
+        Many(
+            [
+                Gather((token_back + residual_grad).astype(BF)),
+                Gather((residual + summed(expert_part, got_result)).astype(BF)),
+            ]
+        ),
+        7,
+    )
+    token_grad, result = token_grad.reshape(count, model), result.reshape(count, model)
+
+    grad_router = lax.dot_general(
+        expert_input, logit_low, (((0,), (1,)), ((), ())), preferred_element_type=F32
+    )
+
+    def over_ranks(array):
+        blocks = array.reshape((ranks, -1) + array.shape[1:])
+
+        def block(d):
+            return lax.dynamic_index_in_dim(blocks, lax.rem(rank + d, ranks), 0, keepdims=False)
+
+        total = block(0).astype(F32)
+        for d in range(1, ranks):
+            route = [(i, (i + d) % ranks) for i in range(ranks)]
+            total = total + lax.ppermute(block(d), "tensor", route).astype(F32)
+        return total
 
     def for_ranks(gain):
         return jnp.repeat(gain.reshape(2 * chips, -1), ranks, axis=0)
 
+    small = jnp.concatenate(
+        [
+            grad_router.reshape(devices, -1),
+            for_ranks(grad_second_gain),
+            for_ranks(grad_first_gain),
+            grad_latent_gain.reshape(devices, -1),
+        ],
+        axis=1,
+    )
+    small = jnp.pad(small, ((0, 0), (0, -small.shape[1] % 1024)))
+    small = lax.psum_scatter(small.reshape(-1, 128), DP, scatter_dimension=0, tiled=True)
+    small = over_ranks(small).reshape(-1)
+    router_size = model // devices * EXPERTS
     gain_size = model // (2 * chips)
-    early = packed([grad_router, for_ranks(grad_second_gain)], F32)
-    router_size = model // devices * EXPERTS
-    grad_router = early[:router_size].reshape(-1, EXPERTS)
-    grad_second_gain = early[router_size : router_size + gain_size]
-    late = packed([grad_latent_down, for_ranks(grad_first_gain), grad_latent_gain], BF)
-    down_size = model // devices * (KVL + RD)
     latent_size = KVL // devices
-
-    def scattered(array, dimension):
-        return lax.psum_scatter(
-            array.astype(BF), DP, scatter_dimension=dimension, tiled=True
-        ).astype(F32)
+    grad_router = small[:router_size].reshape(-1, EXPERTS)
+    small = small[router_size:]
 
     def routed_of(array):
-        return array[:routed_rows].reshape(EXPERTS, unit, half)
+        return array.reshape(EXPERTS, unit, half).astype(F32)
 
     return (
         result,
         token_grad,
-        late[down_size : down_size + gain_size],
-        scattered(grad_query, 0),
-        late[:down_size].reshape(-1, KVL + RD),
-        late[down_size + gain_size : down_size + gain_size + latent_size],
-        scattered(grad_latent_up, 0),
-        scattered(grad_output, 1),
-        grad_second_gain,
+        small[gain_size : 2 * gain_size],
+        grad_query,
+        over_ranks(grad_latent_down),
+        small[2 * gain_size : 2 * gain_size + latent_size],
+        grad_latent_up,
+        grad_output,
+        small[:gain_size],
         grad_router,
-        jnp.swapaxes(routed_of(grads[0]), 1, 2),
-        jnp.swapaxes(routed_of(grads[1]), 1, 2),
-        routed_of(grads[2]),
-        grads[0][routed_rows:].T,
-        grads[1][routed_rows:].T,
-        grads[2][routed_rows:],
+        jnp.swapaxes(routed_of(routed_grads[0]), 1, 2),
+        jnp.swapaxes(routed_of(routed_grads[1]), 1, 2),
+        routed_of(routed_grads[2]),
+        shared_grads[0].astype(F32).T,
+        shared_grads[1].astype(F32).T,
+        shared_grads[2].astype(F32),
     )
 
 

time: 891 us -> 699 us (0.78)
  waiting for transfers between devices: 249 us -> 63.6 us
  Pallas kernels: 407 us -> 450 us
  local copies, waits for them, and re-layouts: 88.5 us -> 56.8 us
  other arithmetic: 65 us -> 49.9 us
    all_gather x3 -> x2, waiting for transfers between devices: 158 us -> 62.4 us  [the longest x1 55 us: shards(): all_input = lax.all_gather(wide_input, 'dpo', axis=0, tiled=True)]
    reduce_scatter x6 -> x2, waiting for transfers between devices: 90.8 us -> 0.01 us  [the longest x1 0.01 us: shards(): lax.psum_scatter(tn(attention_input, down_grad).astype(BF), DP, scatter_d...]
    pallas_call x1 -> x2, Pallas kernels: 52.7 us -> 111 us  [settle(): pl.pallas_call(kernel, name='settle', in_specs=[vmem] * (1 + n_more), out...]
    pallas_call x5 -> x3, Pallas kernels: 239 us -> 223 us  [group_gradients(): pl.pallas_call(kernel, name='group_gradients', grid_spec=pltpu.PrefetchSc...]
    unnamed x112 -> x97, local copies, waits for them, and re-layouts: 25.3 us -> 12.5 us
    convert_element_type x6 -> x0, local copies, waits for them, and re-layouts: 11.6 us -> none  [the longest x5 10.1 us: packed(): a.reshape(devices, -1).astype(dtype)]
    slice x11 -> x5, local copies, waits for them, and re-layouts: 12.9 us -> 2.44 us  [the longest x1 1.35 us: shards(): pair_grad = named * dots[:steps - 1].reshape(EXPERTS, count)]
    transpose x0 -> x5, other arithmetic: none -> 10.2 us  [the longest x1 4.22 us: shards(): jnp.swapaxes(routed_of(routed_grads[0]), 1, 2)]
  transfers between devices with their start and end apart: 24 -> 10, of which waited for: 4 -> 3; matrix products, arithmetic and copies ran while one was open for 17% -> 15% of each run, Pallas kernels for 34% -> 51%
where the time goes in v3:
time: 699 us; the launch traced here: 691 us
  Pallas kernels  450 us (64%)
  waiting for transfers between devices  63.6 us (9%)
  local copies, waits for them, and re-layouts  56.8 us (8%)
  other arithmetic  49.9 us (7%)
  matrix products  46.7 us (7%)
  between operations  14.7 us (2%)
  starting transfers between devices  8.49 us (1%)
    pallas_call x3, Pallas kernels, group_gradients(): pl.pallas_call(kernel, name='group_gradients', grid_spec=pltpu.PrefetchSc...  223 us
    pallas_call x2, Pallas kernels, settle(): pl.pallas_call(kernel, name='settle', in_specs=[vmem] * (1 + n_more), out...  111 us
    pallas_call x1, Pallas kernels, own_experts(): pl.pallas_call(kernel, name='own_experts', grid=(steps,), in_specs=[whole...  81.6 us
    all_gather x1, waiting for transfers between devices, shards(): all_input = lax.all_gather(wide_input, 'dpo', axis=0, tiled=True)  55 us
    pallas_call x1, Pallas kernels, attention_forward(): pl.pallas_call(kernel, name='attention_forward', in_specs=[vmem] * 5, out...  21.5 us
    dot_general x3, matrix products, nt(): lax.dot_general(former, latter, (((1,), (1,)), ((), ())), preferred_eleme...  15 us
  transfers between devices with their start and end apart: 10, of which 3 were waited for; matrix products, arithmetic and copies ran while one was open for 15% of the time, Pallas kernels for 51%

profile of v3, /device:TPU:0, one launch (start us, length us, event | category | flops | bytes accessed | tf_op | source)
XLA Modules:
  0.0 690.6 jit_solution(11696434126293452490)
XLA Ops:
  11.9 4.1 fusion.47
  20.3 3.5 fusion.49
  29.9 21.5 %attention_forward.1 = (bf16[512,512]{1,0:T(8,128)(2,1)}, f32[4,1,512]{2,1,0:T(1,128)}, bf16[8,512,640]{2,1,0:T(8,128)(2,1)}) custom-call(bf16[512,1024]{1,0:T(8,128)(2,1)} %copy.156.q_ref, bf16[512,640]{1,0:T(8,128)(2,1)} %maximum_maximum_fusion.1.lat_ref, bf16[512,1024]{1,0:T(8,128)(2,1)} %up_ref.3, s32[512,1]{1,0:T(8,128)} %copy.134.kid_ref, ...), custom_call_target="tpu_custom_call" | custom-call | flops 1000 | bytes 100000 | tf_op jit(solution)/shard_map/attention_forward/pallas_call | solution.py:879
  57.6 4.3 convolution_convert_fusion.3.refs_0_
  62.0 54.7 %settle.2 = (bf16[512,2176]{1,0:T(8,128)(2,1)}, f32[128,2048]{1,0:T(8,128)}) custom-call(bf16[512,2048]{1,0:T(8,128)(2,1)} %convolution_convert_fusion.3.refs_0_, bf16[128,2048]{1,0:T(8,128)(2,1)} %constant_dynamic-slice_fusion.6.refs_1_, f32[1,2048]{1,0:T(1,128)} %bitcast.155, bf16[2048,128]{1,0:T(8,128)(2,1)} %pad.11.refs_3_, ...), custom_call_target="tpu_custom_call" | custom-call | flops 1000 | bytes 100000 | tf_op jit(solution)/shard_map/settle/pallas_call | solution.py:599
  117.1 2.9 fusion.51
  127.4 81.6 %own_experts.1 = (bf16[512,2048]{1,0:T(8,128)(2,1)}, f32[512,2048]{1,0:T(8,128)}, bf16[7,704,512]{2,1,0:T(8,128)(2,1)}, bf16[7,704,512]{2,1,0:T(8,128)(2,1)}, bf...) custom-call(bf16[512,2176]{1,0:T(8,128)(2,1)} %get-tuple-element.62.x_ref, bf16[512,2048]{1,0:T(8,128)(2,1)} %c_ref.1, ...), custom_call_target="tpu_custom_call" | custom-call | flops 1000 | bytes 100000 | tf_op jit(solution)/shard_map/own_experts/pallas_call | solution.py:171
  219.6 3.3 fusion.5
  222.9 2.5 reshape.293
  227.3 4.2 add_convert_fusion.refs_0_
  231.5 7.4 %all-gather.5.cloned.1.call-done = bf16[2048,2048]{1,0:T(8,128)(2,1)} async-done(((bf16[512,2048]{1,0:T(8,128)(2,1)}), bf16[2048,2048]{1,0:T(8,128)(2,1)}) %all-gather.5.cloned.1.call-update) | async-done | bytes 8388624 | tf_op jit(solution)/shard_map/all_gather | solution.py:1080
  239.0 56.0 %settle.3 = (bf16[512,2048]{1,0:T(8,128)(2,1)}, f32[128,2048]{1,0:T(8,128)}, f32[1,2048]{1,0:T(1,128)}) custom-call(bf16[512,2048]{1,0:T(8,128)(2,1)} %add_convert_fusion.refs_0_, f32[128,2048]{1,0:T(8,128)} %get-tuple-element.72.refs_1_, f32[1,2048]{1,0:T(1,128)} %bitcast.156, bf16[128,2048]{1,0:T(8,128)(2,1)} %constant_dynamic-slice_fusion.refs_3_), custom_call_target="tpu_custom_call" | custom-call | flops 1000 | bytes 100000 | tf_op jit(solution)/shard_map/settle/pallas_call | solution.py:599
  295.0 4.7 convert_multiply_fusion.5
  299.7 2.5 reshape.286
  304.8 13.3 %attention_backward.1 = (f32[512,1024]{1,0:T(8,128)}, f32[512,1024]{1,0:T(8,128)}, bf16[4096,640]{1,0:T(8,128)(2,1)}) custom-call(s32[1]{0:T(128)} %bitcast.21.place_ref, bf16[512,1024]{1,0:T(8,128)(2,1)} %copy.156.q_ref, bf16[4096,640]{1,0:T(8,128)(2,1)} %bitcast.120, bf16[512,1024]{1,0:T(8,128)(2,1)} %up_ref.3, s32[512,1]{1,0:T(8,128)} %copy.134.kid_ref, ...), custom_call_target="tpu_custom_call" | custom-call | flops 1000 | bytes 100000 | tf_op jit(solution)/shard_map/attention_backward/pallas_call | solution.py:969
  319.3 2.8 convert_element_type.134.refs_18_
  322.1 2.9 copy.157
  327.7 3.7 convolution_convert_fusion.refs_17_
  331.4 3.9 fusion.52
  339.4 2.7 convolution_convert_fusion.2.refs_19_
  342.0 55.0 %all-gather.3.cloned.1.call-done = bf16[2048,2176]{1,0:T(8,128)(2,1)} async-done(((bf16[512,2176]{1,0:T(8,128)(2,1)}), bf16[2048,2176]{1,0:T(8,128)(2,1)}) %all-gather.3.cloned.1.call-update) | async-done | bytes 8912912 | tf_op jit(solution)/shard_map/all_gather | solution.py:1113
  402.3 77.0 %group_gradients.3 = (bf16[4224,256]{1,0:T(8,128)(2,1)}, bf16[4224,256]{1,0:T(8,128)(2,1)}, bf16[4224,256]{1,0:T(8,128)(2,1)}, f32[512,640]{1,0:T(8,128)}) custom-call(bf16[4,512,2176]{2,1,0:T(8,128)(2,1)} %bitcast.143, bf16[4,512,2048]{2,1,0:T(8,128)(2,1)} %bitcast.149, bf16[4,512,512]{2,1,0:T(8,128)(2,1)} %pad_maximum_fusion.refs_2_, ...), custom_call_target="tpu_custom_call" | custom-call | flops 35433480192 | bytes 50855936 | tf_op jit(solution)/shard_map/group_gradients/pallas_call | solution.py:740
  483.4 3.0 convolution_convert_fusion.1
  486.4 6.5 fusion.4
  493.8 90.8 %group_gradients.4 = (bf16[4224,256]{1,0:T(8,128)(2,1)}, bf16[4224,256]{1,0:T(8,128)(2,1)}, bf16[4224,256]{1,0:T(8,128)(2,1)}, f32[256,768]{1,0:T(8,128)}, f32[6...) custom-call(bf16[4,512,2176]{2,1,0:T(8,128)(2,1)} %bitcast.144, ...), custom_call_target="tpu_custom_call", output_to_operand_aliasing={{0}: (14, {}), {1}: (15, {}), {2}: (16, {})} | custom-call | flops 53150220288 | bytes 76283904 | tf_op jit(solution)/shard_map/group_gradients/pallas_call | solution.py:740
  584.6 2.8 convert_reduce_fusion
  590.9 2.6 fusion.15.refs_17_
  593.5 55.6 %group_gradients.5 = (bf16[4224,256]{1,0:T(8,128)(2,1)}, bf16[4224,256]{1,0:T(8,128)(2,1)}, bf16[4224,256]{1,0:T(8,128)(2,1)}, bf16[704,256]{1,0:T(8,128)(2,1)},...) custom-call(bf16[4,512,2176]{2,1,0:T(8,128)(2,1)} %bitcast.145, ...), custom_call_target="tpu_custom_call", output_to_operand_aliasing={{0}: (14, {}), {1}: (15, {}), {2}: (16, {})} | custom-call | flops 35433480192 | bytes 50855936 | tf_op jit(solution)/shard_map/group_gradients/pallas_call | solution.py:740
  651.0 4.2 convert_bitcast_fusion.1
  655.3 2.5 convert_bitcast_fusion
  668.5 2.9 collective-permute-start.5
  676.5 3.3 copy.169
  (202 shorter events, 87.4 us)
Async XLA Ops:
  7.2 13.1 %copy-start = (bf16[2048,768]{1,0:T(8,128)(2,1)S(1)}, bf16[2048,768]{1,0:T(8,128)(2,1)}, u32[]{:S(2)}) copy-start(bf16[2048,768]{1,0:T(8,128)(2,1)} %param.23) | copy-start | bytes 9437188
  7.2 4.7 copy-start.26
  7.2 231.8 %all-gather.5.cloned.1.call-start = ((), (), s32[]{:S(2)}) async-start(), calls=%async_computation.3 | async-start | bytes 10485760 | tf_op jit(solution)/shard_map/all_gather | solution.py:1080
  7.3 8.9 %copy-start.38 = (f32[32]{0:T(128)}, f32[32]{0:T(128)S(1)}, u32[]{:S(2)}) copy-start(f32[32]{0:T(128)S(1)} %multiply_power_fusion) | copy-start | bytes 388
  8.0 8.2 %copy-start.30 = (f32[512]{0:T(512)}, f32[512]{0:T(512)S(1)}, u32[]{:S(2)}) copy-start(f32[512]{0:T(512)S(1)} %fusion.42) | copy-start | bytes 6148
  11.0 5.0 copy-start.27
  17.2 10.3 %copy-start.28 = (f32[512]{0:T(512)}, f32[512]{0:T(512)S(1)}, u32[]{:S(2)}) copy-start(f32[512]{0:T(512)S(1)} %add_rsqrt_fusion) | copy-start | bytes 6148
  29.9 21.6 %copy-start.34 = (s32[512,6]{0,1:T(8,128)S(1)}, s32[512,6]{0,1:T(8,128)}, u32[]{:S(2)}) copy-start(s32[512,6]{0,1:T(8,128)} %param.21) | copy-start | bytes 36868
  29.9 22.2 %copy-start.23 = (bf16[2048,12]{0,1:T(8,128)(2,1)S(1)}, bf16[2048,12]{0,1:T(8,128)(2,1)}, u32[]{:S(2)}) copy-start(bf16[2048,12]{0,1:T(8,128)(2,1)} %param.29) | copy-start | bytes 147460
  51.4 345.6 %all-gather.3.cloned.1.call-start = ((), (), s32[]{:S(2)}) async-start(), calls=%async_computation.2 | async-start | bytes 11141120 | tf_op jit(solution)/shard_map/all_gather | solution.py:1113
  52.1 9.9 %copy-start.8 = (f32[512,128]{1,0:T(8,128)}, f32[512,128]{1,0:T(8,128)S(1)}, u32[]{:S(2)}) copy-start(f32[512,128]{1,0:T(8,128)S(1)} %convert_element_type.126) | copy-start | bytes 786436
  116.7 541.1 %reduce-scatter.3.cloned.1.call-start = ((), (), s32[]{:S(2)}) async-start(), calls=%async_computation.4 | async-start | bytes 294912 | tf_op jit(solution)/shard_map/reduce_scatter | solution.py:1271
  222.9 4.4 copy-start.15
  239.0 56.0 %copy-start.43 = (bf16[512,512]{1,0:T(8,128)(2,1)S(1)}, bf16[512,512]{1,0:T(8,128)(2,1)}, u32[]{:S(2)}) copy-start(bf16[512,512]{1,0:T(8,128)(2,1)} %get-tuple-element.61) | copy-start | bytes 1572868
  304.8 13.8 %copy-start.35 = (f32[1,2048]{1,0:T(1,128)S(1)}, f32[1,2048]{1,0:T(1,128)}, u32[]{:S(2)}) copy-start(f32[1,2048]{1,0:T(1,128)} %get-tuple-element.94) | copy-start | bytes 24580
  322.1 4.4 copy-start.24
  402.2 77.1 %copy-start.3 = (f32[512,576]{1,0:T(8,128)S(1)}, f32[512,576]{1,0:T(8,128)}, u32[]{:S(2)}) copy-start(f32[512,576]{1,0:T(8,128)} %copy-done.2) | copy-start | bytes 3538948
  402.2 77.1 %copy-start.29 = (f32[512]{0:T(512)S(1)}, f32[512]{0:T(512)}, u32[]{:S(2)}) copy-start(f32[512]{0:T(512)} %copy-done.28) | copy-start | bytes 6148
  402.2 77.1 %copy-start.33 = (f32[512]{0:T(512)S(1)}, f32[512]{0:T(512)}, u32[]{:S(2)}) copy-start(f32[512]{0:T(512)} %param.25) | copy-start | bytes 6148
  486.4 6.6 copy-start.20
  493.8 173.4 %reduce-scatter.5.cloned.1.call-start = ((), (), s32[]{:S(2)}) async-start(), calls=%async_computation.5 | async-start | bytes 2654208 | tf_op jit(solution)/shard_map/reduce_scatter | solution.py:1214
  651.0 4.2 copy-start.10
  655.3 6.9 copy-start.22
  655.3 7.8 %copy-start.21 = (bf16[704,256]{1,0:T(8,128)(2,1)S(1)}, bf16[704,256]{1,0:T(8,128)(2,1)}, u32[]{:S(2)}) copy-start(bf16[704,256]{1,0:T(8,128)(2,1)} %get-tuple-element.103) | copy-start | bytes 1081348
  657.7 6.2 copy-start.11
  658.6 7.8 %collective-permute-start = (f32[16,128]{1,0:T(8,128)S(1)}, f32[16,128]{1,0:T(8,128)S(1)}, u32[]{:S(2)}, u32[]{:S(2)}) collective-permute-start(f32[16,128]{1,0:T(8,128)S(1)} %get-tuple-element.187), channel_id=1, source_target_pairs={{0,1},{1,2},{2,3},{3,0},{4,5},{5,6},{6,7},{7,4},{8,9},{9,10},{10,1... | collective-permute-start | bytes 24584 | tf_op jit(solution)/shard_map/ppermute | solution.py:1255
  659.2 7.2 %collective-permute-start.2 = (f32[16,128]{1,0:T(8,128)S(1)}, f32[16,128]{1,0:T(8,128)S(1)}, u32[]{:S(2)}, u32[]{:S(2)}) collective-permute-start(f32[16,128]{1,0:T(8,128)S(1)} %get-tuple-element.188), channel_id=1, source_target_pairs={{0,3},{1,0},{2,1},{3,2},{4,7},{5,4},{6,5},{7,6},{8,11},{9,8},{10,9... | collective-permute-start | bytes 24584 | tf_op jit(solution)/shard_map/ppermute | solution.py:1255
  661.5 4.9 collective-permute-start.1
  668.4 6.3 collective-permute-start.3
  668.5 6.3 collective-permute-start.5
  671.4 4.4 collective-permute-start.4
  679.8 4.0 copy-start.1
  (23 other events, 53.7 us)
Sparse Core Ops, SparseCore 0:
  51.5 187.3 all-gather.4
  240.5 156.4 all-gather.2
  493.9 33.1 reduce-scatter.2
  591.1 38.4 reduce-scatter.4

commit v4 on v3

--- a/solution.py
+++ b/solution.py
@@ -110,14 +110,16 @@
     )
 
 
-def own_experts(rows, upstream, gates, weights):
+def own_experts(rows, upstream, router_rows, weights):
     count, model = upstream.shape
-    steps, parts, _ = gates.shape
     width = weights[3].shape[0]
+    steps = weights[0].shape[0] // width + 1
+    parts = EXPERTS // (steps - 1)
     unit = width // parts
     wide = 512
 
-    def kernel(x_ref, c_ref, g_ref, gw, uw, dw, sg, su, sd, out_low, back, kept_h, kept_g, kept_u, dots, held, sems, out):
+    def kernel(x_ref, tail_ref, c_ref, router_ref, gw, uw, dw, sg, su, sd, out_low, back_low, kept_h, kept_g, kept_u, lg_ref,
+               held, sems, out, back, gates, router, dots):
         step = pl.program_id(0)
         slot = lax.rem(step, 2)
         routed, shared = (gw, uw, dw), (sg, su, sd)
@@ -127,6 +129,10 @@
             weight_copies(routed, shared, held, sems, step, slot, steps, width, True)
             out[...] = jnp.zeros_like(out)
             back[...] = jnp.zeros_like(back)
+            tail = tail_ref[...].astype(F32).T
+            for p in range(steps):
+                gates[p] = tail[p * parts : (p + 1) * parts]
+            router[...] = tail[16:32]
 
         weight_copies(routed, shared, held, sems, step, slot, steps, width, False)
 
@@ -137,12 +143,12 @@
         both = nt(held[slot, : 2 * width], x_ref[...])
         hidden_grad = nt(held[slot, 2 * width :], c_ref[...])
         hidden, d_gate, d_up, products = expert_unit(
-            both[:width], both[width:], hidden_grad, gate_rows(g_ref[0], width)
+            both[:width], both[width:], hidden_grad, gate_rows(gates[step], width)
         )
         kept_h[0] = hidden
         kept_g[0] = d_gate
         kept_u[0] = d_up
-        dots[0] = jnp.concatenate(
+        dots[step] = jnp.concatenate(
             [
                 jnp.sum(products[i * unit : (i + 1) * unit], axis=0, keepdims=True)
                 for i in range(parts)
@@ -159,6 +165,19 @@
         @pl.when(step == steps - 1)
         def _():
             out_low[...] = out[...].astype(BF)
+            spare = jnp.zeros((16 - EXPERTS, count), F32)
+            pair_grad = jnp.concatenate([dots[p] for p in range(steps - 1)] + [spare], axis=0)
+            named = jnp.concatenate([gates[p] for p in range(steps - 1)] + [spare], axis=0) > 0
+            pair_grad = jnp.where(named, pair_grad, 0.0)
+            odds = router[...]
+            logit_grad = odds * (pair_grad - jnp.sum(odds * pair_grad, axis=0, keepdims=True))
+            lg_ref[...] = logit_grad
+            turned_logits = logit_grad.T.astype(BF)
+            for at in range(0, model, wide):
+                columns = slice(at, at + wide)
+                back_low[:, columns] = (
+                    back[:, columns] + nn(turned_logits, router_ref[:, columns])
+                ).astype(BF)
 
     def whole(shape):
         return pl.BlockSpec(shape, lambda p: (0,) * len(shape), pipeline_mode=pl.Buffered(1))
@@ -167,25 +186,34 @@
         return pl.BlockSpec((1,) + shape, lambda p: (p, 0, 0))
 
     kept = jax.ShapeDtypeStruct((steps, width, count), BF)
-    total = jax.ShapeDtypeStruct((count, model), F32)
+    total = jax.ShapeDtypeStruct((count, model), BF)
     return pl.pallas_call(
         kernel,
         name="own_experts",
         grid=(steps,),
-        in_specs=[whole((count, model)), whole((count, model)), one((parts, count))]
+        in_specs=[
+            whole((count, model)),
+            pl.BlockSpec((count, 128), lambda p: (0, model // 128), pipeline_mode=pl.Buffered(1)),
+            whole((count, model)),
+            whole((16, model)),
+        ]
         + [pl.BlockSpec(memory_space=pl.ANY)] * 6,
-        out_specs=[whole((count, model))] * 2 + [one((width, count))] * 3 + [one((parts, count))],
-        out_shape=[jax.ShapeDtypeStruct((count, model), BF), total, kept, kept, kept, jax.ShapeDtypeStruct((steps, parts, count), F32)],
+        out_specs=[whole((count, model))] * 2 + [one((width, count))] * 3 + [whole((16, count))],
+        out_shape=[total, total, kept, kept, kept, jax.ShapeDtypeStruct((16, count), F32)],
         scratch_shapes=[
             pltpu.VMEM((2, 3 * width, model), BF),
             pltpu.SemaphoreType.DMA((2, 3)),
             pltpu.VMEM((count, model), F32),
+            pltpu.VMEM((count, model), F32),
+            pltpu.VMEM((steps, parts, count), F32),
+            pltpu.VMEM((16, count), F32),
+            pltpu.VMEM((steps, parts, count), F32),
         ],
         cost_estimate=SHORT,
         compiler_params=pltpu.CompilerParams(
             vmem_limit_bytes=VMEM_LIMIT, dimension_semantics=("arbitrary",)
         ),
-    )(rows, upstream, gates, *weights)
+    )(rows, rows, upstream, router_rows, *weights)
 
 
 def ring_of(axis):
@@ -550,30 +578,42 @@
 
 
 def settle(part, more, finish, extra, wide, collective):
-    count, model = part.shape
+    count, model = part[0].shape[0], part[-1].shape[1]
     ranks = lax.axis_size("tensor")
     quarter = count // ranks
-    n_more, n_extra = len(more), len(extra)
+    n_part, n_more, n_extra = len(part), len(more), len(extra)
 
     def kernel(*refs):
-        part_ref = refs[0]
-        more_refs = refs[1 : 1 + n_more]
-        out_ref = refs[1 + n_more]
-        extra_refs = refs[2 + n_more : 2 + n_more + n_extra]
-        inbox, block, gathered, send, receive, send_on, receive_on = refs[2 + n_more + n_extra :]
+        refs = list(refs)
+
+        def take(n):
+            taken = refs[:n]
+            del refs[:n]
+            return taken
+
+        part_refs, more_refs = take(n_part), take(n_more)
+        (out_ref,), extra_refs = take(1), take(n_extra)
+        inbox, block, gathered, send, receive, send_on, receive_on = take(7)
+        part_ref = refs[0] if refs else part_refs[0]
         rank, peers = ring_of("tensor")
 
         def rows_of(i):
             return pl.ds(pl.multiple_of(i * quarter, quarter), quarter)
 
+        def make(i):
+            if n_part == 2:
+                part_ref[rows_of(i)] = nn(part_refs[0][rows_of(i)], part_refs[1][...]).astype(BF)
+
         greet(rank_friends())
-        copies = [
-            remote(part_ref.at[rows_of(peer)], inbox.at[d], send.at[d], receive.at[d], {"tensor": peer})
-            for d, peer in enumerate(peers)
-            if d
-        ]
-        for copy in copies:
-            copy.start()
+        copies = []
+        for d, peer in enumerate(peers):
+            if d:
+                make(peer)
+                copies.append(
+                    remote(part_ref.at[rows_of(peer)], inbox.at[d], send.at[d], receive.at[d], {"tensor": peer})
+                )
+                copies[-1].start()
+        make(rank)
         total = part_ref[rows_of(rank)].astype(F32)
         for d, copy in enumerate(copies):
             copy.wait()
@@ -599,7 +639,7 @@
     return pl.pallas_call(
         kernel,
         name="settle",
-        in_specs=[vmem] * (1 + n_more),
+        in_specs=[vmem] * (n_part + n_more),
         out_specs=[vmem] * (1 + n_extra),
         out_shape=[jax.ShapeDtypeStruct((count, wide), BF)] + extra,
         scratch_shapes=[
@@ -607,12 +647,13 @@
             pltpu.VMEM((quarter, wide), BF),
             pltpu.VMEM((ranks, quarter, wide), BF),
         ]
-        + sems,
+        + sems
+        + ([pltpu.VMEM((count, model), BF)] if n_part == 2 else []),
         cost_estimate=SHORT,
         compiler_params=pltpu.CompilerParams(
             vmem_limit_bytes=VMEM_LIMIT, collective_id=collective, has_side_effects=True
         ),
-    )(part, *more)
+    )(*part, *more)
 
 
 def group_gradients(rows, upstream, row_cols, up_cols, gates, kept, weights, first, groups, held_back, beside, collective):
@@ -783,32 +824,80 @@
     )
 
 
-def attention_forward(queries, latent, latent_up, key_ids, query_ids, collective):
-    count = queries.shape[0]
-    heads = queries.shape[1] // 256
+def turn_pairs(values, even, odd):
+    lane = lax.broadcasted_iota(jnp.int32, values.shape, 1)
+    other = jnp.where(lane < RD // 2, pltpu.roll(values, 128 - RD // 2, 1), pltpu.roll(values, RD // 2, 1))
+    return values * even + other * odd
+
+
+def attention_forward(tokens, gain, query_weight, latent_rows, latent_gain, latent_up, even, odd, key_ids, query_ids, collective):
+    count, model = tokens.shape
+    heads = latent_up.shape[1] // 256
     chips = lax.axis_size("dpo")
+    ranks = lax.axis_size("tensor")
+    quarter = count // ranks
     scale = (ND + RD) ** (-0.5) * LOG2E
 
-    def kernel(q_ref, lat_ref, up_ref, kid_ref, qid_ref, att_ref, lse_ref, all_ref, keys, top, low, mix,
-               local, send_right, take_left, send_mate, take_mate):
+    def kernel(x_ref, gain_ref, qw_ref, ld_ref, lg_ref, up_ref, even_ref, odd_ref, kid_ref, qid_ref,
+               att_ref, lse_ref, all_ref, in_ref, raw_ref, q_ref, lat_ref, rope_ref, keys, top, low, mix,
+               send_right, take_left, send_mate, take_mate, send_rank, take_rank):
         chip, core = lax.axis_index("dpo"), lax.axis_index("core")
+        rank, peers = ring_of("tensor")
         place = chip * 2 + core
         right = lax.rem(chip + 1, chips)
-        greet({**mate_friend(), **line_friends()})
-
-        def to_right(source, i):
-            return remote(source, all_ref.at[2 * i + core], send_right.at[i], take_left.at[i], {"dpo": right})
-
-        def to_mate(source, i):
-            return remote(source, all_ref.at[2 * i + core], send_mate.at[i], take_mate.at[i], {"core": 1 - core})
+        own_rows = pl.ds(pl.multiple_of(rank * quarter, quarter), quarter)
+        greet({**mate_friend(), **line_friends(), **rank_friends()})
+
+        def to_right(i):
+            return remote(
+                all_ref.at[2 * i + core, own_rows], all_ref.at[2 * i + core, own_rows],
+                send_right.at[i], take_left.at[i], {"dpo": right},
+            )
+
+        def to_mate(i):
+            return remote(
+                all_ref.at[2 * i + core], all_ref.at[2 * i + core],
+                send_mate.at[i], take_mate.at[i], {"core": 1 - core},
+            )
+
+        def to_ranks(i):
+            return [
+                remote(
+                    all_ref.at[2 * i + core, own_rows], all_ref.at[2 * i + core, own_rows],
+                    send_rank.at[i, d], take_rank.at[i, d], {"tensor": peer},
+                )
+                for d, peer in enumerate(peers)
+                if d
+            ]
+
+        x = x_ref[...].astype(F32)
+        normed, _ = norm_rows(x, gain_ref[...])
+        in_ref[...] = normed.astype(BF)
+        raw = nt(in_ref[...], ld_ref[:KVL])
+        raw_ref[...] = raw
+        rope_ref[...] = jnp.zeros_like(rope_ref)
+        rope_ref[:, :RD] = nt(in_ref[...], ld_ref[KVL:])
+        latent, _ = norm_rows(raw, lg_ref[...])
+        lat_ref[:, :KVL] = latent.astype(BF)
+        lat_ref[:, KVL:] = turn_pairs(rope_ref[...], even_ref[...], odd_ref[...]).astype(BF)
+        all_ref[place] = lat_ref[...]
 
         @pl.when(chip < chips - 1)
         def _():
-            to_right(lat_ref, chip).start()
-
-        to_mate(lat_ref, chip).start()
-        keep = pltpu.make_async_copy(lat_ref, all_ref.at[place], local)
-        keep.start()
+            to_right(chip).start()
+
+        to_mate(chip).start()
+        raw_q = nn(in_ref[...], qw_ref[...])
+        lane = lax.broadcasted_iota(jnp.int32, (count, 128), 1)
+        for h in range(0, heads, 2):
+            at = h * (ND + RD)
+            former, between, latter = (raw_q[:, at + i : at + i + 128] for i in (0, 128, 256))
+            rolled = pltpu.roll(latter, 64, 1)
+            nope = jnp.where(lane < 64, pltpu.roll(between, 64, 1), rolled)
+            for i, (plain, rope) in enumerate(((former, between), (nope, rolled))):
+                to = (h + i) * 256
+                q_ref[:, to : to + ND] = plain.astype(BF)
+                q_ref[:, to + ND : to + 256] = turn_pairs(rope, even_ref[...], odd_ref[...]).astype(BF)
         top[...] = jnp.full_like(top, -1e30)
         low[...] = jnp.zeros_like(low)
         mix[...] = jnp.zeros_like(mix)
@@ -832,9 +921,23 @@
                 low[h] = low[h] * decay + jnp.sum(weights, axis=0, keepdims=True)
                 mix[h] = mix[h] * decay + nn(values, weights.astype(BF))
 
+        def intake(i):
+            to_right(i).wait_recv()
+
+            @pl.when(chip < chips - 1)
+            def _():
+                to_right(i).start()
+
+            for copy in to_ranks(i):
+                copy.start()
+
         chunk(lat_ref, True)
-        keep.wait()
-        to_mate(lat_ref, chip).wait()
+
+        @pl.when(chip > 0)
+        def _():
+            intake(chip - 1)
+
+        to_mate(chip).wait()
 
         @pl.when(core == 1)
         def _():
@@ -842,16 +945,16 @@
 
         def earlier(i, carry):
             at = chip - 1 - i
-            arrived = all_ref.at[2 * at + core]
-            to_right(arrived, at).wait_recv()
-
-            @pl.when(chip < chips - 1)
+
+            @pl.when(at > 0)
             def _():
-                to_right(arrived, at).start()
-
-            to_mate(arrived, at).start()
-            chunk(arrived, False)
-            to_mate(arrived, at).wait_recv()
+                intake(at - 1)
+
+            for copy in to_ranks(at):
+                copy.wait_recv()
+            to_mate(at).start()
+            chunk(all_ref.at[2 * at + core], False)
+            to_mate(at).wait_recv()
             chunk(all_ref.at[2 * at + 1 - core], False)
             return carry
 
@@ -861,7 +964,9 @@
             lse_ref[h] = top[h] + jnp.log2(low[h])
 
         def sent(i, carry):
-            to_mate(lat_ref, i).wait_send()
+            to_mate(i).wait_send()
+            for copy in to_ranks(i):
+                copy.wait_send()
             return carry
 
         lax.fori_loop(0, chip, sent, 0)
@@ -869,58 +974,70 @@
         @pl.when(chip < chips - 1)
         def _():
             def sent_right(i, carry):
-                to_right(lat_ref, i).wait_send()
+                to_right(i).wait_send()
                 return carry
 
             lax.fori_loop(0, chip + 1, sent_right, 0)
 
     vmem = pl.BlockSpec(memory_space=pltpu.VMEM)
     sems = pltpu.SemaphoreType.DMA((chips,))
+    rank_sems = pltpu.SemaphoreType.DMA((chips, ranks))
     return pl.pallas_call(
         kernel,
         name="attention_forward",
-        in_specs=[vmem] * 5,
-        out_specs=[vmem] * 3,
+        in_specs=[vmem] * 10,
+        out_specs=[vmem] * 6,
         out_shape=[
             jax.ShapeDtypeStruct((count, heads * VD), BF),
             jax.ShapeDtypeStruct((heads, 1, count), F32),
             jax.ShapeDtypeStruct((2 * chips, count, LAT), BF),
+            jax.ShapeDtypeStruct((count, model), BF),
+            jax.ShapeDtypeStruct((count, KVL), F32),
+            jax.ShapeDtypeStruct((count, heads * 256), BF),
         ],
         scratch_shapes=[
+            pltpu.VMEM((count, LAT), BF),
+            pltpu.VMEM((count, 128), F32),
             pltpu.VMEM((heads, count, 256), BF),
             pltpu.VMEM((heads, 1, count), F32),
             pltpu.VMEM((heads, 1, count), F32),
             pltpu.VMEM((heads, VD, count), F32),
-            pltpu.SemaphoreType.DMA,
             sems,
             sems,
             sems,
             sems,
+            rank_sems,
+            rank_sems,
         ],
         cost_estimate=SHORT,
         compiler_params=pltpu.CompilerParams(
             vmem_limit_bytes=VMEM_LIMIT, collective_id=collective, has_side_effects=True
         ),
-    )(queries, latent, latent_up, key_ids, query_ids)
-
-
-def attention_backward(place, queries, latents, latent_up, key_ids, query_ids, mix_grad, lse, delta):
+    )(tokens, gain, query_weight, latent_rows, latent_gain, latent_up, even, odd, key_ids, query_ids)
+
+
+def attention_backward(queries, latents, latent_up, key_ids, query_ids, attended, output_grad, output_weight, lse, even, odd):
     count = queries.shape[0]
     heads = queries.shape[1] // 256
-    total = latents.shape[0]
+    blocks = latents.shape[0]
     factor = (ND + RD) ** (-0.5)
     scale = factor * LOG2E
 
-    def kernel(place_ref, q_ref, lat_ref, up_ref, kid_ref, qid_ref, do_ref, lse_ref, delta_ref,
-               dq_ref, dup_ref, dlat_ref, keys, dq, dlat):
+    def kernel(q_ref, lat_ref, up_ref, kid_ref, qid_ref, att_ref, og_ref, ow_ref, lse_ref, even_ref, odd_ref,
+               dq_ref, dup_ref, dlat_ref, do_ref, delta, keys, dq, dup, dlat):
+        place = lax.axis_index("dpo") * 2 + lax.axis_index("core")
         dq[...] = jnp.zeros_like(dq)
-        dup_ref[...] = jnp.zeros_like(dup_ref)
+        dup[...] = jnp.zeros_like(dup)
+        do_ref[...] = nt(og_ref[...], ow_ref[...]).astype(BF)
+        for h in range(heads):
+            part = slice(h * VD, (h + 1) * VD)
+            products = do_ref[:, part].astype(F32) * att_ref[:, part].astype(F32)
+            delta[h] = jnp.sum(products.T, axis=0, keepdims=True)
 
         def chunk(at, masked):
-            rows = pl.ds(pl.multiple_of(at * count, count), count)
-            lat = lat_ref[rows, :KVL]
+            lat = lat_ref[at, :, :KVL]
             turned = lat.T
-            rope = lat_ref[rows, KVL:]
+            rope = lat_ref[at, :, KVL:]
             dlat[...] = jnp.zeros_like(dlat)
             for h in range(heads):
                 up = up_ref[:, h * 256 : (h + 1) * 256]
@@ -934,65 +1051,62 @@
                 if masked:
                     chances = jnp.where(kid_ref[...] <= qid_ref[...], chances, 0.0)
                 chance_grad = nt(both[:, ND:], upstream)
-                score_grad = (chances * (chance_grad - delta_ref[h])).astype(BF)
+                score_grad = (chances * (chance_grad - delta[h])).astype(BF)
                 value_grad = nn(chances.astype(BF), upstream)
                 key_grad = nn(score_grad, query) * factor
                 dq[h] += nn(keys[h].T, score_grad)
                 both_grad = jnp.concatenate([key_grad[:, :ND], value_grad], axis=1).astype(BF)
                 dlat[:, :KVL] += nt(both_grad, up)
                 dlat[:, KVL:] += key_grad[:, ND:]
-                dup_ref[:, h * 256 : (h + 1) * 256] += nn(turned, both_grad)
-            dlat_ref[rows, :] = dlat[...].astype(BF)
-
-        place_at = place_ref[0]
-        lax.fori_loop(0, place_at, lambda at, carry: (chunk(at, False), carry)[1], 0)
-        chunk(place_at, True)
+                dup[:, h * 256 : (h + 1) * 256] += nn(turned, both_grad)
+            dlat_ref[at] = dlat[...].astype(BF)
+
+        lax.fori_loop(0, place, lambda at, carry: (chunk(at, False), carry)[1], 0)
+        chunk(place, True)
 
         def clear(at, carry):
-            rows = pl.ds(pl.multiple_of(at * count, count), count)
-            dlat_ref[rows, :] = jnp.zeros((count, LAT), BF)
+            dlat_ref[at] = jnp.zeros((count, LAT), BF)
             return carry
 
-        lax.fori_loop(place_at + 1, total // count, clear, 0)
-        for h in range(heads):
-            dq_ref[:, h * 256 : (h + 1) * 256] = dq[h].T * factor
-
-    def whole(shape):
-        return pl.BlockSpec(shape, lambda i, z: (0,) * len(shape), pipeline_mode=pl.Buffered(1))
-
-    ins = (queries, latents, latent_up, key_ids, query_ids, mix_grad, lse, delta)
-    outs = [
-        jax.ShapeDtypeStruct((count, heads * 256), F32),
-        jax.ShapeDtypeStruct((KVL, heads * 256), F32),
-        jax.ShapeDtypeStruct((total, LAT), BF),
-    ]
+        lax.fori_loop(place + 1, blocks, clear, 0)
+        dup_ref[...] = dup[...].astype(BF)
+        lane = lax.broadcasted_iota(jnp.int32, (count, 128), 1)
+        for h in range(0, heads, 2):
+            plain, ropes = [], []
+            for i in range(2):
+                back = dq[h + i].T * factor
+                plain.append(back[:, :ND])
+                ropes.append(turn_pairs(back[:, ND:], even_ref[...], -odd_ref[...]))
+            moved = pltpu.roll(plain[1], 64, 1)
+            at = h * (ND + RD)
+            dq_ref[:, at : at + 128] = plain[0].astype(BF)
+            dq_ref[:, at + 128 : at + 256] = jnp.where(lane < 64, ropes[0], moved).astype(BF)
+            dq_ref[:, at + 256 : at + 384] = jnp.where(
+                lane < 64, moved, pltpu.roll(ropes[1], 64, 1)
+            ).astype(BF)
+
+    vmem = pl.BlockSpec(memory_space=pltpu.VMEM)
     return pl.pallas_call(
         kernel,
         name="attention_backward",
-        grid_spec=pltpu.PrefetchScalarGridSpec(
-            num_scalar_prefetch=1,
-            grid=(1,),
-            in_specs=[whole(a.shape) for a in ins],
-            out_specs=[whole(o.shape) for o in outs],
-            scratch_shapes=[
-                pltpu.VMEM((heads, count, 256), BF),
-                pltpu.VMEM((heads, 256, count), F32),
-                pltpu.VMEM((count, LAT), F32),
-            ],
-        ),
-        out_shape=outs,
+        in_specs=[vmem] * 11,
+        out_specs=[vmem] * 3,
+        out_shape=[
+            jax.ShapeDtypeStruct((count, heads * (ND + RD)), BF),
+            jax.ShapeDtypeStruct((KVL, heads * 256), BF),
+            jax.ShapeDtypeStruct((blocks, count, LAT), BF),
+        ],
+        scratch_shapes=[
+            pltpu.VMEM((count, heads * VD), BF),
+            pltpu.VMEM((heads, 1, count), F32),
+            pltpu.VMEM((heads, count, 256), BF),
+            pltpu.VMEM((heads, 256, count), F32),
+            pltpu.VMEM((KVL, heads * 256), F32),
+            pltpu.VMEM((count, LAT), F32),
+        ],
         cost_estimate=SHORT,
-        compiler_params=pltpu.CompilerParams(
-            vmem_limit_bytes=VMEM_LIMIT, dimension_semantics=("arbitrary",)
-        ),
-    )(place, *ins)
-
-
-def router_of(rows, router_weight):
-    logits = lax.dot_general(
-        router_weight, rows, (((0,), (1,)), ((), ())), preferred_element_type=F32
-    )
-    return jax.nn.softmax(logits, axis=0)
+        compiler_params=pltpu.CompilerParams(vmem_limit_bytes=VMEM_LIMIT),
+    )(queries, latents, latent_up, key_ids, query_ids, attended, output_grad, output_weight, lse, even, odd)
 
 
 def grouped(gates, steps):
@@ -1051,38 +1165,22 @@
     row_start = place * count
     cosine, sine_table = rotary_tables((row_start + jnp.arange(count, dtype=jnp.int32)) % key_count)
     own_blocks = lax.dynamic_slice_in_dim(block_ids, row_start, count, 0)
-    rows_float = tokens.astype(F32)
-    normed_first, first_factor = norm_rows(rows_float, first_gain)
-    attention_input = normed_first.astype(BF)
-    compressed = nn(attention_input, latent_down)
-    latent_raw = compressed[:, :KVL]
-    latent_float, latent_factor = norm_rows(latent_raw, latent_gain)
-    key_rope = rotate(compressed[:, KVL:], cosine, sine_table)
-    latent = jnp.concatenate(
-        [latent_float, key_rope, jnp.zeros((count, LAT - KVL - RD), F32)], axis=1
-    ).astype(BF)
-    query_raw = nn(attention_input, query_weight).reshape(count, heads, ND + RD)
-    queries = jnp.concatenate(
-        [
-            query_raw[..., :ND],
-            rotate(query_raw[..., ND:], cosine[:, None], sine_table[:, None]),
-            jnp.zeros((count, heads, 256 - ND - RD), F32),
-        ],
-        axis=-1,
-    ).astype(BF).reshape(count, heads * 256)
+    rest = jnp.zeros((count, 128 - RD), F32)
+    even = jnp.concatenate([cosine, cosine, rest], axis=1)
+    odd = jnp.concatenate([-sine_table, sine_table, rest], axis=1)
     key_ids, query_ids = own_blocks[:, None], own_blocks[None, :]
-    attended, lse, latents = attention_forward(
-        queries, latent, latent_up, key_ids, query_ids, 1
-    )
-    latents = latents.reshape(key_count, LAT)
-
-    attended, upstream = lax.optimization_barrier((attended, cotangent))
-    all_upstream = lax.all_gather(upstream, "dpo", axis=0, tiled=True)
+    all_upstream = lax.all_gather(cotangent, "dpo", axis=0, tiled=True)
+    attended, lse, latents, attention_input, latent_raw, queries = attention_forward(
+        tokens, first_gain[None], query_weight, latent_down.T, latent_gain[None], latent_up,
+        even, odd, key_ids, query_ids, 1,
+    )
 
     named = jnp.any(
         routes[:, :, None] == jnp.arange(128, dtype=jnp.int32)[None, None, :], axis=1
-    ).astype(F32)
+    )
+    named = (named | (jnp.arange(128) >= EXPERTS)[None, :]).astype(F32)
     token_quarter = mine(tokens)
+    parts = EXPERTS // (steps - 1)
 
     def second_norm(total, more):
         rows, gain, router_columns, mask = more
@@ -1091,17 +1189,20 @@
         normed = normed.astype(BF)
         logits = nn(normed, router_columns)
         lane = lax.broadcasted_iota(jnp.int32, logits.shape, 1)
-        logits = jnp.where(lane < EXPERTS, logits, -1e30)
+        first = lane < EXPERTS
+        logits = jnp.where(first | ((lane >= 16) & (lane < 16 + EXPERTS)), logits, -1e30)
         odds = jnp.exp(logits - jnp.max(logits, axis=1, keepdims=True))
-        gates = mask * odds / jnp.sum(odds, axis=1, keepdims=True)
+        odds = odds / jnp.sum(jnp.where(first, odds, 0.0), axis=1, keepdims=True)
+        gates = jnp.where((lane >= EXPERTS) & (lane < EXPERTS + parts), 1.0, mask * odds)
         return residual, jnp.concatenate([normed, gates.astype(BF)], axis=1)
 
+    twice = jnp.pad(router_weight, ((0, 0), (0, 16 - EXPERTS)))
     wide_input, residual = settle(
-        nn(attended, output_weight).astype(BF),
+        [attended, output_weight],
         [
             token_quarter,
             second_gain[None],
-            jnp.pad(router_weight, ((0, 0), (0, 128 - EXPERTS))),
+            jnp.pad(jnp.concatenate([twice, twice], axis=1), ((0, 0), (0, 96))),
             mine(named),
         ],
         second_norm,
@@ -1109,25 +1210,12 @@
         model + 128,
         2,
     )
-    expert_input = wide_input[:, :model]
     all_input = lax.all_gather(wide_input, "dpo", axis=0, tiled=True)
     all_input = all_input.reshape(chips, count, model + 128)
 
-    named = named[:, :EXPERTS].T
-    router = router_of(expert_input, router_weight)
-    own_gates = grouped(named * router, steps)
-    expert_part, input_back, kept_h, kept_g, kept_u, dots = own_experts(
-        wide_input, cotangent, own_gates, weights
-    )
-    pair_grad = named * dots[: steps - 1].reshape(EXPERTS, count)
-    logit_grad = router * (pair_grad - jnp.sum(router * pair_grad, axis=0, keepdims=True))
-    logit_low = logit_grad.astype(BF)
-    input_back = (
-        input_back
-        + lax.dot_general(
-            logit_low, router_weight, (((0,), (1,)), ((), ())), preferred_element_type=F32
-        )
-    ).astype(BF)
+    expert_part, input_back, kept_h, kept_g, kept_u, logit_grad = own_experts(
+        wide_input, cotangent, twice.T, weights
+    )
 
     def second_norm_back(total, more):
         rows, gain, upstream_rows = more
@@ -1138,7 +1226,7 @@
 
     input_back, all_upstream = lax.optimization_barrier((input_back, all_upstream))
     output_grad, residual_grad, grad_second_gain = settle(
-        input_back,
+        [input_back],
         [residual, second_gain[None], mine(cotangent)],
         second_norm_back,
         [
@@ -1179,29 +1267,17 @@
     def summed(rows, got):
         return mine(rows).astype(F32) + jnp.sum(got.astype(F32), axis=0)
 
-    attended_grad = nt(output_grad, output_weight).astype(BF)
+    query_grad, grad_latent_up, latent_part = attention_backward(
+        queries, latents, latent_up, key_ids, query_ids, attended, output_grad, output_weight, lse, even, odd
+    )
     grad_output = tn(attended, output_grad).astype(BF)
-    delta = jnp.sum(
-        (attended.astype(F32) * attended_grad.astype(F32)).reshape(count, heads, VD), axis=2
-    ).T[:, None, :]
-    place_arg = place.reshape(1).astype(jnp.int32)
-    query_back, grad_latent_up, latent_part = attention_backward(
-        place_arg, queries, latents, latent_up, key_ids, query_ids, attended_grad, lse, delta
-    )
-    query_back = query_back.reshape(count, heads, 256)
-    query_grad = jnp.concatenate(
-        [
-            query_back[..., :ND],
-            rotate(query_back[..., ND : ND + RD], cosine[:, None], -sine_table[:, None]),
-        ],
-        axis=-1,
-    ).astype(BF).reshape(count, heads * (ND + RD))
     grad_query = tn(attention_input, query_grad).astype(BF)
     query_part = nt(query_grad, query_weight)
     latent_part, grad_query, query_part = lax.optimization_barrier(
         (latent_part, grad_query, query_part)
     )
-    (compressed_grad,) = piece(0, 2, LineSum(latent_part.reshape(2 * chips, count, LAT)), 5)
+    (compressed_grad,) = piece(0, 2, LineSum(latent_part), 5)
+    _, latent_factor = norm_rows(latent_raw, latent_gain)
     latent_grad, grad_latent_gain = norm_back(
         latent_raw, latent_factor, latent_gain, compressed_grad[:, :KVL]
     )
@@ -1209,6 +1285,8 @@
         [latent_grad, rotate(compressed_grad[:, KVL : KVL + RD], cosine, -sine_table)], axis=1
     ).astype(BF)
     attention_grad = query_part + nt(down_grad, latent_down)
+    rows_float = tokens.astype(F32)
+    _, first_factor = norm_rows(rows_float, first_gain)
     grad_first_gain = jnp.sum(attention_grad * rows_float * first_factor, axis=0)
     attention_grad = attention_grad.astype(BF)
     grad_latent_down = lax.psum_scatter(
@@ -1218,7 +1296,7 @@
         2,
         steps - 4,
         Beside(
-            LineSpread([(grad_query, 0), (grad_latent_up.astype(BF), 0), (grad_output, 1)]),
+            LineSpread([(grad_query, 0), (grad_latent_up, 0), (grad_output, 1)]),
             Many([Scatter(attention_grad), Scatter(expert_part)]),
         ),
         6,
@@ -1240,7 +1318,8 @@
     token_grad, result = token_grad.reshape(count, model), result.reshape(count, model)
 
     grad_router = lax.dot_general(
-        expert_input, logit_low, (((0,), (1,)), ((), ())), preferred_element_type=F32
+        wide_input[:, :model], logit_grad[:EXPERTS].astype(BF), (((0,), (1,)), ((), ())),
+        preferred_element_type=F32,
     )
 
     def over_ranks(array):

time: 699 us -> 651 us (0.931)
  local copies, waits for them, and re-layouts: 56.8 us -> 29 us
  Pallas kernels: 450 us -> 476 us
  matrix products: 46.7 us -> 23 us
  other arithmetic: 49.9 us -> 37.2 us
  waiting for transfers between devices: 63.6 us -> 53.2 us
    dot_general x6 -> x1, matrix products: 22.4 us -> 1.72 us  [shards(): lax.dot_general(wide_input[:, :model], logit_grad[:EXPERTS].astype(BF), (...]
    pallas_call x3, Pallas kernels: 223 us -> 242 us  [group_gradients(): pl.pallas_call(kernel, name='group_gradients', grid_spec=pltpu.PrefetchSc...]
    reshape x4 -> x0, local copies, waits for them, and re-layouts: 8.41 us -> none  [the longest x2 2.97 us: shards(): pair_grad = named * dots[:steps - 1].reshape(EXPERTS, count)]
    all_gather x1, waiting for transfers between devices: 7.44 us -> 0.01 us  [shards(): all_upstream = lax.all_gather(cotangent, 'dpo', axis=0, tiled=True)]
    pallas_call x4, Pallas kernels: 145 us -> 153 us  [the longest x2 113 us: settle(): pl.pallas_call(kernel, name='settle', in_specs=[vmem] * (n_part + n_more)...]
    dot_general x3 -> x2, matrix products: 15 us -> 10.3 us  [nt(): lax.dot_general(former, latter, (((1,), (1,)), ((), ())), preferred_eleme...]
  transfers between devices with their start and end apart: 10 -> 10, of which waited for: 3 -> 3; matrix products, arithmetic and copies ran while one was open for 15% -> 10% of each run, Pallas kernels for 51% -> 59%
where the time goes in v4:
time: 651 us; the launch traced here: 642 us
  Pallas kernels  476 us (73%)
  waiting for transfers between devices  53.2 us (8%)
  other arithmetic  37.2 us (6%)
  local copies, waits for them, and re-layouts  29 us (4%)
  matrix products  23 us (4%)
  between operations  14.5 us (2%)
  starting transfers between devices  8.48 us (1%)
    pallas_call x3, Pallas kernels, group_gradients(): pl.pallas_call(kernel, name='group_gradients', grid_spec=pltpu.PrefetchSc...  242 us
    pallas_call x2, Pallas kernels, settle(): pl.pallas_call(kernel, name='settle', in_specs=[vmem] * (n_part + n_more)...  113 us
    pallas_call x1, Pallas kernels, own_experts(): pl.pallas_call(kernel, name='own_experts', grid=(steps,), in_specs=[whole...  81.7 us
    all_gather x1, waiting for transfers between devices, shards(): all_input = lax.all_gather(wide_input, 'dpo', axis=0, tiled=True)  51.3 us
    pallas_call x1, Pallas kernels, attention_forward(): pl.pallas_call(kernel, name='attention_forward', in_specs=[vmem] * 10, ou...  22.2 us
    pallas_call x1, Pallas kernels, attention_backward(): pl.pallas_call(kernel, name='attention_backward', in_specs=[vmem] * 11, o...  17.1 us
  transfers between devices with their start and end apart: 10, of which 3 were waited for; matrix products, arithmetic and copies ran while one was open for 10% of the time, Pallas kernels for 59%

profile of v4, /device:TPU:0, one launch (start us, length us, event | category | flops | bytes accessed | tf_op | source)
XLA Modules:
  0.0 641.7 jit_solution(13932824890818157794)
XLA Ops:
  11.7 22.2 %attention_forward.1 = (bf16[512,512]{1,0:T(8,128)(2,1)}, f32[4,1,512]{2,1,0:T(1,128)}, bf16[8,512,640]{2,1,0:T(8,128)(2,1)}, bf16[512,2048]{1,0:T(8,128)(2,1)},...) custom-call(bf16[512,2048]{1,0:T(8,128)(2,1)} %x_ref.1, f32[1,2048]{1,0:T(1,128)} %bitcast.119, bf16[2048,768]{1,0:T(8,128)(2,1)} %qw_ref.1, ...), custom_call_target="tpu_custom_call" | custom-call | flops 1000 | bytes 100000 | tf_op jit(solution)/shard_map/attention_forward/pallas_call | solution.py:985
  37.1 1.9 constant_dynamic-slice_fusion.5.refs_2_
  39.0 56.8 %settle.2 = (bf16[512,2176]{1,0:T(8,128)(2,1)}, f32[128,2048]{1,0:T(8,128)}) custom-call(bf16[512,512]{1,0:T(8,128)(2,1)} %get-tuple-element.61.refs_0_.att_ref, bf16[512,2048]{1,0:T(8,128)(2,1)} %ow_ref.1, bf16[128,2048]{1,0:T(8,128)(2,1)} %constant_dynamic-slice_fusion.5.refs_2_, f32[1,2048]{1,0:T(1,128)} %bitcast.120, ...), custom_call_target="tpu_custom_call" | custom-call | flops 1000 | bytes 100000 | tf_op jit(solution)/shard_map/settle/pallas_call | solution.py:639
  96.2 81.7 %own_experts.1 = (bf16[512,2048]{1,0:T(8,128)(2,1)}, bf16[512,2048]{1,0:T(8,128)(2,1)}, bf16[7,704,512]{2,1,0:T(8,128)(2,1)}, bf16[7,704,512]{2,1,0:T(8,128)(2,1...) custom-call(bf16[512,2176]{1,0:T(8,128)(2,1)} %get-tuple-element.62.x_ref.tail_ref, ...), custom_call_target="tpu_custom_call" | custom-call | flops 1000 | bytes 100000 | tf_op jit(solution)/shard_map/own_experts/pallas_call | solution.py:190
  178.0 2.4 fusion
  181.0 1.7 fusion.3
  182.7 2.0 reshape.185
  184.9 1.9 constant_dynamic-slice_fusion.refs_3_
  186.7 56.4 %settle.3 = (bf16[512,2048]{1,0:T(8,128)(2,1)}, f32[128,2048]{1,0:T(8,128)}, f32[1,2048]{1,0:T(1,128)}) custom-call(bf16[512,2048]{1,0:T(8,128)(2,1)} %get-tuple-element.70.refs_0_, f32[128,2048]{1,0:T(8,128)} %get-tuple-element.71.refs_1_, f32[1,2048]{1,0:T(1,128)} %bitcast.121, bf16[128,2048]{1,0:T(8,128)(2,1)} %constant_dynamic-slice_fusion.refs_3_), custom_call_target="tpu_custom_call" | custom-call | flops 1000 | bytes 100000 | tf_op jit(solution)/shard_map/settle/pallas_call | solution.py:639
  243.2 17.1 %attention_backward.1 = (bf16[512,768]{1,0:T(8,128)(2,1)}, bf16[512,1024]{1,0:T(8,128)(2,1)}, bf16[8,512,640]{2,1,0:T(8,128)(2,1)}) custom-call(bf16[512,1024]{1,0:T(8,128)(2,1)} %get-tuple-element.68.q_ref, bf16[8,512,640]{2,1,0:T(8,128)(2,1)} %get-tuple-element.69.lat_ref, bf16[512,1024]{1,0:T(8,128)(2,1)} %up_ref.3, s32[512,1]{1,0:T(8,128)} %copy.64.kid_ref, ...), custom_call_target="tpu_custom_call" | custom-call | flops 1000 | bytes 100000 | tf_op jit(solution)/shard_map/attention_backward/pallas_call | solution.py:1089
  261.5 5.4 convolution_convert_fusion.refs_17_
  267.0 3.8 fusion.23
  270.8 1.7 constant_dynamic-slice_fusion.2
  275.1 2.6 convolution_convert_fusion.2.refs_19_
  277.7 51.3 %all-gather.3.cloned.1.call-done = bf16[2048,2176]{1,0:T(8,128)(2,1)} async-done(((bf16[512,2176]{1,0:T(8,128)(2,1)}), bf16[2048,2176]{1,0:T(8,128)(2,1)}) %all-gather.3.cloned.1.call-update) | async-done | bytes 8912912 | tf_op jit(solution)/shard_map/all_gather | solution.py:1213
  331.1 1.7 constant_dynamic-slice_fusion.4
  334.3 95.4 %group_gradients.3 = (bf16[4224,256]{1,0:T(8,128)(2,1)}, bf16[4224,256]{1,0:T(8,128)(2,1)}, bf16[4224,256]{1,0:T(8,128)(2,1)}, f32[512,640]{1,0:T(8,128)}) custom-call(bf16[4,512,2176]{2,1,0:T(8,128)(2,1)} %bitcast.109, bf16[4,512,2048]{2,1,0:T(8,128)(2,1)} %bitcast.113, bf16[4,512,512]{2,1,0:T(8,128)(2,1)} %pad_maximum_fusion.refs_2_, ...), custom_call_target="tpu_custom_call" | custom-call | flops 35433480192 | bytes 50855936 | tf_op jit(solution)/shard_map/group_gradients/pallas_call | solution.py:781
  429.7 2.3 subtract_convert_fusion.1
  432.0 1.7 multiply_reduce_fusion
  434.1 6.5 %fusion.2 = (f32[2048]{0:T(1024)S(1)}, bf16[512,2048]{1,0:T(8,128)(2,1)}) fusion(bf16[512,2048]{1,0:T(8,128)(2,1)S(1)} %copy-done.1, f32[512]{0:T(512)S(1)} %add_rsqrt_fusion, f32[512,2048]{1,0:T(8,128)} %fusion.23, bf16[2048,576]{0,1:T(8,128)(2,1)} %param.24, bf16[512,32]{1,0:T(8,128)(2,1)S(1)} %get-tuple-element.163, ...), kind=kOutput, calls=%fused_computation.6 | convolution fusion | flops 1216018432 | bytes 11347968 | tf_op jit(solution)/shard_map/dot_general | solution.py:31
  441.5 90.8 %group_gradients.4 = (bf16[4224,256]{1,0:T(8,128)(2,1)}, bf16[4224,256]{1,0:T(8,128)(2,1)}, bf16[4224,256]{1,0:T(8,128)(2,1)}, f32[256,768]{1,0:T(8,128)}, f32[6...) custom-call(bf16[4,512,2176]{2,1,0:T(8,128)(2,1)} %bitcast.110, ...), custom_call_target="tpu_custom_call", output_to_operand_aliasing={{0}: (14, {}), {1}: (15, {}), {2}: (16, {})} | custom-call | flops 53150220288 | bytes 76283904 | tf_op jit(solution)/shard_map/group_gradients/pallas_call | solution.py:781
  532.3 1.9 convert_reduce_fusion.1
  537.0 2.9 convolution_convert_fusion.1
  540.5 3.8 fusion.11
  544.3 56.0 %group_gradients.5 = (bf16[4224,256]{1,0:T(8,128)(2,1)}, bf16[4224,256]{1,0:T(8,128)(2,1)}, bf16[4224,256]{1,0:T(8,128)(2,1)}, bf16[704,256]{1,0:T(8,128)(2,1)},...) custom-call(bf16[4,512,2176]{2,1,0:T(8,128)(2,1)} %bitcast.111, ...), custom_call_target="tpu_custom_call", output_to_operand_aliasing={{0}: (14, {}), {1}: (15, {}), {2}: (16, {})} | custom-call | flops 35433480192 | bytes 50855936 | tf_op jit(solution)/shard_map/group_gradients/pallas_call | solution.py:781
  600.3 1.9 convert_bitcast_fusion.3
  602.2 4.2 convert_bitcast_fusion.1
  606.4 2.5 convert_bitcast_fusion
  610.3 2.4 collective-permute-start.2
  615.1 2.5 convert.32
  619.6 2.9 collective-permute-start.5
  627.6 3.3 copy.85
  (135 shorter events, 35.8 us)
Async XLA Ops:
  7.2 179.6 %all-gather.5.cloned.1.call-start = ((), (), s32[]{:S(2)}) async-start(), calls=%async_computation.3 | async-start | bytes 10485760 | tf_op jit(solution)/shard_map/all_gather | solution.py:1172
  7.9 321.1 %all-gather.3.cloned.1.call-start = ((), (), s32[]{:S(2)}) async-start(), calls=%async_computation.2 | async-start | bytes 11141120 | tf_op jit(solution)/shard_map/all_gather | solution.py:1213
  8.7 3.0 copy-start.20
  11.7 22.3 %copy-start.19 = (bf16[2048,12]{0,1:T(8,128)(2,1)S(1)}, bf16[2048,12]{0,1:T(8,128)(2,1)}, u32[]{:S(2)}) copy-start(bf16[2048,12]{0,1:T(8,128)(2,1)} %param.29) | copy-start | bytes 147460
  11.7 24.1 %copy-start.22 = (s32[512,6]{0,1:T(8,128)S(1)}, s32[512,6]{0,1:T(8,128)}, u32[]{:S(2)}) copy-start(s32[512,6]{0,1:T(8,128)} %param.21) | copy-start | bytes 36868
  95.8 513.1 %reduce-scatter.3.cloned.1.call-start = ((), (), s32[]{:S(2)}) async-start(), calls=%async_computation.4 | async-start | bytes 294912 | tf_op jit(solution)/shard_map/reduce_scatter | solution.py:1350
  96.2 84.7 %copy-start = (bf16[512,2176]{1,0:T(8,128)(2,1)S(1)}, bf16[512,2176]{1,0:T(8,128)(2,1)}, u32[]{:S(2)}) copy-start(bf16[512,2176]{1,0:T(8,128)(2,1)} %get-tuple-element.62.x_ref.tail_ref) | copy-start | bytes 6684676
  177.9 3.0 copy-start.27
  181.0 3.7 copy-start.2
  243.2 17.6 %copy-start.23 = (f32[1,2048]{1,0:T(1,128)S(1)}, f32[1,2048]{1,0:T(1,128)}, u32[]{:S(2)}) copy-start(f32[1,2048]{1,0:T(1,128)} %get-tuple-element.96) | copy-start | bytes 24580
  261.5 5.5 copy-start.4
  261.5 5.5 copy-start.26
  334.3 97.7 %copy-start.21 = (f32[512]{0:T(512)S(1)}, f32[512]{0:T(512)}, u32[]{:S(2)}) copy-start(f32[512]{0:T(512)} %param.25) | copy-start | bytes 6148
  429.7 4.1 copy-start.3
  434.1 6.5 %copy-start.13 = (bf16[512,512]{1,0:T(8,128)(2,1)}, bf16[512,512]{1,0:T(8,128)(2,1)S(1)}, u32[]{:S(2)}) copy-start(bf16[512,512]{1,0:T(8,128)(2,1)S(1)} %subtract_convert_fusion) | copy-start | bytes 1572868
  441.5 176.8 %reduce-scatter.5.cloned.1.call-start = ((), (), s32[]{:S(2)}) async-start(), calls=%async_computation.5 | async-start | bytes 2654208 | tf_op jit(solution)/shard_map/reduce_scatter | solution.py:1292
  532.3 3.4 copy-start.10
  534.2 2.8 copy-start.14
  534.2 2.8 copy-start.25
  602.2 4.2 copy-start.5
  606.4 6.8 %copy-start.16 = (bf16[704,256]{1,0:T(8,128)(2,1)S(1)}, bf16[704,256]{1,0:T(8,128)(2,1)}, u32[]{:S(2)}) copy-start(bf16[704,256]{1,0:T(8,128)(2,1)} %get-tuple-element.104) | copy-start | bytes 1081348
  606.4 7.8 %copy-start.15 = (bf16[704,256]{1,0:T(8,128)(2,1)S(1)}, bf16[704,256]{1,0:T(8,128)(2,1)}, u32[]{:S(2)}) copy-start(bf16[704,256]{1,0:T(8,128)(2,1)} %get-tuple-element.105) | copy-start | bytes 1081348
  608.9 6.2 copy-start.6
  609.8 7.8 %collective-permute-start = (f32[16,128]{1,0:T(8,128)S(1)}, f32[16,128]{1,0:T(8,128)S(1)}, u32[]{:S(2)}, u32[]{:S(2)}) collective-permute-start(f32[16,128]{1,0:T(8,128)S(1)} %get-tuple-element.169), channel_id=1, source_target_pairs={{0,1},{1,2},{2,3},{3,0},{4,5},{5,6},{6,7},{7,4},{8,9},{9,10},{10,1... | collective-permute-start | bytes 24584 | tf_op jit(solution)/shard_map/ppermute | solution.py:1334
  610.3 7.2 %collective-permute-start.2 = (f32[16,128]{1,0:T(8,128)S(1)}, f32[16,128]{1,0:T(8,128)S(1)}, u32[]{:S(2)}, u32[]{:S(2)}) collective-permute-start(f32[16,128]{1,0:T(8,128)S(1)} %get-tuple-element.170), channel_id=1, source_target_pairs={{0,3},{1,0},{2,1},{3,2},{4,7},{5,4},{6,5},{7,6},{8,11},{9,8},{10,9... | collective-permute-start | bytes 24584 | tf_op jit(solution)/shard_map/ppermute | solution.py:1334
  612.7 4.9 collective-permute-start.1
  619.5 6.3 collective-permute-start.3
  619.6 6.3 collective-permute-start.5
  622.5 4.4 collective-permute-start.4
  627.6 3.3 copy-start.8
  631.0 2.5 copy-start.17
  631.0 3.2 copy-start.12
  (6 other events, 10.4 us)
Sparse Core Ops, SparseCore 0:
  9.6 152.3 all-gather.4
  163.6 165.4 all-gather.2
  441.6 33.5 reduce-scatter.2
  540.0 38.4 reduce-scatter.4

commit v5 on v4

--- a/solution.py
+++ b/solution.py
@@ -110,15 +110,14 @@
     )
 
 
-def own_experts(rows, upstream, router_rows, weights):
-    count, model = upstream.shape
-    width = weights[3].shape[0]
-    steps = weights[0].shape[0] // width + 1
+def own_experts(rows, products_back, router_rows, weights):
+    steps, _, width, count = products_back.shape
+    model = rows.shape[1] - 128
     parts = EXPERTS // (steps - 1)
     unit = width // parts
     wide = 512
 
-    def kernel(x_ref, tail_ref, c_ref, router_ref, gw, uw, dw, sg, su, sd, out_low, back_low, kept_h, kept_g, kept_u, lg_ref,
+    def kernel(x_ref, tail_ref, b_ref, router_ref, gw, uw, dw, sg, su, sd, out_low, back_low, kept_h, kept_g, kept_u, lg_ref,
                held, sems, out, back, gates, router, dots):
         step = pl.program_id(0)
         slot = lax.rem(step, 2)
@@ -141,9 +140,8 @@
             weight_copies(routed, shared, held, sems, step + 1, 1 - slot, steps, width, True)
 
         both = nt(held[slot, : 2 * width], x_ref[...])
-        hidden_grad = nt(held[slot, 2 * width :], c_ref[...])
         hidden, d_gate, d_up, products = expert_unit(
-            both[:width], both[width:], hidden_grad, gate_rows(gates[step], width)
+            both[:width], both[width:], b_ref[0, 0].astype(F32), gate_rows(gates[step], width)
         )
         kept_h[0] = hidden
         kept_g[0] = d_gate
@@ -194,7 +192,7 @@
         in_specs=[
             whole((count, model)),
             pl.BlockSpec((count, 128), lambda p: (0, model // 128), pipeline_mode=pl.Buffered(1)),
-            whole((count, model)),
+            pl.BlockSpec((1, 1, width, count), lambda p: (p, 0, 0, 0)),
             whole((16, model)),
         ]
         + [pl.BlockSpec(memory_space=pl.ANY)] * 6,
@@ -213,7 +211,7 @@
         compiler_params=pltpu.CompilerParams(
             vmem_limit_bytes=VMEM_LIMIT, dimension_semantics=("arbitrary",)
         ),
-    )(rows, rows, upstream, router_rows, *weights)
+    )(rows, rows, products_back, router_rows, *weights)
 
 
 def ring_of(axis):
@@ -339,6 +337,7 @@
         chips = lax.axis_size("dpo")
         self.chips = chips
         shape = blocks.shape[1:]
+        self.rows = shape[0] // 2
         self.ins = [blocks]
         self.in_specs = [pl.BlockSpec(memory_space=pl.ANY)]
         self.outs = [jax.ShapeDtypeStruct(shape, F32)]
@@ -347,72 +346,96 @@
             pltpu.VMEM((chips,) + shape, blocks.dtype),
             pltpu.VMEM((chips,) + shape, blocks.dtype),
             pltpu.VMEM(shape, blocks.dtype),
-        ] + [pltpu.SemaphoreType.DMA((chips,))] * 4 + [pltpu.SemaphoreType.DMA]
-
-    def swap(self, refs, i):
+        ] + [pltpu.SemaphoreType.DMA((chips, 2))] * 4 + [pltpu.SemaphoreType.DMA((2,))]
+
+    def friends(self):
+        return line_friends()
+
+    def part(self, s):
+        return pl.ds(s * self.rows, self.rows)
+
+    def swap(self, refs, i, s):
         source, _, mate, _, _, sends, receives, _, _, _ = refs
         core = lax.axis_index("core")
-        return remote(source.at[2 * i + 1 - core], mate.at[i], sends.at[i], receives.at[i], {"core": 1 - core})
-
-    def onward(self, refs, i):
+        return remote(
+            source.at[2 * i + 1 - core, self.part(s)], mate.at[i, self.part(s)],
+            sends.at[i, s], receives.at[i, s], {"core": 1 - core},
+        )
+
+    def onward(self, refs, i, s):
         _, _, mate, inbox, _, _, _, sends, receives, _ = refs
-        chip = lax.axis_index("dpo")
-        return remote(mate.at[i], inbox.at[i], sends.at[i], receives.at[i], {"dpo": lax.rem(chip + self.chips - 1, self.chips)})
-
-    def friends(self):
-        return line_friends()
+        left = lax.rem(lax.axis_index("dpo") + self.chips - 1, self.chips)
+        return remote(
+            mate.at[i, self.part(s)], inbox.at[i, self.part(s)], sends.at[i, s], receives.at[i, s], {"dpo": left}
+        )
 
     def begin(self, refs):
         chip = lax.axis_index("dpo")
         for i in range(self.chips):
             @pl.when(i <= chip)
             def _():
-                self.swap(refs, i).start()
+                for s in range(2):
+                    self.swap(refs, i, s).start()
 
     def middle(self, refs, step, last):
-        source, out, mate, inbox, mine, _, _, _, _, sem = refs
+        source, out, mate, inbox, mine, _, _, _, _, sems = refs
         chip, core = lax.axis_index("dpo"), lax.axis_index("core")
         for i in range(self.chips):
-            due = jnp.minimum(1 + 3 * (self.chips - 1 - chip) + i, last)
-
-            @pl.when((i <= chip) & (step == due))
-            def _():
-                local = pltpu.make_async_copy(source.at[2 * i + core], mine, sem)
+            for s in range(2):
+                self.one(refs, step, last, i, s)
+
+    def one(self, refs, step, last, i, s):
+        source, out, mate, inbox, mine, _, _, _, _, sems = refs
+        chip, core = lax.axis_index("dpo"), lax.axis_index("core")
+        part = self.part(s)
+        due = 1 + 2 * (self.chips - 1 - chip) + 2 * i + s
+        local = pltpu.make_async_copy(source.at[2 * i + core, part], mine.at[part], sems.at[s])
+
+        @pl.when((i <= chip) & (step == due - 1) & (due <= last))
+        def _():
+            local.start()
+
+        @pl.when((i <= chip) & (step == jnp.minimum(due, last)))
+        def _():
+            @pl.when(due > last)
+            def _():
                 local.start()
-                self.swap(refs, i).wait()
-                local.wait()
-
-                @pl.when(chip < self.chips - 1)
-                def _():
-                    self.onward(refs, i).wait_recv()
-                    mate[i] = (
-                        mate[i].astype(F32) + mine[...].astype(F32) + inbox[i].astype(F32)
-                    ).astype(mate.dtype)
-
-                @pl.when(chip == self.chips - 1)
-                def _():
-                    mate[i] = (mate[i].astype(F32) + mine[...].astype(F32)).astype(mate.dtype)
-
-                @pl.when(chip > i)
-                def _():
-                    self.onward(refs, i).start()
-
-                @pl.when(chip == i)
-                def _():
-                    out[...] = mate[i].astype(F32)
+
+            self.swap(refs, i, s).wait()
+            local.wait()
+
+            @pl.when(chip == self.chips - 1)
+            def _():
+                mate[i, part] = (mate[i, part].astype(F32) + mine[part].astype(F32)).astype(mate.dtype)
+
+            @pl.when(chip < self.chips - 1)
+            def _():
+                self.onward(refs, i, s).wait_recv()
+                mate[i, part] = (
+                    mate[i, part].astype(F32) + mine[part].astype(F32) + inbox[i, part].astype(F32)
+                ).astype(mate.dtype)
+
+            @pl.when(chip > i)
+            def _():
+                self.onward(refs, i, s).start()
+
+            @pl.when(chip == i)
+            def _():
+                out[part] = mate[i, part].astype(F32)
 
     def end(self, refs):
         chip = lax.axis_index("dpo")
         for i in range(self.chips):
             @pl.when(chip > i)
             def _():
-                self.onward(refs, i).wait_send()
-
-
-class LineSpread(LineSum):
-    def __init__(self, arrays):
+                for s in range(2):
+                    self.onward(refs, i, s).wait_send()
+
+
+class LineFlow:
+    def __init__(self, arrays, rightward, first, hop):
         chips = lax.axis_size("dpo")
-        self.chips = chips
+        self.chips, self.rightward, self.first, self.hop = chips, rightward, first, hop
         self.dimensions = [d for _, d in arrays]
         self.shapes = [
             tuple(n // (2 * chips) if i == d else n for i, n in enumerate(a.shape)) for a, d in arrays
@@ -420,7 +443,7 @@
         n = len(arrays)
         self.ins = [a for a, _ in arrays]
         self.in_specs = [pl.BlockSpec(memory_space=pl.ANY)] * n
-        self.outs = [jax.ShapeDtypeStruct(shape, F32) for shape in self.shapes]
+        self.outs = [jax.ShapeDtypeStruct(shape, BF if rightward else F32) for shape in self.shapes]
         self.out_specs = [
             pl.BlockSpec(shape, lambda *_: (0, 0), pipeline_mode=pl.Buffered(1)) for shape in self.shapes
         ]
@@ -428,16 +451,13 @@
         for shape in self.shapes:
             self.scratch += [
                 pltpu.VMEM((chips,) + shape, BF),
-                pltpu.VMEM((chips + 1,) + shape, BF),
+                pltpu.VMEM((chips,) + shape, BF),
                 pltpu.VMEM(shape, BF),
             ]
-        self.scratch += [
-            pltpu.SemaphoreType.DMA((n, chips)),
-            pltpu.SemaphoreType.DMA((n, chips)),
-            pltpu.SemaphoreType.DMA((n, chips)),
-            pltpu.SemaphoreType.DMA((n, chips + 1)),
-            pltpu.SemaphoreType.DMA((n,)),
-        ]
+        self.scratch += [pltpu.SemaphoreType.DMA((n, chips))] * 4 + [pltpu.SemaphoreType.DMA((n,))]
+
+    def friends(self):
+        return line_friends()
 
     def parts(self, refs):
         n = len(self.shapes)
@@ -449,97 +469,103 @@
         part = pl.ds(pl.multiple_of(place * size, size), size)
         return source.at[part] if self.dimensions[j] == 0 else source.at[:, part]
 
-    def swaps(self, refs, i):
+    def distance(self, i):
+        chip = lax.axis_index("dpo")
+        return i - chip if self.rightward else chip - i
+
+    def swap(self, refs, i, j):
         parts, sems = self.parts(refs)
+        source, _, mate, _, _ = parts[j]
         core = lax.axis_index("core")
-        return [
-            remote(
-                self.block(j, source, 2 * i + 1 - core), mate.at[i], sems[0].at[j, i], sems[1].at[j, i],
-                {"core": 1 - core},
-            )
-            for j, (source, _, mate, _, _) in enumerate(parts)
-        ]
-
-    def onwards(self, refs, i, slot, step):
+        return remote(
+            self.block(j, source, 2 * i + 1 - core), mate.at[i], sems[0].at[j, i], sems[1].at[j, i],
+            {"core": 1 - core},
+        )
+
+    def onward(self, refs, i, j):
         parts, sems = self.parts(refs)
-        chip = lax.axis_index("dpo")
-        to = lax.rem(chip + step + self.chips, self.chips)
-        return [
-            remote(mate.at[i], inbox.at[slot], sems[2].at[j, i], sems[3].at[j, slot], {"dpo": to})
-            for j, (_, _, mate, inbox, _) in enumerate(parts)
-        ]
+        _, _, mate, inbox, _ = parts[j]
+        step = 1 if self.rightward else self.chips - 1
+        to = lax.rem(lax.axis_index("dpo") + step, self.chips)
+        return remote(mate.at[i], inbox.at[i], sems[2].at[j, i], sems[3].at[j, i], {"dpo": to})
 
     def begin(self, refs):
         for i in range(self.chips):
-            for copy in self.swaps(refs, i):
-                copy.start()
+            @pl.when(self.distance(i) >= (1 if self.rightward else 0))
+            def _():
+                for j in range(len(self.shapes)):
+                    self.swap(refs, i, j).start()
 
     def middle(self, refs, step, last):
+        order = range(self.chips - 1, -1, -1) if self.rightward else range(self.chips)
+        for i in order:
+            for j in range(len(self.shapes)):
+                self.one(refs, step, last, i, j)
+
+    def one(self, refs, step, last, i, j):
         chip, core = lax.axis_index("dpo"), lax.axis_index("core")
         parts, sems = self.parts(refs)
+        source, out, mate, inbox, mine = parts[j]
         end = self.chips - 1
-
-        def arrive(i, slot):
-            for copy in self.onwards(refs, i, slot, 0):
-                copy.wait_recv()
-            for _, _, mate, inbox, _ in parts:
-                mate[i] = (mate[i].astype(F32) + inbox[slot].astype(F32)).astype(BF)
-
+        away = self.distance(i)
+        begins = chip == (0 if self.rightward else end)
+        adds = away >= (1 if self.rightward else 0)
+        due = self.first + self.hop * (end - away) + min(j, 1)
+        ahead = pltpu.make_async_copy(self.block(j, source, 2 * i + core), mine, sems[4].at[j])
+
+        @pl.when(adds & (step == due - 1) & (due <= last))
+        def _():
+            ahead.start()
+
+        @pl.when(adds & (step == jnp.minimum(due, last)))
+        def _():
+            @pl.when(due > last)
+            def _():
+                ahead.start()
+
+            self.swap(refs, i, j).wait()
+            ahead.wait()
+
+            @pl.when(begins)
+            def _():
+                mate[i] = (mate[i].astype(F32) + mine[...].astype(F32)).astype(BF)
+
+        @pl.when((away >= 0) & (step == jnp.minimum(due, last)))
+        def _():
+            @pl.when(jnp.logical_not(begins))
+            def _():
+                self.onward(refs, i, j).wait_recv()
+
+            @pl.when(jnp.logical_not(begins) & adds)
+            def _():
+                mate[i] = (
+                    mate[i].astype(F32) + mine[...].astype(F32) + inbox[i].astype(F32)
+                ).astype(BF)
+
+            @pl.when(away > 0)
+            def _():
+                self.onward(refs, i, j).start()
+
+            @pl.when(away == 0)
+            def _():
+                if not self.rightward:
+                    out[...] = mate[i].astype(F32)
+                    return
+
+                @pl.when(begins)
+                def _():
+                    out[...] = jnp.zeros_like(out)
+
+                @pl.when(jnp.logical_not(begins))
+                def _():
+                    out[...] = inbox[i]
+
+    def end(self, refs):
         for i in range(self.chips):
-            due = jnp.minimum(1 + 3 * (end - jnp.abs(chip - i)), last)
-
-            @pl.when(step == due)
-            def _():
-                locals_ = [
-                    pltpu.make_async_copy(self.block(j, source, 2 * i + core), mine, sems[4].at[j])
-                    for j, (source, _, _, _, mine) in enumerate(parts)
-                ]
-                for copy in locals_:
-                    copy.start()
-                for copy in self.swaps(refs, i) + locals_:
-                    copy.wait()
-                for _, _, mate, _, mine in parts:
-                    mate[i] = (mate[i].astype(F32) + mine[...].astype(F32)).astype(BF)
-
-                @pl.when((i <= chip) & (chip < end))
-                def _():
-                    arrive(i, i)
-
-                @pl.when((i > chip) & (chip > 0))
-                def _():
-                    arrive(i, i)
-
-                @pl.when((i == chip) & (chip > 0))
-                def _():
-                    arrive(i, self.chips)
-
-                @pl.when(i < chip)
-                def _():
-                    for copy in self.onwards(refs, i, i, -1):
-                        copy.start()
-
-                @pl.when(i == chip + 1)
-                def _():
-                    for copy in self.onwards(refs, i, self.chips, 1):
-                        copy.start()
-
-                @pl.when(i > chip + 1)
-                def _():
-                    for copy in self.onwards(refs, i, i, 1):
-                        copy.start()
-
-                @pl.when(i == chip)
-                def _():
-                    for _, out, mate, _, _ in parts:
-                        out[...] = mate[i].astype(F32)
-
-    def end(self, refs):
-        chip = lax.axis_index("dpo")
-        for i in range(self.chips):
-            @pl.when(chip != i)
-            def _():
-                for copy in self.onwards(refs, i, i, 0):
-                    copy.wait_send()
+            @pl.when(self.distance(i) > 0)
+            def _():
+                for j in range(len(self.shapes)):
+                    self.onward(refs, i, j).wait_send()
 
 
 class Beside:
@@ -577,10 +603,81 @@
             t.end(held)
 
 
-def settle(part, more, finish, extra, wide, collective):
+class DownProducts:
+    def __init__(self, upstream, count, block_of, down, shared_down):
+        _, rows, model = upstream.shape
+        self.width = shared_down.shape[0]
+        self.steps = down.shape[0] // self.width + 1
+        self.count, self.block_of, self.units = count, block_of, self.steps * count
+        self.ins = [upstream, down, shared_down]
+        self.outs = [jax.ShapeDtypeStruct((self.steps, count, self.width, rows), BF)]
+        self.scratch = [
+            pltpu.VMEM((2, self.width, model), BF),
+            pltpu.VMEM((count, rows, model), BF),
+            pltpu.VMEM((2, self.width, rows), BF),
+            pltpu.SemaphoreType.DMA((2, 1)),
+            pltpu.SemaphoreType.DMA((count,)),
+            pltpu.SemaphoreType.DMA((2,)),
+        ]
+
+    def load(self, refs, step, begin):
+        _, down, shared, _, held, _, _, sems, _, _ = refs
+        weight_copies((down,), (shared,), held, sems, step, lax.rem(step, 2), self.steps, self.width, begin)
+
+    def block(self, refs, i):
+        source, _, _, _, _, rows, _, _, sems, _ = refs
+        return pltpu.make_async_copy(source.at[self.block_of(i)], rows.at[i], sems.at[i])
+
+    def put(self, refs, unit):
+        out, stage, sems = refs[3], refs[6], refs[9]
+        slot = lax.rem(unit, 2)
+        return pltpu.make_async_copy(
+            stage.at[slot], out.at[unit // self.count, lax.rem(unit, self.count)], sems.at[slot]
+        )
+
+    def begin(self, refs):
+        self.load(refs, 0, True)
+        for i in range(self.count):
+            self.block(refs, i).start()
+
+    def run(self, refs, first, last):
+        held, rows, stage = refs[4], refs[5], refs[6]
+
+        def one(unit, carry):
+            step, i = unit // self.count, lax.rem(unit, self.count)
+
+            @pl.when(i == 0)
+            def _():
+                self.load(refs, step, False)
+
+                @pl.when(step < self.steps - 1)
+                def _():
+                    self.load(refs, step + 1, True)
+
+            @pl.when(step == 0)
+            def _():
+                self.block(refs, i).wait()
+
+            @pl.when(unit >= 2)
+            def _():
+                self.put(refs, unit - 2).wait()
+
+            stage[lax.rem(unit, 2)] = nt(held[lax.rem(step, 2)], rows[i]).astype(BF)
+            self.put(refs, unit).start()
+            return carry
+
+        lax.fori_loop(first, last, one, 0)
+
+    def end(self, refs):
+        for unit in (self.units - 2, self.units - 1):
+            self.put(refs, unit).wait()
+
+
+def settle(part, more, finish, extra, wide, fill, splits, collective):
     count, model = part[0].shape[0], part[-1].shape[1]
     ranks = lax.axis_size("tensor")
     quarter = count // ranks
+    size = quarter // 2
     n_part, n_more, n_extra = len(part), len(more), len(extra)
 
     def kernel(*refs):
@@ -592,79 +689,103 @@
             return taken
 
         part_refs, more_refs = take(n_part), take(n_more)
+        fill_refs = take(len(fill.ins))
         (out_ref,), extra_refs = take(1), take(n_extra)
+        fill_refs += take(len(fill.outs))
         inbox, block, gathered, send, receive, send_on, receive_on = take(7)
+        fill_refs += take(len(fill.scratch))
         part_ref = refs[0] if refs else part_refs[0]
         rank, peers = ring_of("tensor")
 
-        def rows_of(i):
-            return pl.ds(pl.multiple_of(i * quarter, quarter), quarter)
-
-        def make(i):
-            if n_part == 2:
-                part_ref[rows_of(i)] = nn(part_refs[0][rows_of(i)], part_refs[1][...]).astype(BF)
-
+        def rows_of(i, s):
+            return pl.ds(pl.multiple_of(i * quarter + s * size, size), size)
+
+        fill.begin(fill_refs)
         greet(rank_friends())
-        copies = []
-        for d, peer in enumerate(peers):
-            if d:
-                make(peer)
-                copies.append(
-                    remote(part_ref.at[rows_of(peer)], inbox.at[d], send.at[d], receive.at[d], {"tensor": peer})
-                )
-                copies[-1].start()
-        make(rank)
-        total = part_ref[rows_of(rank)].astype(F32)
-        for d, copy in enumerate(copies):
-            copy.wait()
-            total = total + inbox[d + 1].astype(F32)
-        results = finish(total, [r[...] for r in more_refs])
-        for ref, value in zip(extra_refs, results):
-            ref[...] = value
-        block[...] = results[-1]
-        copies = [
-            remote(block, gathered.at[d], send_on.at[d], receive_on.at[d], {"tensor": peer})
-            for d, peer in enumerate(peers)
-            if d
-        ]
-        for copy in copies:
-            copy.start()
-        out_ref[rows_of(rank)] = block[...]
-        for d, copy in enumerate(copies):
-            copy.wait()
-            out_ref[rows_of(lax.rem(rank + ranks - d - 1, ranks))] = gathered[d + 1]
+        first, then = [[], []], [[], []]
+        for s in range(2):
+            own = pl.ds(s * size, size)
+            for d, peer in enumerate(peers):
+                rows = rows_of(peer, s)
+                if n_part == 2:
+                    part_ref[rows] = nn(part_refs[0][rows], part_refs[1][...]).astype(BF)
+                if d:
+                    first[s].append(
+                        remote(part_ref.at[rows], inbox.at[d, own], send.at[s, d], receive.at[s, d], {"tensor": peer})
+                    )
+                    first[s][-1].start()
+                    then[s].append(
+                        remote(block.at[own], gathered.at[d, own], send_on.at[s, d], receive_on.at[s, d], {"tensor": peer})
+                    )
+        for s in range(2):
+            own = pl.ds(s * size, size)
+            rows = rows_of(rank, s)
+            fill.run(fill_refs, splits[s], splits[s + 1])
+            total = part_ref[rows].astype(F32)
+            for d, copy in enumerate(first[s]):
+                copy.wait()
+                total = total + inbox[d + 1, own].astype(F32)
+            results = finish(
+                total,
+                [
+                    r[rows] if r.shape[0] == count else r[own] if r.shape[0] == quarter else r[...]
+                    for r in more_refs
+                ],
+            )
+            for ref, value in zip(extra_refs, results):
+                if ref.shape[0] > 1:
+                    ref[own] = value
+                elif s:
+                    ref[...] += value
+                else:
+                    ref[...] = value
+            block[own] = results[-1]
+            for copy in then[s]:
+                copy.start()
+            out_ref[rows] = block[own]
+        fill.run(fill_refs, splits[2], fill.units)
+        fill.end(fill_refs)
+        for s in range(2):
+            for d, copy in enumerate(then[s]):
+                copy.wait()
+                out_ref[rows_of(lax.rem(rank + ranks - d - 1, ranks), s)] = gathered[d + 1, pl.ds(s * size, size)]
 
     vmem = pl.BlockSpec(memory_space=pltpu.VMEM)
-    sems = [pltpu.SemaphoreType.DMA((ranks,))] * 4
+    anywhere = pl.BlockSpec(memory_space=pl.ANY)
+    sems = [pltpu.SemaphoreType.DMA((2, ranks))] * 4
     return pl.pallas_call(
         kernel,
         name="settle",
-        in_specs=[vmem] * (n_part + n_more),
-        out_specs=[vmem] * (1 + n_extra),
-        out_shape=[jax.ShapeDtypeStruct((count, wide), BF)] + extra,
+        in_specs=[vmem] * (n_part + n_more) + [anywhere] * len(fill.ins),
+        out_specs=[vmem] * (1 + n_extra) + [anywhere] * len(fill.outs),
+        out_shape=[jax.ShapeDtypeStruct((count, wide), BF)] + extra + fill.outs,
         scratch_shapes=[
             pltpu.VMEM((ranks, quarter, model), BF),
             pltpu.VMEM((quarter, wide), BF),
             pltpu.VMEM((ranks, quarter, wide), BF),
         ]
         + sems
+        + fill.scratch
         + ([pltpu.VMEM((count, model), BF)] if n_part == 2 else []),
         cost_estimate=SHORT,
         compiler_params=pltpu.CompilerParams(
             vmem_limit_bytes=VMEM_LIMIT, collective_id=collective, has_side_effects=True
         ),
-    )(*part, *more)
-
-
-def group_gradients(rows, upstream, row_cols, up_cols, gates, kept, weights, first, groups, held_back, beside, collective):
+    )(*part, *more, *fill.ins)
+
+
+def group_gradients(rows, upstream, products_back, gates, kept, weights, first, groups, held_back, beside, collective):
     chips, count, model = upstream.shape
     steps, _, parts, _ = gates.shape
     width = weights[3].shape[0]
-    half = row_cols.shape[2] // 2
+    half = model // (2 * chips)
     unit = width // 2
-    n_ins, n_outs, n_held = len(beside.ins), len(beside.outs), len(held_back)
+    weights = weights[:2] + weights[3:5]
+    n_ins, n_outs = len(beside.ins), len(beside.outs)
     last = groups * chips - 1
-    ends = first + groups == steps
+    ends, routes = first + groups == steps, first < steps - 1
+    held_back = held_back if routes else []
+    n_held = len(held_back)
 
     def kernel(*refs):
         refs = list(refs)
@@ -674,11 +795,11 @@
             del refs[:n]
             return taken
 
-        x_ref, c_ref, xc, cc, g_ref, kept_h, kept_g, kept_u = take(8)
-        routed, shared = take(3), take(3)
+        x_ref, xc, cc, b_ref, g_ref, kept_h, kept_g, kept_u = take(8)
+        routed, shared = take(2), take(2)
         take(n_held)
         link_refs = take(n_ins)
-        outs = take(3)
+        outs = take(3) if routes else None
         shared_outs = take(3) if ends else None
         link_refs += take(n_outs)
         held, sems, sum_g, sum_u, sum_d, outbox, inbox, sends, receives = take(9)
@@ -689,6 +810,10 @@
         slot = lax.rem(at_group, 2)
         tick = at_group * chips + turn
         sums = (sum_g, sum_u, sum_d)
+        core = lax.axis_index("core")
+
+        def columns_of(i):
+            return pl.ds(pl.multiple_of(i * half, half), half)
 
         def swap(i):
             part = pl.ds(i * unit, unit)
@@ -719,22 +844,31 @@
 
         def work(final):
             x = x_ref[0]
-            c = c_ref[0]
             gate = gate_rows(g_ref[0, 0], width)
-            for i in range(2):
-                at = i * unit
-                part = slice(at, at + unit)
-                gate_pre = nt(held[slot, at : at + unit], x)
-                up_pre = nt(held[slot, width + at : width + at + unit], x)
-                hidden_grad = nt(held[slot, 2 * width + at : 2 * width + at + unit], c)
-                hidden, d_gate, d_up, _ = expert_unit(gate_pre, up_pre, hidden_grad, gate[part])
-                sum_g[part] += nn(d_gate, xc[0])
-                sum_u[part] += nn(d_up, xc[0])
-                sum_d[part] += nn(hidden, cc[0])
-                if final:
-                    for j, total in enumerate(sums):
-                        outbox[j, part] = total[part, half:].astype(BF)
-                    swap(i).start()
+            parts_ = [slice(i * unit, (i + 1) * unit) for i in range(2)]
+            pre = [
+                (nt(held[slot, part], x), nt(held[slot, width + part.start : width + part.stop], x))
+                for part in parts_
+            ]
+            terms = []
+            for part, (gate_pre, up_pre) in zip(parts_, pre):
+                hidden, d_gate, d_up, _ = expert_unit(
+                    gate_pre, up_pre, b_ref[0, 0, part].astype(F32), gate[part]
+                )
+                terms.append(((d_gate, xc), (d_up, xc), (hidden, cc)))
+                if not final:
+                    for total, (term, columns) in zip(sums, terms[-1]):
+                        total[part] += nn(term, columns[0])
+            if not final:
+                return
+            far, near = columns_of(1 - core), columns_of(core)
+            for i, part in enumerate(parts_):
+                for j, (total, (term, columns)) in enumerate(zip(sums, terms[i])):
+                    outbox[j, part] = (total[part, far] + nn(term, columns[0, :, far])).astype(BF)
+                swap(i).start()
+            for part, made in zip(parts_, terms):
+                for total, (term, columns) in zip(sums, made):
+                    total[part, near] += nn(term, columns[0, :, near])
 
         @pl.when((turn > 0) & (turn < chips - 1))
         def _():
@@ -747,14 +881,15 @@
                 swap(i).wait()
                 part = slice(i * unit, (i + 1) * unit)
                 for j, total in enumerate(sums):
-                    value = (total[part, :half] + inbox[slot, j, part].astype(F32)).astype(BF)
+                    value = (total[part, columns_of(core)] + inbox[slot, j, part].astype(F32)).astype(BF)
                     if not ends:
                         outs[j][part] = value
                         continue
 
-                    @pl.when(step < steps - 1)
-                    def _():
-                        outs[j][part] = value
+                    if routes:
+                        @pl.when(step < steps - 1)
+                        def _():
+                            outs[j][part] = value
 
                     @pl.when(step == steps - 1)
                     def _():
@@ -774,6 +909,8 @@
 
     def one(shape):
         return pl.BlockSpec((1,) + shape, lambda p, k: (p + first, 0, 0))
+
+    columns = pl.BlockSpec((1, count, 2 * half), lambda p, k: (chip_at(k), 0, lax.axis_index("dpo")))
 
     anywhere = pl.BlockSpec(memory_space=pl.ANY)
     block = pl.BlockSpec((width, half), lambda p, k: (jnp.minimum(p + first, steps - 2), 0))
@@ -784,16 +921,17 @@
         grid_spec=pltpu.PrefetchScalarGridSpec(
             num_scalar_prefetch=0,
             grid=(groups, chips),
-            in_specs=[at_chip((count, model))] * 2
-            + [at_chip((count, 2 * half))] * 2
+            in_specs=[at_chip((count, model))]
+            + [columns] * 2
+            + [pl.BlockSpec((1, 1, width, count), lambda p, k: (p + first, jnp.maximum(k - 1, 0), 0, 0))]
             + [pl.BlockSpec((1, 1, parts, count), lambda p, k: (p + first, chip_at(k), 0, 0))]
             + [one((width, count))] * 3
-            + [anywhere] * (6 + n_held)
+            + [anywhere] * (4 + n_held)
             + beside.in_specs,
-            out_specs=[block] * 3 + ([shared_block] * 3 if ends else []) + beside.out_specs,
+            out_specs=([block] * 3 if routes else []) + ([shared_block] * 3 if ends else []) + beside.out_specs,
             scratch_shapes=[
-                pltpu.VMEM((2, 3 * width, model), BF),
-                pltpu.SemaphoreType.DMA((2, 3)),
+                pltpu.VMEM((2, 2 * width, model), BF),
+                pltpu.SemaphoreType.DMA((2, 2)),
             ]
             + [pltpu.VMEM((width, 2 * half), F32)] * 3
             + [
@@ -804,12 +942,12 @@
             ]
             + beside.scratch,
         ),
-        out_shape=[jax.ShapeDtypeStruct(((steps - 1) * width, half), BF)] * 3
+        out_shape=([jax.ShapeDtypeStruct(((steps - 1) * width, half), BF)] * 3 if routes else [])
         + ([jax.ShapeDtypeStruct((width, half), BF)] * 3 if ends else [])
         + beside.outs,
-        input_output_aliases={14 + i: i for i in range(n_held)},
+        input_output_aliases={12 + i: i for i in range(n_held)},
         cost_estimate=pl.CostEstimate(
-            flops=groups * 2 * width * count * (3 * (chips - 1) * model + 6 * chips * half),
+            flops=groups * 2 * width * count * (2 * (chips - 1) * model + 6 * chips * half),
             bytes_accessed=groups * (6 * width * model + 4 * chips * count * model),
             transcendentals=0,
         ),
@@ -820,7 +958,7 @@
             has_side_effects=True,
         ),
     )(
-        rows, upstream, row_cols, up_cols, gates, *kept, *weights, *held_back, *beside.ins,
+        rows, rows, upstream, products_back, gates, *kept, *weights, *held_back, *beside.ins,
     )
 
 
@@ -839,7 +977,7 @@
     scale = (ND + RD) ** (-0.5) * LOG2E
 
     def kernel(x_ref, gain_ref, qw_ref, ld_ref, lg_ref, up_ref, even_ref, odd_ref, kid_ref, qid_ref,
-               att_ref, lse_ref, all_ref, in_ref, raw_ref, q_ref, lat_ref, rope_ref, keys, top, low, mix,
+               att_ref, lse_ref, all_ref, in_ref, raw_ref, q_ref, factor_ref, lat_ref, rope_ref, keys, top, low, mix,
                send_right, take_left, send_mate, take_mate, send_rank, take_rank):
         chip, core = lax.axis_index("dpo"), lax.axis_index("core")
         rank, peers = ring_of("tensor")
@@ -871,7 +1009,8 @@
             ]
 
         x = x_ref[...].astype(F32)
-        normed, _ = norm_rows(x, gain_ref[...])
+        normed, factor = norm_rows(x, gain_ref[...])
+        factor_ref[...] = jnp.broadcast_to(factor, (count, 128))
         in_ref[...] = normed.astype(BF)
         raw = nt(in_ref[...], ld_ref[:KVL])
         raw_ref[...] = raw
@@ -986,7 +1125,7 @@
         kernel,
         name="attention_forward",
         in_specs=[vmem] * 10,
-        out_specs=[vmem] * 6,
+        out_specs=[vmem] * 7,
         out_shape=[
             jax.ShapeDtypeStruct((count, heads * VD), BF),
             jax.ShapeDtypeStruct((heads, 1, count), F32),
@@ -994,6 +1133,7 @@
             jax.ShapeDtypeStruct((count, model), BF),
             jax.ShapeDtypeStruct((count, KVL), F32),
             jax.ShapeDtypeStruct((count, heads * 256), BF),
+            jax.ShapeDtypeStruct((count, 128), F32),
         ],
         scratch_shapes=[
             pltpu.VMEM((count, LAT), BF),
@@ -1016,15 +1156,19 @@
     )(tokens, gain, query_weight, latent_rows, latent_gain, latent_up, even, odd, key_ids, query_ids)
 
 
-def attention_backward(queries, latents, latent_up, key_ids, query_ids, attended, output_grad, output_weight, lse, even, odd):
-    count = queries.shape[0]
+def attention_backward(queries, latents, latent_up, key_ids, query_ids, attended, output_grad, output_weight, lse, even, odd, rows, query_weight, beside, collective):
+    count, model = rows.shape
     heads = queries.shape[1] // 256
     blocks = latents.shape[0]
     factor = (ND + RD) ** (-0.5)
     scale = factor * LOG2E
 
-    def kernel(q_ref, lat_ref, up_ref, kid_ref, qid_ref, att_ref, og_ref, ow_ref, lse_ref, even_ref, odd_ref,
-               dq_ref, dup_ref, dlat_ref, do_ref, delta, keys, dq, dup, dlat):
+    def kernel(q_ref, lat_ref, up_ref, kid_ref, qid_ref, att_ref, og_ref, ow_ref, lse_ref, even_ref, odd_ref, in_ref, qw_ref,
+               sent_ref, dqw_ref, dow_ref, din_ref, dup_ref, dlat_ref, got_ref, dq_ref, do_ref, delta, keys, dq, dup, dlat,
+               send, receive):
+        link_refs = [sent_ref, got_ref, send, receive]
+        greet(beside.friends())
+        beside.begin(link_refs)
         place = lax.axis_index("dpo") * 2 + lax.axis_index("core")
         dq[...] = jnp.zeros_like(dq)
         dup[...] = jnp.zeros_like(dup)
@@ -1084,29 +1228,97 @@
             dq_ref[:, at + 256 : at + 384] = jnp.where(
                 lane < 64, moved, pltpu.roll(ropes[1], 64, 1)
             ).astype(BF)
+        turned_mix = att_ref[...].T
+        for at in range(0, model, 512):
+            part = slice(at, at + 512)
+            dqw_ref[part] = nn(in_ref[:, part].T, dq_ref[...]).astype(BF)
+            dow_ref[:, part] = nn(turned_mix, og_ref[:, part]).astype(BF)
+            din_ref[:, part] = nt(dq_ref[...], qw_ref[part]).astype(BF)
+        beside.end(link_refs)
 
     vmem = pl.BlockSpec(memory_space=pltpu.VMEM)
     return pl.pallas_call(
         kernel,
         name="attention_backward",
-        in_specs=[vmem] * 11,
-        out_specs=[vmem] * 3,
+        in_specs=[vmem] * 13 + beside.in_specs,
+        out_specs=[vmem] * 5 + beside.out_specs,
         out_shape=[
-            jax.ShapeDtypeStruct((count, heads * (ND + RD)), BF),
+            jax.ShapeDtypeStruct(query_weight.shape, BF),
+            jax.ShapeDtypeStruct(output_weight.shape, BF),
+            jax.ShapeDtypeStruct((count, model), BF),
             jax.ShapeDtypeStruct((KVL, heads * 256), BF),
             jax.ShapeDtypeStruct((blocks, count, LAT), BF),
-        ],
+        ]
+        + beside.outs,
         scratch_shapes=[
+            pltpu.VMEM((count, heads * (ND + RD)), BF),
             pltpu.VMEM((count, heads * VD), BF),
             pltpu.VMEM((heads, 1, count), F32),
             pltpu.VMEM((heads, count, 256), BF),
             pltpu.VMEM((heads, 256, count), F32),
             pltpu.VMEM((KVL, heads * 256), F32),
             pltpu.VMEM((count, LAT), F32),
+        ]
+        + beside.scratch,
+        cost_estimate=SHORT,
+        compiler_params=pltpu.CompilerParams(
+            vmem_limit_bytes=VMEM_LIMIT, collective_id=collective, has_side_effects=True
+        ),
+    )(queries, latents, latent_up, key_ids, query_ids, attended, output_grad, output_weight, lse, even, odd, rows, query_weight,
+      *beside.ins)
+
+
+def latents_back(compressed_grad, raw, latent_gain, even, odd, latent_rows, query_part, tokens, first_factor, rows):
+    count, model = tokens.shape
+    wide = 512
+    lanes = KVL + RD
+
+    def kernel(cg_ref, raw_ref, gain_ref, even_ref, odd_ref, ld_ref, qp_ref, x_ref, ff_ref, in_ref,
+               out_ref, dld_ref, lgain_ref, fgain_ref, down):
+        @pl.when(pl.program_id(0) == 0)
+        def _():
+            raw = raw_ref[...]
+            factor = lax.rsqrt(jnp.mean(raw * raw, axis=-1, keepdims=True) + EPSILON)
+            back, gain_grad = norm_back(raw, factor, gain_ref[...], cg_ref[:, :KVL])
+            lgain_ref[...] = gain_grad[None]
+            down[:, :KVL] = back.astype(BF)
+            down[:, KVL:] = turn_pairs(cg_ref[:, KVL:], even_ref[...], -odd_ref[...])[:, :RD].astype(BF)
+
+        grad = qp_ref[...].astype(F32) + nn(down[...], ld_ref[...])
+        out_ref[...] = grad.astype(BF)
+        fgain_ref[...] = jnp.sum(grad * x_ref[...].astype(F32) * ff_ref[:, :1], axis=0, keepdims=True)
+        dld_ref[...] = nn(in_ref[...].T, down[...]).astype(BF)
+
+    def whole(shape):
+        return pl.BlockSpec(shape, lambda p: (0,) * len(shape), pipeline_mode=pl.Buffered(1))
+
+    def columns(size):
+        return pl.BlockSpec((size, wide), lambda p: (0, p))
+
+    return pl.pallas_call(
+        kernel,
+        name="latents_back",
+        grid=(model // wide,),
+        in_specs=[whole(a.shape) for a in (compressed_grad, raw, latent_gain, even, odd)]
+        + [columns(lanes), columns(count), columns(count), whole(first_factor.shape), columns(count)],
+        out_specs=[
+            columns(count),
+            pl.BlockSpec((wide, lanes), lambda p: (p, 0)),
+            whole((1, KVL)),
+            columns(1),
         ],
+        out_shape=[
+            jax.ShapeDtypeStruct((count, model), BF),
+            jax.ShapeDtypeStruct((model, lanes), BF),
+            jax.ShapeDtypeStruct((1, KVL), F32),
+            jax.ShapeDtypeStruct((1, model), F32),
+        ],
+        scratch_shapes=[pltpu.VMEM((count, lanes), BF)],
         cost_estimate=SHORT,
-        compiler_params=pltpu.CompilerParams(vmem_limit_bytes=VMEM_LIMIT),
-    )(queries, latents, latent_up, key_ids, query_ids, attended, output_grad, output_weight, lse, even, odd)
+        compiler_params=pltpu.CompilerParams(
+            vmem_limit_bytes=VMEM_LIMIT, dimension_semantics=("arbitrary",)
+        ),
+    )(compressed_grad, raw, latent_gain, even, odd, latent_rows, query_part, tokens, first_factor, rows)
 
 
 def grouped(gates, steps):
@@ -1170,7 +1382,7 @@
     odd = jnp.concatenate([-sine_table, sine_table, rest], axis=1)
     key_ids, query_ids = own_blocks[:, None], own_blocks[None, :]
     all_upstream = lax.all_gather(cotangent, "dpo", axis=0, tiled=True)
-    attended, lse, latents, attention_input, latent_raw, queries = attention_forward(
+    attended, lse, latents, attention_input, latent_raw, queries, first_factor = attention_forward(
         tokens, first_gain[None], query_weight, latent_down.T, latent_gain[None], latent_up,
         even, odd, key_ids, query_ids, 1,
     )
@@ -1197,24 +1409,27 @@
         return residual, jnp.concatenate([normed, gates.astype(BF)], axis=1)
 
     twice = jnp.pad(router_weight, ((0, 0), (0, 16 - EXPERTS)))
-    wide_input, residual = settle(
+    own_fill = DownProducts(cotangent[None], 1, lambda i: i, weights[2], weights[5])
+    wide_input, residual, own_products = settle(
         [attended, output_weight],
         [
-            token_quarter,
+            tokens,
             second_gain[None],
             jnp.pad(jnp.concatenate([twice, twice], axis=1), ((0, 0), (0, 96))),
-            mine(named),
+            named,
         ],
         second_norm,
         [jax.ShapeDtypeStruct((quarter, model), F32)],
         model + 128,
+        own_fill,
+        (0, own_fill.units - 2, own_fill.units),
         2,
     )
     all_input = lax.all_gather(wide_input, "dpo", axis=0, tiled=True)
     all_input = all_input.reshape(chips, count, model + 128)
 
     expert_part, input_back, kept_h, kept_g, kept_u, logit_grad = own_experts(
-        wide_input, cotangent, twice.T, weights
+        wide_input, own_products, twice.T, weights
     )
 
     def second_norm_back(total, more):
@@ -1225,15 +1440,21 @@
         return back, gain_grad[None], back.astype(BF)
 
     input_back, all_upstream = lax.optimization_barrier((input_back, all_upstream))
-    output_grad, residual_grad, grad_second_gain = settle(
+    all_upstream = all_upstream.reshape(chips, count, model)
+    far_fill = DownProducts(
+        all_upstream, chips - 1, lambda i: lax.rem(lax.axis_index("dpo") + 1 + i, chips), weights[2], weights[5]
+    )
+    output_grad, residual_grad, grad_second_gain, far_products = settle(
         [input_back],
-        [residual, second_gain[None], mine(cotangent)],
+        [residual, second_gain[None], cotangent],
         second_norm_back,
         [
             jax.ShapeDtypeStruct((quarter, model), F32),
             jax.ShapeDtypeStruct((1, model), F32),
         ],
         model,
+        far_fill,
+        (0, far_fill.units * 2 // 7, far_fill.units * 4 // 7),
         3,
     )
     grad_second_gain = grad_second_gain[0]
@@ -1243,96 +1464,52 @@
     )
     all_gates = jnp.swapaxes(all_gates, 1, 2)
 
-    def chip_columns(array):
-        return jnp.concatenate(
-            [
-                lax.dynamic_slice_in_dim(array, (chip * 2 + c) * half, half, 2)
-                for c in (core, 1 - core)
-            ],
-            axis=2,
-        )
-
-    all_upstream = all_upstream.reshape(chips, count, model)
-    input_cols, upstream_cols = chip_columns(all_input), chip_columns(all_upstream)
     routed_grads = []
 
     def piece(first, groups, beside, collective):
         made = group_gradients(
-            all_input, all_upstream, input_cols, upstream_cols, all_gates,
+            all_input, all_upstream, far_products, all_gates,
             (kept_h, kept_g, kept_u), weights, first, groups, routed_grads, beside, collective,
         )
+        if first == steps - 1:
+            return made
         routed_grads[:] = made[:3]
         return made[3:]
 
     def summed(rows, got):
         return mine(rows).astype(F32) + jnp.sum(got.astype(F32), axis=0)
 
-    query_grad, grad_latent_up, latent_part = attention_backward(
-        queries, latents, latent_up, key_ids, query_ids, attended, output_grad, output_weight, lse, even, odd
-    )
-    grad_output = tn(attended, output_grad).astype(BF)
-    grad_query = tn(attention_input, query_grad).astype(BF)
-    query_part = nt(query_grad, query_weight)
-    latent_part, grad_query, query_part = lax.optimization_barrier(
-        (latent_part, grad_query, query_part)
-    )
-    (compressed_grad,) = piece(0, 2, LineSum(latent_part), 5)
-    _, latent_factor = norm_rows(latent_raw, latent_gain)
-    latent_grad, grad_latent_gain = norm_back(
-        latent_raw, latent_factor, latent_gain, compressed_grad[:, :KVL]
-    )
-    down_grad = jnp.concatenate(
-        [latent_grad, rotate(compressed_grad[:, KVL : KVL + RD], cosine, -sine_table)], axis=1
-    ).astype(BF)
-    attention_grad = query_part + nt(down_grad, latent_down)
-    rows_float = tokens.astype(F32)
-    _, first_factor = norm_rows(rows_float, first_gain)
-    grad_first_gain = jnp.sum(attention_grad * rows_float * first_factor, axis=0)
-    attention_grad = attention_grad.astype(BF)
-    grad_latent_down = lax.psum_scatter(
-        tn(attention_input, down_grad).astype(BF), DP, scatter_dimension=0, tiled=True
-    )
-    grad_query, grad_latent_up, grad_output, got, got_result = piece(
-        2,
-        steps - 4,
+    grad_query, grad_output, query_part, grad_latent_up, latent_part, got_result = attention_backward(
+        queries, latents, latent_up, key_ids, query_ids, attended, output_grad, output_weight, lse, even, odd,
+        attention_input, query_weight, Scatter(expert_part), 4,
+    )
+    query_flow = [(grad_query, 0)]
+    other_flow = [(grad_latent_up, 0), (grad_output, 1)]
+    compressed_grad, *flows, result = piece(
+        0,
+        4,
         Beside(
-            LineSpread([(grad_query, 0), (grad_latent_up, 0), (grad_output, 1)]),
-            Many([Scatter(attention_grad), Scatter(expert_part)]),
+            LineSum(latent_part),
+            Beside(
+                LineFlow(query_flow + other_flow, True, 2, 3),
+                Beside(
+                    LineFlow(other_flow, False, 6, 3),
+                    Gather((residual + summed(expert_part, got_result)).astype(BF)),
+                ),
+            ),
         ),
-        6,
-    )
-    token_back, _ = norm_back(
-        token_quarter.astype(F32), mine(first_factor), first_gain, summed(attention_grad, got)
-    )
-    *shared_grads, token_grad, result = piece(
-        steps - 2,
-        2,
-        Many(
-            [
-                Gather((token_back + residual_grad).astype(BF)),
-                Gather((residual + summed(expert_part, got_result)).astype(BF)),
-            ]
-        ),
-        7,
-    )
-    token_grad, result = token_grad.reshape(count, model), result.reshape(count, model)
+        5,
+    )
+    attention_grad, grad_latent_down, grad_latent_gain, grad_first_gain = latents_back(
+        compressed_grad, latent_raw, latent_gain[None], even, odd, latent_down.T, query_part, tokens,
+        first_factor, attention_input,
+    )
+    grad_latent_down = lax.psum_scatter(grad_latent_down, DP, scatter_dimension=0, tiled=True)
 
     grad_router = lax.dot_general(
         wide_input[:, :model], logit_grad[:EXPERTS].astype(BF), (((0,), (1,)), ((), ())),
         preferred_element_type=F32,
     )
-
-    def over_ranks(array):
-        blocks = array.reshape((ranks, -1) + array.shape[1:])
-
-        def block(d):
-            return lax.dynamic_index_in_dim(blocks, lax.rem(rank + d, ranks), 0, keepdims=False)
-
-        total = block(0).astype(F32)
-        for d in range(1, ranks):
-            route = [(i, (i + d) % ranks) for i in range(ranks)]
-            total = total + lax.ppermute(block(d), "tensor", route).astype(F32)
-        return total
 
     def for_ranks(gain):
         return jnp.repeat(gain.reshape(2 * chips, -1), ranks, axis=0)
@@ -1345,10 +1522,46 @@
             grad_latent_gain.reshape(devices, -1),
         ],
         axis=1,
-    )
-    small = jnp.pad(small, ((0, 0), (0, -small.shape[1] % 1024)))
-    small = lax.psum_scatter(small.reshape(-1, 128), DP, scatter_dimension=0, tiled=True)
-    small = over_ranks(small).reshape(-1)
+    ).astype(BF)
+    small = jnp.pad(small, ((0, 0), (0, 2048 - small.shape[1]))).reshape(devices * 16, 128)
+
+    query_flow, small_left, small_right, got = piece(
+        4,
+        steps - 5,
+        Beside(
+            Beside(LineFlow(query_flow + [(small, 0)], False, 1, 2), LineFlow([(small, 0)], True, 1, 2)),
+            Scatter(attention_grad),
+        ),
+        6,
+    )
+    grad_query, grad_latent_up, grad_output = (
+        near + far.astype(F32) for near, far in zip([query_flow] + flows[3:], flows[:3])
+    )
+    token_float = token_quarter.astype(F32)
+    _, token_factor = norm_rows(token_float, first_gain)
+    token_back, _ = norm_back(token_float, token_factor, first_gain, summed(attention_grad, got))
+    small = (small_left + small_right.astype(F32)).astype(BF)
+    *shared_grads, token_grad, got_down, got_small = piece(
+        steps - 1,
+        1,
+        Many(
+            [
+                Gather((token_back + residual_grad).astype(BF)),
+                Scatter(grad_latent_down),
+                Scatter(small),
+            ]
+        ),
+        7,
+    )
+    token_grad, result = token_grad.reshape(count, model), result.reshape(count, model)
+
+    def over_ranks(rows, got):
+        size = got.shape[1]
+        own = lax.dynamic_slice_in_dim(rows, rank * size, size, 0)
+        return own.astype(F32) + jnp.sum(got.astype(F32), axis=0)
+
+    grad_latent_down = over_ranks(grad_latent_down, got_down)
+    small = over_ranks(small, got_small).reshape(-1)
     router_size = model // devices * EXPERTS
     gain_size = model // (2 * chips)
     latent_size = KVL // devices
@@ -1363,7 +1576,7 @@
         token_grad,
         small[gain_size : 2 * gain_size],
         grad_query,
-        over_ranks(grad_latent_down),
+        grad_latent_down,
         small[2 * gain_size : 2 * gain_size + latent_size],
         grad_latent_up,
         grad_output,

time: 651 us -> 583 us (0.90)
  Pallas kernels: 476 us -> 443 us
  matrix products: 23 us -> 1.14 us
  local copies, waits for them, and re-layouts: 29 us -> 14.4 us
  waiting for transfers between devices: 53.2 us -> 67.8 us
  starting transfers between devices: 8.48 us -> 0.52 us
    pallas_call x3, Pallas kernels: 242 us -> 194 us  [group_gradients(): pl.pallas_call(kernel, name='group_gradients', grid_spec=pltpu.PrefetchSc...]
    pallas_call x1 -> x2, Pallas kernels: 17.1 us -> 46.6 us  [the longest x1 37.3 us: attention_backward(): pl.pallas_call(kernel, name='attention_backward', in_specs=[vmem] * 13 +...]
    dot_general x5 -> x0, matrix products: 21.3 us -> none  [the longest x3 10.9 us: tn(): lax.dot_general(former, latter, (((0,), (0,)), ((), ())), preferred_eleme...]
    all_gather x1, waiting for transfers between devices: 51.3 us -> 67.1 us  [shards(): all_input = lax.all_gather(wide_input, 'dpo', axis=0, tiled=True)]
    pallas_call x1, Pallas kernels: 81.7 us -> 71.6 us  [own_experts(): pl.pallas_call(kernel, name='own_experts', grid=(steps,), in_specs=[whole...]
    ppermute x6 -> x0, starting transfers between devices: 7.92 us -> none  [over_ranks(): total = total + lax.ppermute(block(d), 'tensor', route).astype(F32)]
    dynamic_slice x4 -> x0, local copies, waits for them, and re-layouts: 7.18 us -> none  [the longest x2 3.77 us: mine(): return lax.dynamic_slice_in_dim(array, rank * quarter, quarter, 0)]
  transfers between devices with their start and end apart: 10 -> 3, of which waited for: 3 -> 1; matrix products, arithmetic and copies ran while one was open for 10% -> 5% of each run, Pallas kernels for 59% -> 54%
where the time goes in v5:
time: 583 us; the launch traced here: 573 us
  Pallas kernels  443 us (76%)
  waiting for transfers between devices  67.8 us (12%)
  other arithmetic  31.4 us (5%)
  between operations  14.5 us (2%)
  local copies, waits for them, and re-layouts  14.4 us (2%)
    pallas_call x3, Pallas kernels, group_gradients(): pl.pallas_call(kernel, name='group_gradients', grid_spec=pltpu.PrefetchSc...  194 us
    pallas_call x2, Pallas kernels, settle(): pl.pallas_call(kernel, name='settle', in_specs=[vmem] * (n_part + n_more)...  109 us
    pallas_call x1, Pallas kernels, own_experts(): pl.pallas_call(kernel, name='own_experts', grid=(steps,), in_specs=[whole...  71.6 us
    all_gather x1, waiting for transfers between devices, shards(): all_input = lax.all_gather(wide_input, 'dpo', axis=0, tiled=True)  67.1 us
    pallas_call x1, Pallas kernels, attention_backward(): pl.pallas_call(kernel, name='attention_backward', in_specs=[vmem] * 13 +...  37.3 us
    pallas_call x1, Pallas kernels, attention_forward(): pl.pallas_call(kernel, name='attention_forward', in_specs=[vmem] * 10, ou...  22.3 us
  transfers between devices with their start and end apart: 3, of which 1 were waited for; matrix products, arithmetic and copies ran while one was open for 5% of the time, Pallas kernels for 54%

profile of v5, /device:TPU:0, one launch (start us, length us, event | category | flops | bytes accessed | tf_op | source)
XLA Modules:
  0.0 573.0 jit_solution(2568430264416150467)
XLA Ops:
  9.7 1.0 fusion.17
  10.7 1.0 maximum_maximum_fusion.1
  11.7 22.3 %attention_forward.1 = (bf16[512,512]{1,0:T(8,128)(2,1)}, f32[4,1,512]{2,1,0:T(1,128)}, bf16[8,512,640]{2,1,0:T(8,128)(2,1)}, bf16[512,2048]{1,0:T(8,128)(2,1)},...) custom-call(bf16[512,2048]{1,0:T(8,128)(2,1)} %x_ref.3, f32[1,2048]{1,0:T(1,128)} %bitcast.94, ...), custom_call_target="tpu_custom_call" | custom-call | flops 1000 | bytes 100000 | tf_op jit(solution)/shard_map/attention_forward/pallas_call | solution.py:1124
  35.0 0.9 pad.15.clone.refs_4_
  37.2 55.3 %settle.2 = (bf16[512,2176]{1,0:T(8,128)(2,1)}, f32[128,2048]{1,0:T(8,128)}, bf16[7,1,704,512]{3,2,1,0:T(8,128)(2,1)}) custom-call(bf16[512,512]{1,0:T(8,128)(2,1)} %get-tuple-element.71.refs_0_.att_ref, bf16[512,2048]{1,0:T(8,128)(2,1)} %ow_ref.1, bf16[512,2048]{1,0:T(8,128)(2,1)} %x_ref.3, f32[1,2048]{1,0:T(1,128)} %bitcast.95, ...), custom_call_target="tpu_custom_call" | custom-call | flops 1000 | bytes 100000 | tf_op jit(solution)/shard_map/settle/pallas_call | solution.py:756
  93.0 71.6 %own_experts.1 = (bf16[512,2048]{1,0:T(8,128)(2,1)}, bf16[512,2048]{1,0:T(8,128)(2,1)}, bf16[7,704,512]{2,1,0:T(8,128)(2,1)}, bf16[7,704,512]{2,1,0:T(8,128)(2,1...) custom-call(bf16[512,2176]{1,0:T(8,128)(2,1)} %get-tuple-element.72.x_ref.tail_ref, ...), custom_call_target="tpu_custom_call" | custom-call | flops 1000 | bytes 100000 | tf_op jit(solution)/shard_map/own_experts/pallas_call | solution.py:188
  164.5 1.1 convolution_convert_fusion
  166.8 53.6 %settle.3 = (bf16[512,2048]{1,0:T(8,128)(2,1)}, f32[128,2048]{1,0:T(8,128)}, f32[1,2048]{1,0:T(1,128)}, bf16[7,3,704,512]{3,2,1,0:T(8,128)(2,1)}) custom-call(bf16[512,2048]{1,0:T(8,128)(2,1)} %get-tuple-element.76.refs_0_, f32[128,2048]{1,0:T(8,128)} %get-tuple-element.77.refs_1_, f32[1,2048]{1,0:T(1,128)} %bitcast.96, bf16[512,2048]{1,0:T(8,128)(2,1)} %refs_3_.1, ...), custom_call_target="tpu_custom_call" | custom-call | flops 1000 | bytes 100000 | tf_op jit(solution)/shard_map/settle/pallas_call | solution.py:756
  220.5 37.3 %attention_backward.1 = (bf16[2048,768]{1,0:T(8,128)(2,1)}, bf16[512,2048]{1,0:T(8,128)(2,1)}, bf16[512,2048]{1,0:T(8,128)(2,1)}, bf16[512,1024]{1,0:T(8,128)(2,...) custom-call(bf16[512,1024]{1,0:T(8,128)(2,1)} %get-tuple-element.82.q_ref, ...), custom_call_target="tpu_custom_call" | custom-call | flops 1000 | bytes 100000 | tf_op jit(solution)/shard_map/attention_backward/pallas_call | solution.py:1240
  257.9 1.9 convert_reduce_fusion.1
  259.9 2.1 add_convert_fusion.refs_18_
  261.9 67.1 %all-gather.3.cloned.1.call-done = bf16[2048,2176]{1,0:T(8,128)(2,1)} async-done(((bf16[512,2176]{1,0:T(8,128)(2,1)}), bf16[2048,2176]{1,0:T(8,128)(2,1)}) %all-gather.3.cloned.1.call-update) | async-done | bytes 8912912 | tf_op jit(solution)/shard_map/all_gather | solution.py:1428
  329.0 1.1 slice_bitcast_fusion
  331.1 92.1 %group_gradients.3 = (bf16[4224,256]{1,0:T(8,128)(2,1)}, bf16[4224,256]{1,0:T(8,128)(2,1)}, bf16[4224,256]{1,0:T(8,128)(2,1)}, f32[512,640]{1,0:T(8,128)}, bf16[...) custom-call(bf16[4,512,2176]{2,1,0:T(8,128)(2,1)} %bitcast.63, ...), custom_call_target="tpu_custom_call" | custom-call | flops 53150220288 | bytes 101711872 | tf_op jit(solution)/shard_map/group_gradients/pallas_call | solution.py:918
  423.2 9.3 %latents_back.1 = (bf16[512,2048]{1,0:T(8,128)(2,1)}, bf16[2048,576]{1,0:T(8,128)(2,1)}, f32[1,512]{1,0:T(1,128)}, f32[1,2048]{1,0:T(1,128)}) custom-call(f32[512,640]{1,0:T(8,128)} %get-tuple-element.94.cg_ref, f32[512,512]{1,0:T(8,128)} %get-tuple-element.95.raw_ref, f32[1,512]{1,0:T(1,128)} %bitcast.101, f32[512,128]{1,0:T(8,128)} %get-tuple-element.200.even_ref, ...), custom_call_target="tpu_custom_call" | custom-call | flops 1000 | bytes 100000 | tf_op jit(solution)/shard_map/latents_back/pallas_call | solution.py:1298
  434.2 67.8 %group_gradients.4 = (bf16[4224,256]{1,0:T(8,128)(2,1)}, bf16[4224,256]{1,0:T(8,128)(2,1)}, bf16[4224,256]{1,0:T(8,128)(2,1)}, f32[256,768]{1,0:T(8,128)}, f32[6...) custom-call(bf16[4,512,2176]{2,1,0:T(8,128)(2,1)} %bitcast.65, ...), custom_call_target="tpu_custom_call", output_to_operand_aliasing={{0}: (12, {}), {1}: (13, {}), {2}: (14, {})} | custom-call | flops 26575110144 | bytes 50855936 | tf_op jit(solution)/shard_map/group_gradients/pallas_call | solution.py:918
  502.0 4.2 convert.42
  506.6 1.2 copy-done
  509.6 0.9 convert_add_fusion.1
  510.4 0.9 convert_add_fusion
  511.4 1.3 fusion.8.refs_12_
  513.4 4.5 convert_bitcast_fusion
  517.8 33.9 %group_gradients.5 = (bf16[704,256]{1,0:T(8,128)(2,1)}, bf16[704,256]{1,0:T(8,128)(2,1)}, bf16[704,256]{1,0:T(8,128)(2,1)}, bf16[4,128,2048]{2,1,0:T(8,128)(2,1)...) custom-call(bf16[4,512,2176]{2,1,0:T(8,128)(2,1)} %bitcast.67, bf16[4,512,2176]{2,1,0:T(8,128)(2,1)} %bitcast.68, ...), custom_call_target="tpu_custom_call" | custom-call | flops 13287555072 | bytes 25427968 | tf_op jit(solution)/shard_map/group_gradients/pallas_call | solution.py:918
  551.8 0.9 convert_reduce_fusion.3
  555.2 1.0 convert_reduce_fusion.2
  556.2 1.9 convert_bitcast_fusion.3
  558.1 1.9 convert_bitcast_fusion.2
  560.0 0.9 convert_element_type.108
  560.9 1.6 convert_add_fusion.3
  562.5 1.3 copy.69
  563.8 1.0 copy-done.7
  564.8 1.3 copy.70
  (97 shorter events, 14.4 us)
Async XLA Ops:
  7.2 159.7 %all-gather.5.cloned.1.call-start = ((), (), s32[]{:S(2)}) async-start(), calls=%async_computation.2 | async-start | bytes 10485760 | tf_op jit(solution)/shard_map/all_gather | solution.py:1384
  7.9 321.1 %all-gather.3.cloned.1.call-start = ((), (), s32[]{:S(2)}) async-start(), calls=%async_computation.1 | async-start | bytes 11141120 | tf_op jit(solution)/shard_map/all_gather | solution.py:1428
  8.7 3.0 copy-start.19
  11.7 22.3 %copy-start.18 = (bf16[2048,12]{0,1:T(8,128)(2,1)S(1)}, bf16[2048,12]{0,1:T(8,128)(2,1)}, u32[]{:S(2)}) copy-start(bf16[2048,12]{0,1:T(8,128)(2,1)} %param.29) | copy-start | bytes 147460
  11.7 24.2 %copy-start.21 = (s32[512,6]{0,1:T(8,128)S(1)}, s32[512,6]{0,1:T(8,128)}, u32[]{:S(2)}) copy-start(s32[512,6]{0,1:T(8,128)} %param.21) | copy-start | bytes 36868
  92.5 425.4 %reduce-scatter.2.cloned.1.call-start = ((), (), s32[]{:S(2)}) async-start(), calls=%async_computation.3 | async-start | bytes 2949120 | tf_op jit(solution)/shard_map/reduce_scatter | solution.py:1507
  92.9 71.6 %copy-start.1 = (bf16[512,2176]{1,0:T(8,128)(2,1)S(1)}, bf16[512,2176]{1,0:T(8,128)(2,1)}, u32[]{:S(2)}) copy-start(bf16[512,2176]{1,0:T(8,128)(2,1)} %get-tuple-element.72.x_ref.tail_ref) | copy-start | bytes 6684676
  220.5 37.3 %copy-start.23 = (f32[1,2048]{1,0:T(1,128)S(1)}, f32[1,2048]{1,0:T(1,128)}, u32[]{:S(2)}) copy-start(f32[1,2048]{1,0:T(1,128)} %get-tuple-element.103) | copy-start | bytes 24580
  257.8 2.0 copy-start.5
  432.5 0.8 copy-start.24
  502.0 4.3 copy-start.8
  502.0 4.6 copy-start.4
  506.2 1.6 copy-start
  506.2 1.6 copy-start.17
  506.2 2.0 copy-start.20
  506.2 2.0 copy-start.22
  506.2 2.6 copy-start.15
  506.2 2.6 copy-start.16
  506.3 3.3 copy-start.11
  506.3 3.3 copy-start.14
  507.8 2.6 copy-start.10
  507.8 2.6 copy-start.12
  508.2 3.2 copy-start.9
  510.4 2.2 copy-start.3
  511.4 2.0 copy-start.2
  551.7 8.2 %copy-start.13 = (bf16[704,256]{1,0:T(8,128)(2,1)S(1)}, bf16[704,256]{1,0:T(8,128)(2,1)}, u32[]{:S(2)}) copy-start(bf16[704,256]{1,0:T(8,128)(2,1)} %get-tuple-element.125) | copy-start | bytes 1081348
  551.7 10.7 %copy-start.6 = (bf16[4,128,2048]{2,1,0:T(8,128)(2,1)S(1)}, bf16[4,128,2048]{2,1,0:T(8,128)(2,1)}, u32[]{:S(2)}) copy-start(bf16[4,128,2048]{2,1,0:T(8,128)(2,1)} %get-tuple-element.93) | copy-start | bytes 6291460
  562.4 2.3 copy-start.7
Sparse Core Ops, SparseCore 0:
  9.6 152.3 all-gather.4
  163.6 165.4 all-gather.2
  433.4 60.1 reduce-scatter.1

commit v6 on v5

--- a/solution.py
+++ b/solution.py
@@ -1483,22 +1483,24 @@
         queries, latents, latent_up, key_ids, query_ids, attended, output_grad, output_weight, lse, even, odd,
         attention_input, query_weight, Scatter(expert_part), 4,
     )
-    query_flow = [(grad_query, 0)]
-    other_flow = [(grad_latent_up, 0), (grad_output, 1)]
+    spread = [(grad_query, 0), (grad_latent_up, 0), (grad_output, 1)]
     compressed_grad, *flows, result = piece(
         0,
-        4,
+        steps - 2,
         Beside(
             LineSum(latent_part),
             Beside(
-                LineFlow(query_flow + other_flow, True, 2, 3),
+                LineFlow(spread, True, 2, 3),
                 Beside(
-                    LineFlow(other_flow, False, 6, 3),
+                    LineFlow(spread, False, 6, 4),
                     Gather((residual + summed(expert_part, got_result)).astype(BF)),
                 ),
             ),
         ),
         5,
+    )
+    grad_query, grad_latent_up, grad_output = (
+        near + far.astype(F32) for near, far in zip(flows[3:], flows[:3])
     )
     attention_grad, grad_latent_down, grad_latent_gain, grad_first_gain = latents_back(
         compressed_grad, latent_raw, latent_gain[None], even, odd, latent_down.T, query_part, tokens,
@@ -1525,17 +1527,14 @@
     ).astype(BF)
     small = jnp.pad(small, ((0, 0), (0, 2048 - small.shape[1]))).reshape(devices * 16, 128)
 
-    query_flow, small_left, small_right, got = piece(
-        4,
-        steps - 5,
+    small_left, small_right, got = piece(
+        steps - 2,
+        1,
         Beside(
-            Beside(LineFlow(query_flow + [(small, 0)], False, 1, 2), LineFlow([(small, 0)], True, 1, 2)),
+            Beside(LineFlow([(small, 0)], False, 1, 1), LineFlow([(small, 0)], True, 1, 1)),
             Scatter(attention_grad),
         ),
         6,
-    )
-    grad_query, grad_latent_up, grad_output = (
-        near + far.astype(F32) for near, far in zip([query_flow] + flows[3:], flows[:3])
     )
     token_float = token_quarter.astype(F32)
     _, token_factor = norm_rows(token_float, first_gain)

time: 583 us -> 571 us (0.979)
  Pallas kernels: 443 us -> 430 us
    pallas_call x3, Pallas kernels: 194 us -> 181 us  [group_gradients(): pl.pallas_call(kernel, name='group_gradients', grid_spec=pltpu.PrefetchSc...]
  transfers between devices with their start and end apart: 3 -> 3, of which waited for: 1 -> 1; matrix products, arithmetic and copies ran while one was open for 5% -> 5% of each run, Pallas kernels for 54% -> 49%
where the time goes in v6:
time: 571 us; the launch traced here: 562 us
  Pallas kernels  430 us (75%)
  waiting for transfers between devices  70.6 us (12%)
  other arithmetic  30.7 us (5%)
  local copies, waits for them, and re-layouts  16 us (3%)
  between operations  14.4 us (3%)
    pallas_call x3, Pallas kernels, group_gradients(): pl.pallas_call(kernel, name='group_gradients', grid_spec=pltpu.PrefetchSc...  181 us
    pallas_call x2, Pallas kernels, settle(): pl.pallas_call(kernel, name='settle', in_specs=[vmem] * (n_part + n_more)...  109 us
    pallas_call x1, Pallas kernels, own_experts(): pl.pallas_call(kernel, name='own_experts', grid=(steps,), in_specs=[whole...  71.4 us
    all_gather x1, waiting for transfers between devices, shards(): all_input = lax.all_gather(wide_input, 'dpo', axis=0, tiled=True)  69.8 us
    pallas_call x1, Pallas kernels, attention_backward(): pl.pallas_call(kernel, name='attention_backward', in_specs=[vmem] * 13 +...  37.3 us
    pallas_call x1, Pallas kernels, attention_forward(): pl.pallas_call(kernel, name='attention_forward', in_specs=[vmem] * 10, ou...  22.3 us
  transfers between devices with their start and end apart: 3, of which 1 were waited for; matrix products, arithmetic and copies ran while one was open for 5% of the time, Pallas kernels for 49%

profile of v6, /device:TPU:0, one launch (start us, length us, event | category | flops | bytes accessed | tf_op | source)
XLA Modules:
  0.0 562.2 jit_solution(5647165061144064330)
XLA Ops:
  9.7 1.0 fusion.17
  10.7 1.0 maximum_maximum_fusion.1
  11.7 22.3 %attention_forward.1 = (bf16[512,512]{1,0:T(8,128)(2,1)}, f32[4,1,512]{2,1,0:T(1,128)}, bf16[8,512,640]{2,1,0:T(8,128)(2,1)}, bf16[512,2048]{1,0:T(8,128)(2,1)},...) custom-call(bf16[512,2048]{1,0:T(8,128)(2,1)} %x_ref.3, f32[1,2048]{1,0:T(1,128)} %bitcast.94, ...), custom_call_target="tpu_custom_call" | custom-call | flops 1000 | bytes 100000 | tf_op jit(solution)/shard_map/attention_forward/pallas_call | solution.py:1124
  35.0 0.9 pad.15.clone.refs_4_
  37.2 55.2 %settle.2 = (bf16[512,2176]{1,0:T(8,128)(2,1)}, f32[128,2048]{1,0:T(8,128)}, bf16[7,1,704,512]{3,2,1,0:T(8,128)(2,1)}) custom-call(bf16[512,512]{1,0:T(8,128)(2,1)} %get-tuple-element.71.refs_0_.att_ref, bf16[512,2048]{1,0:T(8,128)(2,1)} %ow_ref.1, bf16[512,2048]{1,0:T(8,128)(2,1)} %x_ref.3, f32[1,2048]{1,0:T(1,128)} %bitcast.95, ...), custom_call_target="tpu_custom_call" | custom-call | flops 1000 | bytes 100000 | tf_op jit(solution)/shard_map/settle/pallas_call | solution.py:756
  92.7 71.4 %own_experts.1 = (bf16[512,2048]{1,0:T(8,128)(2,1)}, bf16[512,2048]{1,0:T(8,128)(2,1)}, bf16[7,704,512]{2,1,0:T(8,128)(2,1)}, bf16[7,704,512]{2,1,0:T(8,128)(2,1...) custom-call(bf16[512,2176]{1,0:T(8,128)(2,1)} %get-tuple-element.72.x_ref.tail_ref, ...), custom_call_target="tpu_custom_call" | custom-call | flops 1000 | bytes 100000 | tf_op jit(solution)/shard_map/own_experts/pallas_call | solution.py:188
  164.2 53.8 %settle.3 = (bf16[512,2048]{1,0:T(8,128)(2,1)}, f32[128,2048]{1,0:T(8,128)}, f32[1,2048]{1,0:T(1,128)}, bf16[7,3,704,512]{3,2,1,0:T(8,128)(2,1)}) custom-call(bf16[512,2048]{1,0:T(8,128)(2,1)} %get-tuple-element.76.refs_0_, f32[128,2048]{1,0:T(8,128)} %get-tuple-element.77.refs_1_, f32[1,2048]{1,0:T(1,128)} %bitcast.96, bf16[512,2048]{1,0:T(8,128)(2,1)} %refs_3_.1, ...), custom_call_target="tpu_custom_call" | custom-call | flops 1000 | bytes 100000 | tf_op jit(solution)/shard_map/settle/pallas_call | solution.py:756
  218.0 37.3 %attention_backward.1 = (bf16[2048,768]{1,0:T(8,128)(2,1)}, bf16[512,2048]{1,0:T(8,128)(2,1)}, bf16[512,2048]{1,0:T(8,128)(2,1)}, bf16[512,1024]{1,0:T(8,128)(2,...) custom-call(bf16[512,1024]{1,0:T(8,128)(2,1)} %get-tuple-element.82.q_ref, ...), custom_call_target="tpu_custom_call" | custom-call | flops 1000 | bytes 100000 | tf_op jit(solution)/shard_map/attention_backward/pallas_call | solution.py:1240
  255.2 1.9 convert_reduce_fusion.1
  257.1 2.1 add_convert_fusion.refs_19_
  259.2 69.8 %all-gather.3.cloned.1.call-done = bf16[2048,2176]{1,0:T(8,128)(2,1)} async-done(((bf16[512,2176]{1,0:T(8,128)(2,1)}), bf16[2048,2176]{1,0:T(8,128)(2,1)}) %all-gather.3.cloned.1.call-update) | async-done | bytes 8912912 | tf_op jit(solution)/shard_map/all_gather | solution.py:1428
  329.0 1.1 slice_bitcast_fusion
  331.1 109.8 %group_gradients.3 = (bf16[4224,256]{1,0:T(8,128)(2,1)}, bf16[4224,256]{1,0:T(8,128)(2,1)}, bf16[4224,256]{1,0:T(8,128)(2,1)}, f32[512,640]{1,0:T(8,128)}, bf16[...) custom-call(bf16[4,512,2176]{2,1,0:T(8,128)(2,1)} %bitcast.63, ...), custom_call_target="tpu_custom_call" | custom-call | flops 66437775360 | bytes 127139840 | tf_op jit(solution)/shard_map/group_gradients/pallas_call | solution.py:918
  440.9 9.3 %latents_back.1 = (bf16[512,2048]{1,0:T(8,128)(2,1)}, bf16[2048,576]{1,0:T(8,128)(2,1)}, f32[1,512]{1,0:T(1,128)}, f32[1,2048]{1,0:T(1,128)}) custom-call(f32[512,640]{1,0:T(8,128)} %get-tuple-element.94.cg_ref, f32[512,512]{1,0:T(8,128)} %get-tuple-element.95.raw_ref, f32[1,512]{1,0:T(1,128)} %bitcast.101, f32[512,128]{1,0:T(8,128)} %get-tuple-element.200.even_ref, ...), custom_call_target="tpu_custom_call" | custom-call | flops 1000 | bytes 100000 | tf_op jit(solution)/shard_map/latents_back/pallas_call | solution.py:1298
  450.2 1.5 copy-done.1
  454.4 36.9 %group_gradients.4 = (bf16[4224,256]{1,0:T(8,128)(2,1)}, bf16[4224,256]{1,0:T(8,128)(2,1)}, bf16[4224,256]{1,0:T(8,128)(2,1)}, f32[64,128]{1,0:T(8,128)}, bf16[6...) custom-call(bf16[4,512,2176]{2,1,0:T(8,128)(2,1)} %bitcast.65, ...), custom_call_target="tpu_custom_call", output_to_operand_aliasing={{0}: (12, {}), {1}: (13, {}), {2}: (14, {})} | custom-call | flops 13287555072 | bytes 25427968 | tf_op jit(solution)/shard_map/group_gradients/pallas_call | solution.py:918
  491.3 4.3 convert.42
  495.9 1.2 copy-done
  498.9 0.9 convert_add_fusion.1
  499.8 0.9 convert_add_fusion
  500.7 1.3 fusion.8.refs_12_
  502.7 4.5 convert_bitcast_fusion
  507.1 33.9 %group_gradients.5 = (bf16[704,256]{1,0:T(8,128)(2,1)}, bf16[704,256]{1,0:T(8,128)(2,1)}, bf16[704,256]{1,0:T(8,128)(2,1)}, bf16[4,128,2048]{2,1,0:T(8,128)(2,1)...) custom-call(bf16[4,512,2176]{2,1,0:T(8,128)(2,1)} %bitcast.67, bf16[4,512,2176]{2,1,0:T(8,128)(2,1)} %bitcast.68, ...), custom_call_target="tpu_custom_call" | custom-call | flops 13287555072 | bytes 25427968 | tf_op jit(solution)/shard_map/group_gradients/pallas_call | solution.py:918
  541.1 0.9 convert_reduce_fusion.3
  544.5 1.0 convert_reduce_fusion.2
  545.5 1.9 convert_bitcast_fusion.3
  547.4 1.9 convert_bitcast_fusion.2
  549.3 0.9 convert_element_type.108
  550.2 1.6 convert_add_fusion.3
  551.8 1.3 copy.69
  553.1 1.0 copy-done.7
  554.1 1.3 copy.70
  (101 shorter events, 13.8 us)
Async XLA Ops:
  7.2 157.0 %all-gather.5.cloned.1.call-start = ((), (), s32[]{:S(2)}) async-start(), calls=%async_computation.2 | async-start | bytes 10485760 | tf_op jit(solution)/shard_map/all_gather | solution.py:1384
  7.9 321.1 %all-gather.3.cloned.1.call-start = ((), (), s32[]{:S(2)}) async-start(), calls=%async_computation.1 | async-start | bytes 11141120 | tf_op jit(solution)/shard_map/all_gather | solution.py:1428
  8.7 3.0 copy-start.19
  11.7 22.3 %copy-start.18 = (bf16[2048,12]{0,1:T(8,128)(2,1)S(1)}, bf16[2048,12]{0,1:T(8,128)(2,1)}, u32[]{:S(2)}) copy-start(bf16[2048,12]{0,1:T(8,128)(2,1)} %param.29) | copy-start | bytes 147460
  11.7 24.2 %copy-start.21 = (s32[512,6]{0,1:T(8,128)S(1)}, s32[512,6]{0,1:T(8,128)}, u32[]{:S(2)}) copy-start(s32[512,6]{0,1:T(8,128)} %param.21) | copy-start | bytes 36868
  92.5 414.6 %reduce-scatter.2.cloned.1.call-start = ((), (), s32[]{:S(2)}) async-start(), calls=%async_computation.3 | async-start | bytes 2949120 | tf_op jit(solution)/shard_map/reduce_scatter | solution.py:1509
  255.2 1.9 copy-start.5
  450.2 1.6 copy-start.1
  450.2 1.6 copy-start.26
  450.2 3.1 copy-start.23
  450.2 3.2 copy-start.24
  450.2 3.2 copy-start.25
  491.2 4.3 copy-start.8
  491.3 4.6 copy-start.4
  495.5 1.6 copy-start
  495.5 1.6 copy-start.17
  495.5 2.0 copy-start.20
  495.5 2.0 copy-start.22
  495.5 2.6 copy-start.15
  495.6 2.6 copy-start.16
  495.6 3.3 copy-start.11
  495.6 3.3 copy-start.14
  497.1 2.6 copy-start.10
  497.1 2.6 copy-start.12
  497.5 3.2 copy-start.9
  499.7 2.2 copy-start.3
  500.7 2.0 copy-start.2
  541.1 8.2 %copy-start.13 = (bf16[704,256]{1,0:T(8,128)(2,1)S(1)}, bf16[704,256]{1,0:T(8,128)(2,1)}, u32[]{:S(2)}) copy-start(bf16[704,256]{1,0:T(8,128)(2,1)} %get-tuple-element.125) | copy-start | bytes 1081348
  541.1 10.7 %copy-start.6 = (bf16[4,128,2048]{2,1,0:T(8,128)(2,1)S(1)}, bf16[4,128,2048]{2,1,0:T(8,128)(2,1)}, u32[]{:S(2)}) copy-start(bf16[4,128,2048]{2,1,0:T(8,128)(2,1)} %get-tuple-element.93) | copy-start | bytes 6291460
  551.8 2.3 copy-start.7
Sparse Core Ops, SparseCore 0:
  9.6 152.3 all-gather.4
  163.6 165.4 all-gather.2
  450.3 44.0 reduce-scatter.1
